TPU v7x, 32 devices: a whole 2x2x4 slice. The times are simulated.
32 devices in a mesh: rec: 4 (over z), ani: 4 (over x, core), chain: 2 (over y).
Axes of the slice: x: 2, y: 2, z: 4, core: 2. Of those that a mesh axis runs over, the one named last changes fastest.
Arguments:
- genotypes: bfloat16 [131072, 4096], P('ani', 'rec'), may hold values from -0.09375 to 0.09375
- effects: float32 [8192], P(('chain', 'rec')), parts along dimension 0, may hold values from -6 to 6
- gaussian_draw: float32 [8192], P(('chain', 'rec')), parts along dimension 0, may hold values from -6 to 6
- prior_prec: float32 [4096], P('rec'), may hold values from 2 to 40
- accept: int32 [64], P(('chain', 'rec')), parts along dimension 0, may hold values 0 or 1
- herd_effect: float32 [16384], P(('chain', 'rec')), parts along dimension 0, may hold values from -6 to 6
- phenotype: float32 [131072], P(('rec', 'ani')), may hold values from -12 to 12
- record_animal: int32 [131072], P(('rec', 'ani')), may hold values from 0 to 131071
- record_bin: int32 [131072], P(('rec', 'ani')), may hold values from 0 to 8191, as said below
- live_records: int32 [16], P(('rec', 'ani')), may hold values from 1 to 8192, 81920 in all
Outputs:
- next_effects: float32 [8192], P(('chain', 'rec')), parts along dimension 0
- resid_sum: float32 [262144], P(('chain', 'ani')), parts along dimension 0
There are 2 independent parts, one for each index of `chain`. A program takes and returns all parts, laid end to end along the dimension named above; an argument that names none is the same for every part. Nothing has to cross between parts.
Inputs may be any that keep to these rules, and one draw needn't show every extreme that they name: `record_bin`: a record held by rec index k names a group of k * 2048 to (k + 1) * 2048 - 1.
All inputs are finite; a program needn't handle non-finite values. No bound on the sum of `accept` or of `live_records` on one device may be relied on, other than what follows from the above.
Results may differ from a plain program's by a relative error of at most 0.0033.
Values sent between devices are 32-bit elements; how exact they have to be, the bound alone decides.
No kernel may reach another device: no remote copies, remote signals or barrier semaphores. Data moves between devices by JAX's collectives and lax.ppermute only.
A program may use at most 128 MiB of HBM per device.

v0:
```python
import math

import jax
import jax.numpy as jnp
from jax import lax
from jax.sharding import PartitionSpec as P

BLOCK = 128


def on_device(
    genotypes,
    effects,
    gaussian_draw,
    prior_prec,
    accept,
    herd_effect,
    phenotype,
    record_animal,
    record_bin,
    live_records,
):
    step_size = 0.005
    effects_half = effects.astype(jnp.bfloat16)
    partial_value = jnp.dot(genotypes, effects_half, preferred_element_type=jnp.float32)
    breeding_block = lax.psum(partial_value, "rec")
    breeding = lax.all_gather(breeding_block, "ani", axis=0, tiled=True)
    local_bin = record_bin - lax.axis_index("rec") * herd_effect.shape[0]
    position = jnp.arange(phenotype.shape[0], dtype=jnp.int32)
    live = position < live_records[0]
    herd_value = jnp.take(herd_effect, local_bin)
    residual = jnp.where(
        live, phenotype - herd_value - jnp.take(breeding, record_animal), jnp.zeros_like(phenotype)
    )
    animals = breeding.shape[0]
    partial_sums = jax.ops.segment_sum(residual, record_animal, num_segments=animals)
    share = lax.psum_scatter(partial_sums, "ani", scatter_dimension=0, tiled=True)
    resid_sum = lax.psum(share, "rec")
    resid_half = resid_sum.astype(jnp.bfloat16)
    grad_part = jnp.dot(resid_half, genotypes, preferred_element_type=jnp.float32)
    likelihood_grad = lax.psum(grad_part, "ani")
    gradient = likelihood_grad - prior_prec * effects
    proposal = effects + step_size * gradient + math.sqrt(2.0 * step_size) * gaussian_draw
    accepted = jnp.repeat(accept, BLOCK) == 1
    return (jnp.where(accepted, proposal, effects), resid_sum)


def solution(mesh):
    return jax.shard_map(
        on_device,
        mesh=mesh,
        in_specs=(
            P("ani", "rec"),
            P(("chain", "rec")),
            P(("chain", "rec")),
            P("rec"),
            P(("chain", "rec")),
            P(("chain", "rec")),
            P(("rec", "ani")),
            P(("rec", "ani")),
            P(("rec", "ani")),
            P(("rec", "ani")),
        ),
        out_specs=(P(("chain", "rec")), P(("chain", "ani"))),
        check_vma=False,
    )
```

profile of v0, /device:TPU:0, one launch (start us, length us, event | category | flops | bytes accessed | tf_op | source)
XLA Modules:
  0.0 288.7 jit_solution(391070170383022111)
XLA Ops:
  7.2 0.0 copy-start
  7.2 0.0 all-reduce.5.cloned.1.call-start
  7.2 0.7 convert_element_type.6
  7.9 0.0 copy-start.9
  8.0 0.0 copy-start.8
  8.0 26.3 %fusion.4 = f32[1,32768]{1,0:T(1,128)} fusion(bf16[32768,1024]{1,0:T(8,128)(2,1)} %param.10, bf16[1024,1]{0,1:T(2,128)(2,1)S(1)} %reshape.44), kind=kOutput, calls=%fused_computation.13 | convolution fusion | flops 67108864 | bytes 67241984 | tf_op jit(solution)/shard_map/dot_general | solution.py:25
  34.2 0.0 all-reduce.5.cloned.1.call-update
  34.3 0.0 all-reduce.9.cloned.1.call-start
  35.0 0.0 copy-done
  35.0 0.0 copy-start.5
  35.0 0.0 copy-start.6
  35.0 0.0 copy-start.7
  35.0 45.5 %gather_fusion = f32[8192]{0:T(1024)S(1)} fusion(f32[2048]{0:T(1024)S(1)} %copy-done, s32[8192]{0:T(1024)S(1)} %fusion.3), kind=kCustom, calls=%fused_computation | custom fusion | bytes 98304 | tf_op jit(solution)/shard_map/jit(_take)/gather | solution.py:31
  80.6 0.0 copy-done.3
  80.6 0.0 all-reduce.5.cloned.1.call-done
  80.6 8.8 %all_gather.3 = f32[131072]{0:T(1024)S(1)} all-gather(f32[32768]{0:T(1024)} %all-reduce.5.cloned.1.call-done), channel_id=1, replica_groups=mesh['rec'=4,'ani'=4,'chain'=2] {'ani'}, dimensions={0}, use_global_device_ids=true | all-gather | bytes 655360 | tf_op jit(solution)/shard_map/all_gather | solution.py:27
  89.5 45.5 %gather_fusion.1 = f32[8192]{0:T(1024)S(1)} fusion(f32[131072]{0:T(1024)S(1)} %all_gather.3, s32[8192]{0:T(1024)S(1)} %fusion.2), kind=kCustom, calls=%fused_computation.1 | custom fusion | bytes 98304 | tf_op jit(solution)/shard_map/jit(_take)/gather | solution.py:33
  135.0 44.0 %scatter_custom_fusion = f32[131072]{0:T(1024)} fusion(s32[8192]{0:T(1024)S(1)} %copy-done.3, f32[8192]{0:T(1024)S(1)} %subtract_select_fusion, f32[]{:T(128)} %constant.21.clone.1), kind=kCustom, calls=%fused_computation.3 | custom fusion | flops 8192 | bytes 524292 | tf_op jit(solution)/shard_map/scatter-add | solution.py:36
  179.0 0.0 all-reduce.9.cloned.1.call-update
  179.1 0.0 all-reduce.7.cloned.1.call-start
  179.1 0.6 dynamic-slice
  180.4 32.9 %all-reduce.9.cloned.1.call-done = f32[131072]{0:T(1024)} async-done(((f32[131072]{0:T(1024)}), f32[131072]{0:T(1024)}) %all-reduce.9.cloned.1.call-update) | async-done | bytes 524304
  213.3 1.6 dynamic-slice.1
  214.8 0.0 all-reduce.7.cloned.1.call-update
  214.8 0.0 copy-done.8
  214.9 35.9 %all-reduce.7.cloned.1.call-done = f32[32768]{0:T(1024)} async-done(((f32[32768]{0:T(1024)}), f32[32768]{0:T(1024)}) %all-reduce.7.cloned.1.call-update) | async-done | bytes 131088 | tf_op jit(solution)/shard_map/psum | solution.py:38
  250.7 1.0 convert_element_type.7
  251.7 0.1 reshape.46
  251.8 23.4 %fusion.5 = f32[1,1024]{1,0:T(1,128)S(1)} fusion(bf16[32768,1]{0,1:T(2,128)(2,1)S(1)} %reshape.46, bf16[32768,1024]{1,0:T(8,128)(2,1)} %param.10), kind=kOutput, calls=%fused_computation.14 | convolution fusion | flops 67108864 | bytes 67178496 | tf_op jit(solution)/shard_map/dot_general | solution.py:40
  275.2 5.6 %psum.23 = f32[1024]{0:T(1024)S(1)} all-reduce(f32[1024]{0:T(1024)S(1)} %bitcast.12), channel_id=1, replica_groups=mesh['rec'=4,'ani'=4,'chain'=2] {'ani'}, use_global_device_ids=true, to_apply=%region_4.5 | all-reduce | flops 1024 | bytes 8192 | tf_op jit(solution)/shard_map/psum | solution.py:41
  280.8 0.7 add_select_fusion
  281.5 0.7 copy.16
  (16 shorter events, 0.1 us)
Async XLA Ops:
  7.2 27.8 %copy-start = (f32[2048]{0:T(1024)S(1)}, f32[2048]{0:T(1024)}, u32[]{:S(2)}) copy-start(f32[2048]{0:T(1024)} %param.15) | copy-start | bytes 24580
  7.2 27.8 %copy-start.2 = (s32[8192]{0:T(1024)S(1)}, s32[8192]{0:T(1024)}, u32[]{:S(2)}) copy-start(s32[8192]{0:T(1024)} %param.18) | copy-start | bytes 98308
  7.2 73.4 %copy-start.3 = (s32[8192]{0:T(1024)S(1)}, s32[8192]{0:T(1024)}, u32[]{:S(2)}) copy-start(s32[8192]{0:T(1024)} %param.17) | copy-start | bytes 98308
  7.2 73.4 %all-reduce.5.cloned.1.call-start = ((), (), s32[]{:S(2)}) async-start(), calls=%async_computation | async-start | bytes 262144 | tf_op jit(solution)/shard_map/psum | solution.py:26
  7.9 127.1 %copy-start.4 = (f32[8192]{0:T(1024)S(1)}, f32[8192]{0:T(1024)}, u32[]{:S(2)}) copy-start(f32[8192]{0:T(1024)} %param.16) | copy-start | bytes 98308
  7.9 171.2 %copy-start.9 = (u32[32]{0:T(128)S(1)}, u32[32]{0:T(128)}, u32[]{:S(2)}) copy-start(u32[32]{0:T(128)} %constant.48) | copy-start | bytes 388
  8.0 206.9 %copy-start.8 = (s32[8]{0:T(128)S(1)}, s32[8]{0:T(128)}, u32[]{:S(2)}) copy-start(s32[8]{0:T(128)} %param.14) | copy-start | bytes 100
  34.3 179.0 %all-reduce.9.cloned.1.call-start = ((), (), s32[]{:S(2)}) async-start(), calls=%async_computation.2 | async-start | bytes 1048576
  35.0 245.8 %copy-start.5 = (f32[1024]{0:T(1024)S(1)}, f32[1024]{0:T(1024)}, u32[]{:S(2)}) copy-start(f32[1024]{0:T(1024)} %param.11) | copy-start | bytes 12292
  35.0 245.8 %copy-start.6 = (f32[1024]{0:T(1024)S(1)}, f32[1024]{0:T(1024)}, u32[]{:S(2)}) copy-start(f32[1024]{0:T(1024)} %param.12) | copy-start | bytes 12292
  35.0 245.8 %copy-start.7 = (f32[1024]{0:T(1024)S(1)}, f32[1024]{0:T(1024)}, u32[]{:S(2)}) copy-start(f32[1024]{0:T(1024)} %param.13) | copy-start | bytes 12292
  179.1 71.7 %all-reduce.7.cloned.1.call-start = ((), (), s32[]{:S(2)}) async-start(), calls=%async_computation.1 | async-start | bytes 262144 | tf_op jit(solution)/shard_map/psum | solution.py:38
  250.7 30.8 %copy-start.1 = (f32[32768]{0:T(1024)S(1)}, f32[32768]{0:T(1024)}, u32[]{:S(2)}) copy-start(f32[32768]{0:T(1024)} %all-reduce.7.cloned.1.call-done) | copy-start | bytes 393220
Sparse Core Ops, SparseCore 0:
  34.4 37.1 all-reduce.4
  179.2 34.0 all-reduce.8
  216.3 34.4 all-reduce.6
where the time goes:
time: 289 us
  local copies, waits for them, and re-layouts  94 us (33%)
  waiting for transfers between devices  68.8 us (24%)
  matrix products  49.6 us (17%)
  other arithmetic  46.4 us (16%)
  between operations  15.2 us (5%)
  blocking collectives  14.5 us (5%)
    gather x1, local copies, waits for them, and re-layouts, on_device(): herd_value = jnp.take(herd_effect, local_bin)  45.5 us
    gather x1, local copies, waits for them, and re-layouts, on_device(): jnp.take(breeding, record_animal)  45.5 us
    scatter-add x1, other arithmetic, on_device(): jax.ops.segment_sum(residual, record_animal, num_segments=animals)  44 us
    psum x1, waiting for transfers between devices, on_device(): resid_sum = lax.psum(share, 'rec')  35.9 us
    unnamed x4, waiting for transfers between devices  32.9 us
    dot_general x1, matrix products, on_device(): jnp.dot(genotypes, effects_half, preferred_element_type=jnp.float32)  26.3 us
    dot_general x1, matrix products, on_device(): jnp.dot(resid_half, genotypes, preferred_element_type=jnp.float32)  23.4 us
    all_gather x1, blocking collectives, on_device(): breeding = lax.all_gather(breeding_block, 'ani', axis=0, tiled=True)  8.83 us
  transfers between devices with their start and end apart: 3, of which 2 were waited for; matrix products, arithmetic and copies ran while one was open for 16% of the time, Pallas kernels for 0%

commit v1 on v0

v1 whole, which is shorter than its diff:
```python
import functools
import math

import jax
import jax.numpy as jnp
from jax import lax
from jax.experimental import pallas as pl
from jax.experimental.pallas import tpu as pltpu
from jax.sharding import PartitionSpec as P

BLOCK = 128
LANES = 128
SUBS = 64
CHUNK_ROWS = 16
F32 = jnp.float32
BF16 = jnp.bfloat16
NT = (((1,), (1,)), ((), ()))


def permute(x, axis, size, shift):
    return lax.ppermute(x, axis, [(i, (i + shift) % size) for i in range(size)])


def product1_kernel(n, per, tile, where_ref, e_ref, g_ref, out_ref):
    step = pl.program_id(0)
    piece, part = step // per, step % per
    rows = out_ref.shape[1] // 2
    res = lax.dot_general(e_ref[...], g_ref[...], NT, preferred_element_type=F32)
    for i in range(tile // LANES):
        at = part * (tile // LANES) + i
        out_ref[piece, pl.ds(at, 1), :] = res[0:1, i * LANES : (i + 1) * LANES]
        out_ref[piece, pl.ds(rows + at, 1), :] = res[1:2, i * LANES : (i + 1) * LANES]


def product1(genotypes, e2, where, n, half):
    markers = genotypes.shape[1]
    quarter = half // n
    tile = min(quarter, 2048)
    per = quarter // tile
    rows = quarter // LANES

    def g_map(step, where_ref):
        chain, rec = where_ref[0], where_ref[1]
        piece, part = step // per, step % per
        return (chain * (half // tile) + lax.rem(rec + piece, n) * per + part, 0)

    return pl.pallas_call(
        functools.partial(product1_kernel, n, per, tile),
        grid_spec=pltpu.PrefetchScalarGridSpec(
            num_scalar_prefetch=1,
            grid=(n * per,),
            in_specs=[
                pl.BlockSpec((8, markers), lambda s, w: (0, 0)),
                pl.BlockSpec((tile, markers), g_map),
            ],
            out_specs=pl.BlockSpec((n, 2 * rows, LANES), lambda s, w: (0, 0, 0)),
        ),
        out_shape=jax.ShapeDtypeStruct((n, 2 * rows, LANES), F32),
        compiler_params=pltpu.CompilerParams(
            dimension_semantics=("arbitrary",), vmem_limit_bytes=32 << 20
        ),
        cost_estimate=pl.CostEstimate(
            flops=4 * half * markers, bytes_accessed=2 * half * markers, transcendentals=0
        ),
        name="product1",
    )(where, e2, genotypes)


def records_kernel(n, n_src, where_ref, herd_ref, b_ref, *refs):
    srcs, out_ref = refs[:n_src], refs[n_src]
    lane_s, sub_s, v_s, acc, tab = refs[n_src + 1 :]
    src_rows = srcs[0].shape[0] // 3
    bins = herd_ref.shape[1]
    base = where_ref[2]
    span = 2 * SUBS * LANES
    for k, src in enumerate(srcs):
        for g in range(src_rows // 8):
            at = pl.ds(k * src_rows + g * 8, 8)
            local = src[g * 8 : g * 8 + 8, :].astype(jnp.int32) - base
            y = src[src_rows + g * 8 : src_rows + g * 8 + 8, :]
            which = src[2 * src_rows + g * 8 : 2 * src_rows + g * 8 + 8, :].astype(jnp.int32)
            known = (local >= 0) & (local < span)
            lane = (local & (LANES - 1)) | ((local >> 13) << 7)
            lane_s[at, :] = jnp.where(known, lane, -1).astype(F32)
            sub_s[at, :] = ((local >> 7) & (SUBS - 1)).astype(F32)
            low, high = which & (LANES - 1), which >> 7
            for ch in range(2):
                found = jnp.zeros((8, LANES), F32)
                for t in range(bins):
                    row = jnp.broadcast_to(herd_ref[ch, t : t + 1, :], (8, LANES))
                    got = jnp.take_along_axis(row, low, axis=1, mode="promise_in_bounds")
                    found = jnp.where(high == t, got, found)
                value = y - found
                upper = value.astype(BF16).astype(F32)
                v_s[2 * ch, at, :] = upper
                v_s[2 * ch + 1, at, :] = value - upper
    acc[...] = jnp.zeros_like(acc)
    lanes_iota = lax.broadcasted_iota(jnp.int32, (2 * LANES, LANES), 0).astype(F32).astype(BF16)
    subs_iota = lax.broadcasted_iota(jnp.int32, (SUBS, LANES), 0).astype(F32).astype(BF16)

    def spread(ref_row, count):
        return jnp.broadcast_to(
            jnp.broadcast_to(ref_row, (16, LANES)).astype(BF16)[None], (count // 16, 16, LANES)
        ).reshape(count, LANES)

    def chunk(t, carry):
        a_cols, b_cols = [], []
        for i in range(CHUNK_ROWS):
            at = pl.ds(t * CHUNK_ROWS + i, 1)
            lane = spread(lane_s[at, :], 2 * LANES)
            a_cols.append(jnp.where(lanes_iota == lane, jnp.ones((), BF16), jnp.zeros((), BF16)))
            mask = subs_iota == spread(sub_s[at, :], SUBS)
            pieces = [
                jnp.where(mask, spread(v_s[p, at, :], SUBS), jnp.zeros((), BF16)) for p in range(4)
            ]
            pieces.append(jnp.where(mask, jnp.ones((), BF16), jnp.zeros((), BF16)))
            b_cols.append(jnp.concatenate(pieces, axis=0))
        acc[...] += lax.dot_general(
            jnp.concatenate(b_cols, axis=1),
            jnp.concatenate(a_cols, axis=1),
            NT,
            preferred_element_type=F32,
        )
        return carry

    lax.fori_loop(0, n_src * src_rows // CHUNK_ROWS, chunk, 0)
    rows = 2 * SUBS // n
    for q in range(n):
        wide, first = divmod(q * rows, SUBS)
        cols = slice(wide * LANES, (wide + 1) * LANES)
        window = lambda p: acc[p * SUBS + first : p * SUBS + first + rows, cols]
        tab[0, q] = window(0) + window(1)
        tab[1, q] = window(2) + window(3)
        tab[2, q] = window(4)
    for j in range(n):
        owner = lax.rem(where_ref[1] + j, n)
        out_ref[j, 0 : 2 * rows, :] = b_ref[j]
        for p in range(3):
            out_ref[j, (2 + p) * rows : (3 + p) * rows, :] = tab[p, owner]


def records(where, herd2, b, srcs, n):
    n_src = len(srcs)
    src_rows = srcs[0].shape[0] // 3
    total = n_src * src_rows
    rows = 2 * SUBS // n
    full = lambda x: pl.BlockSpec(x.shape, lambda: (0,) * x.ndim)
    return pl.pallas_call(
        functools.partial(records_kernel, n, n_src),
        in_specs=[pl.BlockSpec(memory_space=pltpu.SMEM), full(herd2), full(b)]
        + [full(s) for s in srcs],
        out_specs=pl.BlockSpec((n, 5 * rows, LANES), lambda: (0, 0, 0)),
        out_shape=jax.ShapeDtypeStruct((n, 5 * rows, LANES), F32),
        scratch_shapes=[
            pltpu.VMEM((total, LANES), F32),
            pltpu.VMEM((total, LANES), F32),
            pltpu.VMEM((4, total, LANES), F32),
            pltpu.VMEM((5 * SUBS, 2 * LANES), F32),
            pltpu.VMEM((3, n, rows, LANES), F32),
        ],
        compiler_params=pltpu.CompilerParams(vmem_limit_bytes=24 << 20),
        cost_estimate=pl.CostEstimate(
            flops=2 * total * LANES * 5 * SUBS * 2 * LANES,
            bytes_accessed=16 * total * LANES,
            transcendentals=0,
        ),
        name="records",
    )(where, herd2, b, *srcs)


def assemble_kernel(n, where_ref, *refs):
    parts, (own_ref, other_ref) = refs[:n], refs[n:]
    rows = parts[0].shape[0] // 2
    for j in range(n):
        owner = lax.rem(where_ref[1] + j, n)
        own_ref[owner] = parts[j][0:rows, :]
        other_ref[owner] = parts[j][rows : 2 * rows, :]


def assemble(where, parts, n):
    rows = parts[0].shape[0] // 2
    full = pl.BlockSpec(parts[0].shape, lambda: (0, 0))
    out = pl.BlockSpec((n, rows, LANES), lambda: (0, 0, 0))
    own, other = pl.pallas_call(
        functools.partial(assemble_kernel, n),
        in_specs=[pl.BlockSpec(memory_space=pltpu.SMEM)] + [full] * n,
        out_specs=[out, out],
        out_shape=[jax.ShapeDtypeStruct((n, rows, LANES), F32)] * 2,
        name="assemble",
    )(where, *parts)
    return own.reshape(n * rows, LANES), other.reshape(n * rows, LANES)


def product2_kernel(where_ref, own_ref, other_ref, g_ref, out_ref):
    step = pl.program_id(0)

    @pl.when(step == 0)
    def _():
        out_ref[...] = jnp.zeros_like(out_ref)

    rows = own_ref.shape[0]
    cols = []
    for i in range(rows):
        pair = jnp.concatenate([own_ref[i : i + 1, :], other_ref[i : i + 1, :]], axis=0)
        cols.append(jnp.concatenate([pair, jnp.zeros((6, LANES), F32)], axis=0))
    lhs = jnp.concatenate(cols, axis=1).astype(BF16)
    out_ref[...] += jnp.dot(lhs, g_ref[...], preferred_element_type=F32)


def product2(genotypes, own, other, where, half):
    markers = genotypes.shape[1]
    tile = min(half, 2048)
    spec = pl.BlockSpec((tile // LANES, LANES), lambda s, w: (s, 0))
    return pl.pallas_call(
        product2_kernel,
        grid_spec=pltpu.PrefetchScalarGridSpec(
            num_scalar_prefetch=1,
            grid=(half // tile,),
            in_specs=[
                spec,
                spec,
                pl.BlockSpec((tile, markers), lambda s, w: (w[0] * (half // tile) + s, 0)),
            ],
            out_specs=pl.BlockSpec((8, markers), lambda s, w: (0, 0)),
        ),
        out_shape=jax.ShapeDtypeStruct((8, markers), F32),
        compiler_params=pltpu.CompilerParams(
            dimension_semantics=("arbitrary",), vmem_limit_bytes=32 << 20
        ),
        cost_estimate=pl.CostEstimate(
            flops=4 * half * markers, bytes_accessed=2 * half * markers, transcendentals=0
        ),
        name="product2",
    )(where, own, other, genotypes)


def on_device(
    n_rec,
    n_ani,
    genotypes,
    effects,
    gaussian_draw,
    prior_prec,
    accept,
    herd_effect,
    phenotype,
    record_animal,
    record_bin,
    live_records,
):
    step_size = 0.005
    block, markers = genotypes.shape
    half = block // 2
    slots = phenotype.shape[0]
    bins = herd_effect.shape[0]
    chain, rec, ani = lax.axis_index("chain"), lax.axis_index("rec"), lax.axis_index("ani")
    where = jnp.stack([chain, rec, ani * block + chain * half]).astype(jnp.int32)

    mine = jnp.concatenate([effects, herd_effect])
    theirs = permute(mine, "chain", 2, 1)
    live = jnp.arange(slots, dtype=jnp.int32) < live_records[0]
    raw = jnp.concatenate(
        [
            jnp.where(live, record_animal, -1).astype(F32),
            phenotype,
            (record_bin - rec * bins).astype(F32),
        ]
    ).reshape(3 * slots // LANES, LANES)
    srcs = [raw] + [permute(raw, "ani", n_ani, k) for k in range(1, n_ani)]

    e2 = jnp.concatenate(
        [effects[None], theirs[None, :markers], jnp.zeros((6, markers), F32)]
    ).astype(BF16)
    herd2 = jnp.stack([herd_effect, theirs[markers:]]).reshape(2, bins // LANES, LANES)

    b = product1(genotypes, e2, where, n_rec, half)
    sums = records(where, herd2, b, srcs, n_rec)
    total = sums[0]
    for k in range(1, n_rec):
        total = total + permute(sums[k], "rec", n_rec, k)
    rows = half // n_rec // LANES
    count = total[4 * rows :]
    resid = total[2 * rows : 4 * rows] - jnp.concatenate([count, count]) * total[: 2 * rows]

    parts = [resid] + [permute(resid, "rec", n_rec, n_rec - k) for k in range(1, n_rec)]
    own, other = assemble(where, parts, n_rec)
    back = permute(other, "chain", 2, 1)
    grads = product2(genotypes, own, other, where, half)
    grad_part = grads[0] + permute(grads[1], "chain", 2, 1)
    resid_sum = jnp.where(
        chain == 0, jnp.concatenate([own, back]), jnp.concatenate([back, own])
    ).reshape(block)

    likelihood_grad = lax.psum(grad_part, "ani")
    gradient = likelihood_grad - prior_prec * effects
    proposal = effects + step_size * gradient + math.sqrt(2.0 * step_size) * gaussian_draw
    accepted = jnp.repeat(accept, BLOCK) == 1
    return (jnp.where(accepted, proposal, effects), resid_sum)


def solution(mesh):
    return jax.shard_map(
        functools.partial(on_device, mesh.shape["rec"], mesh.shape["ani"]),
        mesh=mesh,
        in_specs=(
            P("ani", "rec"),
            P(("chain", "rec")),
            P(("chain", "rec")),
            P("rec"),
            P(("chain", "rec")),
            P(("chain", "rec")),
            P(("rec", "ani")),
            P(("rec", "ani")),
            P(("rec", "ani")),
            P(("rec", "ani")),
        ),
        out_specs=(P(("chain", "rec")), P(("chain", "ani"))),
        check_vma=False,
    )
```

time: 289 us -> 86.2 us (0.30)
  local copies, waits for them, and re-layouts: 94 us -> 3.12 us
  waiting for transfers between devices: 68.8 us -> 11.7 us
  matrix products: 49.6 us -> 0 us
  Pallas kernels: 0 us -> 42 us
  other arithmetic: 46.4 us -> 4.48 us
  starting transfers between devices: 0.12 us -> 17 us
  between operations: 15.2 us -> 1.45 us
  blocking collectives: 14.5 us -> 5.64 us
    gather x2 -> x0, local copies, waits for them, and re-layouts: 91.1 us -> none  [the longest x1 45.5 us: on_device(): herd_value = jnp.take(herd_effect, local_bin)]
    dot_general x2 -> x0, matrix products: 49.6 us -> none  [the longest x1 26.3 us: on_device(): jnp.dot(genotypes, effects_half, preferred_element_type=jnp.float32)]
    scatter-add x1 -> x0, other arithmetic: 44 us -> none  [on_device(): jax.ops.segment_sum(residual, record_animal, num_segments=animals)]
    pallas_call x0 -> x4, Pallas kernels: none -> 42 us  [the longest x1 16 us: product1(): pl.pallas_call(functools.partial(product1_kernel, n, per, tile), grid_spe...]
    psum x2 -> x0, waiting for transfers between devices: 35.9 us -> none  [the longest x1 35.9 us: on_device(): resid_sum = lax.psum(share, 'rec')]
    unnamed x4 -> x0, waiting for transfers between devices: 32.9 us -> none
    ppermute x0 -> x12, starting transfers between devices: none -> 17 us  [permute(): return lax.ppermute(x, axis, [(i, (i + shift) % size) for i in range(size)])]
    ppermute x0 -> x12, waiting for transfers between devices: none -> 11.7 us  [permute(): return lax.ppermute(x, axis, [(i, (i + shift) % size) for i in range(size)])]
  transfers between devices with their start and end apart: 3 -> 12, of which waited for: 2 -> 8; matrix products, arithmetic and copies ran while one was open for 16% -> 3% of each run, Pallas kernels for 0% -> 19%
where the time goes in v1:
time: 86.2 us; the launch traced here: 85.4 us
  Pallas kernels  42 us (49%)
  starting transfers between devices  17 us (20%)
  waiting for transfers between devices  11.7 us (14%)
  blocking collectives  5.64 us (7%)
  other arithmetic  4.48 us (5%)
  local copies, waits for them, and re-layouts  3.12 us (4%)
  between operations  1.45 us (2%)
    ppermute x12, starting transfers between devices, permute(): return lax.ppermute(x, axis, [(i, (i + shift) % size) for i in range(size)])  17 us
    pallas_call x1, Pallas kernels, product1(): pl.pallas_call(functools.partial(product1_kernel, n, per, tile), grid_spe...  16 us
    pallas_call x1, Pallas kernels, product2(): pl.pallas_call(product2_kernel, grid_spec=pltpu.PrefetchScalarGridSpec(nu...  14 us
    ppermute x12, waiting for transfers between devices, permute(): return lax.ppermute(x, axis, [(i, (i + shift) % size) for i in range(size)])  11.7 us
    pallas_call x1, Pallas kernels, records(): pl.pallas_call(functools.partial(records_kernel, n, n_src), in_specs=[pl....  10.5 us
    psum x1, blocking collectives, on_device(): likelihood_grad = lax.psum(grad_part, 'ani')  5.64 us
    unnamed x30, local copies, waits for them, and re-layouts  2.99 us
  transfers between devices with their start and end apart: 12, of which 8 were waited for; matrix products, arithmetic and copies ran while one was open for 3% of the time, Pallas kernels for 19%

profile of v1, /device:TPU:0, one launch (start us, length us, event | category | flops | bytes accessed | tf_op | source)
XLA Modules:
  0.0 85.4 jit_solution(4019649119845033075)
XLA Ops:
  1.3 0.8 convert_bitcast_fusion
  2.1 0.8 pad_maximum_fusion.refs_0_
  3.3 2.6 %collective-permute-start.2 = (f32[192,128]{1,0:T(8,128)S(1)}, f32[192,128]{1,0:T(8,128)S(1)}, u32[]{:S(2)}, u32[]{:S(2)}) collective-permute-start(f32[192,128]{1,0:T(8,128)S(1)} %pad_maximum_fusion.refs_0_), channel_id=1, source_target_pairs={{0,4},{2,6},{4,0},{6,2},{1,5},{3,7},{5,1},{7,3},{8,12},{10,14},{12... | collective-permute-start | bytes 294920 | tf_op jit(solution)/shard_map/ppermute | solution.py:21
  5.9 1.4 %collective-permute-start.3 = (f32[192,128]{1,0:T(8,128)S(1)}, f32[192,128]{1,0:T(8,128)S(1)}, u32[]{:S(2)}, u32[]{:S(2)}) collective-permute-start(f32[192,128]{1,0:T(8,128)S(1)} %pad_maximum_fusion.refs_0_), channel_id=1, source_target_pairs={{0,6},{2,0},{4,2},{6,4},{1,7},{3,1},{5,3},{7,5},{8,14},{10,8},{12,... | collective-permute-start | bytes 294920 | tf_op jit(solution)/shard_map/ppermute | solution.py:21
  7.3 0.7 pad_maximum_fusion.2
  8.0 1.5 %collective-permute-start = (f32[3072]{0:T(1024)S(1)}, f32[3072]{0:T(1024)S(1)}, u32[]{:S(2)}, u32[]{:S(2)}) collective-permute-start(f32[3072]{0:T(1024)S(1)} %pad_maximum_fusion.2), channel_id=1, source_target_pairs={{0,1},{1,0},{2,3},{3,2},{4,5},{5,4},{6,7},{7,6},{8,9},{9,8},{10,11... | collective-permute-start | bytes 36872 | tf_op jit(solution)/shard_map/ppermute | solution.py:21
  9.6 0.7 convert.11
  10.4 1.3 %collective-permute-done = f32[3072]{0:T(1024)S(1)} collective-permute-done((f32[3072]{0:T(1024)S(1)}, f32[3072]{0:T(1024)S(1)}, u32[]{:S(2)}, u32[]{:S(2)}) %collective-permute-start) | collective-permute-done | bytes 12320 | tf_op jit(solution)/shard_map/ppermute | solution.py:21
  11.8 16.0 %product1.1.b_ref = f32[4,64,128]{2,1,0:T(8,128)S(1)} custom-call(s32[3]{0:T(128)S(1)} %pad_add_fusion.where_ref, bf16[8,1024]{1,0:T(8,128)(2,1)S(1)} %maximum_maximum_fusion.e_ref, bf16[32768,1024]{1,0:T(8,128)(2,1)} %g_ref.3), custom_call_target="tpu_custom_call" | custom-call | flops 67108864 | bytes 33554432 | tf_op jit(solution)/shard_map/product1/pallas_call | solution.py:47
  27.8 10.5 %records.1 = f32[4,160,128]{2,1,0:T(8,128)S(1)} custom-call(s32[3]{0:T(128)S(1)} %pad_add_fusion.where_ref, f32[2,16,128]{2,1,0:T(8,128)S(1)} %pad_maximum_fusion.1.herd_ref, f32[4,64,128]{2,1,0:T(8,128)S(1)} %product1.1.b_ref, f32[192,128]{1,0:T(8,128)S(1)} %pad_maximum_fusion.refs_0_, f32[192,128]{1,0:T(8,128)S(1)} %collective-permute-done.1.refs_1_, ...), custom_call_target="tpu_custom_call" | custom-call | flops 5368709120 | bytes 524288 | tf_op jit(solution)/shard_map/records/pallas_call | solution.py:148
  38.4 1.6 %collective-permute-start.4 = (f32[160,128]{1,0:T(8,128)S(1)}, f32[160,128]{1,0:T(8,128)S(1)}, u32[]{:S(2)}, u32[]{:S(2)}) collective-permute-start(f32[160,128]{1,0:T(8,128)S(1)} %get-tuple-element.6), channel_id=1, source_target_pairs={{0,8},{8,16},{16,24},{24,0},{1,9},{9,17},{17,25},{25,1},{2,10},{10... | collective-permute-start | bytes 245768 | tf_op jit(solution)/shard_map/ppermute | solution.py:21
  40.0 2.6 %collective-permute-start.5 = (f32[160,128]{1,0:T(8,128)S(1)}, f32[160,128]{1,0:T(8,128)S(1)}, u32[]{:S(2)}, u32[]{:S(2)}) collective-permute-start(f32[160,128]{1,0:T(8,128)S(1)} %get-tuple-element.8), channel_id=1, source_target_pairs={{0,16},{8,24},{16,0},{24,8},{1,17},{9,25},{17,1},{25,9},{2,18},{10... | collective-permute-start | bytes 245768 | tf_op jit(solution)/shard_map/ppermute | solution.py:21
  42.6 1.3 %collective-permute-start.6 = (f32[160,128]{1,0:T(8,128)S(1)}, f32[160,128]{1,0:T(8,128)S(1)}, u32[]{:S(2)}, u32[]{:S(2)}) collective-permute-start(f32[160,128]{1,0:T(8,128)S(1)} %get-tuple-element.7), channel_id=1, source_target_pairs={{0,24},{8,0},{16,8},{24,16},{1,25},{9,1},{17,9},{25,17},{2,26},{10... | collective-permute-start | bytes 245768 | tf_op jit(solution)/shard_map/ppermute | solution.py:21
  44.0 1.3 %collective-permute-done.4 = f32[160,128]{1,0:T(8,128)S(1)} collective-permute-done((f32[160,128]{1,0:T(8,128)S(1)}, f32[160,128]{1,0:T(8,128)S(1)}, u32[]{:S(2)}, u32[]{:S(2)}) %collective-permute-start.4) | collective-permute-done | bytes 81952 | tf_op jit(solution)/shard_map/ppermute | solution.py:21
  45.2 2.2 %collective-permute-done.5 = f32[160,128]{1,0:T(8,128)S(1)} collective-permute-done((f32[160,128]{1,0:T(8,128)S(1)}, f32[160,128]{1,0:T(8,128)S(1)}, u32[]{:S(2)}, u32[]{:S(2)}) %collective-permute-start.5) | collective-permute-done | bytes 81952 | tf_op jit(solution)/shard_map/ppermute | solution.py:21
  47.8 2.7 %collective-permute-start.7 = (f32[64,128]{1,0:T(8,128)S(1)}, f32[64,128]{1,0:T(8,128)S(1)}, u32[]{:S(2)}, u32[]{:S(2)}) collective-permute-start(f32[64,128]{1,0:T(8,128)S(1)} %fusion.4.refs_0_), channel_id=1, source_target_pairs={{0,24},{8,0},{16,8},{24,16},{1,25},{9,1},{17,9},{25,17},{2,26},{10... | collective-permute-start | bytes 98312 | tf_op jit(solution)/shard_map/ppermute | solution.py:21
  50.5 0.6 collective-permute-start.9
  51.1 1.0 %collective-permute-done.7.refs_1_ = f32[64,128]{1,0:T(8,128)S(1)} collective-permute-done((f32[64,128]{1,0:T(8,128)S(1)}, f32[64,128]{1,0:T(8,128)S(1)}, u32[]{:S(2)}, u32[]{:S(2)}) %collective-permute-start.7) | collective-permute-done | bytes 32800 | tf_op jit(solution)/shard_map/ppermute | solution.py:21
  52.1 3.2 %collective-permute-done.8.refs_2_ = f32[64,128]{1,0:T(8,128)S(1)} collective-permute-done((f32[64,128]{1,0:T(8,128)S(1)}, f32[64,128]{1,0:T(8,128)S(1)}, u32[]{:S(2)}, u32[]{:S(2)}) %collective-permute-start.8) | collective-permute-done | bytes 32800 | tf_op jit(solution)/shard_map/ppermute | solution.py:21
  55.3 0.9 %collective-permute-done.9.refs_3_ = f32[64,128]{1,0:T(8,128)S(1)} collective-permute-done((f32[64,128]{1,0:T(8,128)S(1)}, f32[64,128]{1,0:T(8,128)S(1)}, u32[]{:S(2)}, u32[]{:S(2)}) %collective-permute-start.9) | collective-permute-done | bytes 32800 | tf_op jit(solution)/shard_map/ppermute | solution.py:21
  56.2 0.6 copy-done.11
  56.8 1.5 %assemble.1 = (f32[4,32,128]{2,1,0:T(8,128)}, f32[4,32,128]{2,1,0:T(8,128)}) custom-call(s32[3]{0:T(128)} %copy-done.4, f32[64,128]{1,0:T(8,128)} %copy-done.6, f32[64,128]{1,0:T(8,128)} %copy-done.9, f32[64,128]{1,0:T(8,128)} %copy-done.10, f32[64,128]{1,0:T(8,128)} %copy-done.11), custom_call_target="tpu_custom_call" | custom-call | tf_op jit(solution)/shard_map/assemble/pallas_call | solution.py:184
  58.3 0.8 copy-done
  59.2 0.8 copy-done.2
  60.0 0.7 copy-done.5
  60.7 14.0 %product2.1 = f32[8,1024]{1,0:T(8,128)S(1)} custom-call(s32[3]{0:T(128)S(1)} %copy-done.5, f32[128,128]{1,0:T(8,128)S(1)} %bitcast.35, f32[128,128]{1,0:T(8,128)S(1)} %bitcast.37, bf16[32768,1024]{1,0:T(8,128)(2,1)} %g_ref.3), custom_call_target="tpu_custom_call" | custom-call | flops 67108864 | bytes 33554432 | tf_op jit(solution)/shard_map/product2/pallas_call | solution.py:214
  74.7 1.6 %collective-permute-start.10 = (f32[1024]{0:T(1024)S(1)}, f32[1024]{0:T(1024)S(1)}, u32[]{:S(2)}, u32[]{:S(2)}) collective-permute-start(f32[1024]{0:T(1024)S(1)} %bitcast.42), channel_id=1, source_target_pairs={{0,1},{1,0},{2,3},{3,2},{4,5},{5,4},{6,7},{7,6},{8,9},{9,8},{10,11... | collective-permute-start | bytes 12296 | tf_op jit(solution)/shard_map/ppermute | solution.py:21
  76.3 0.6 collective-permute-start.11
  76.9 1.5 %collective-permute-done.10 = f32[1024]{0:T(1024)S(1)} collective-permute-done((f32[1024]{0:T(1024)S(1)}, f32[1024]{0:T(1024)S(1)}, u32[]{:S(2)}, u32[]{:S(2)}) %collective-permute-start.10) | collective-permute-done | bytes 4128 | tf_op jit(solution)/shard_map/ppermute | solution.py:21
  78.4 5.6 %psum.7 = f32[1024]{0:T(1024)S(1)} all-reduce(f32[1024]{0:T(1024)S(1)} %add.27), channel_id=1, replica_groups=mesh['rec'=4,'ani'=4,'chain'=2] {'ani'}, use_global_device_ids=true, to_apply=%region_0.1 | all-reduce | flops 1024 | bytes 8192 | tf_op jit(solution)/shard_map/psum | solution.py:294
  84.0 0.7 add_select_fusion
  84.7 0.7 fusion
  (49 shorter events, 1.2 us)
Async XLA Ops:
  0.6 27.1 %copy-start.8 = (f32[2048]{0:T(1024)S(1)}, f32[2048]{0:T(1024)}, u32[]{:S(2)}) copy-start(f32[2048]{0:T(1024)} %param.15) | copy-start | bytes 24580
  2.9 24.9 %collective-permute-start.1 = (f32[192,128]{1,0:T(8,128)S(1)}, f32[192,128]{1,0:T(8,128)S(1)}, u32[]{:S(2)}, u32[]{:S(2)}) collective-permute-start(f32[192,128]{1,0:T(8,128)S(1)} %pad_maximum_fusion.refs_0_), channel_id=1, source_target_pairs={{0,2},{2,4},{4,6},{6,0},{1,3},{3,5},{5,7},{7,1},{8,10},{10,12},{12... | collective-permute-start | bytes 294920 | tf_op jit(solution)/shard_map/ppermute | solution.py:21
  3.3 24.5 %collective-permute-start.2 = (f32[192,128]{1,0:T(8,128)S(1)}, f32[192,128]{1,0:T(8,128)S(1)}, u32[]{:S(2)}, u32[]{:S(2)}) collective-permute-start(f32[192,128]{1,0:T(8,128)S(1)} %pad_maximum_fusion.refs_0_), channel_id=1, source_target_pairs={{0,4},{2,6},{4,0},{6,2},{1,5},{3,7},{5,1},{7,3},{8,12},{10,14},{12... | collective-permute-start | bytes 294920 | tf_op jit(solution)/shard_map/ppermute | solution.py:21
  5.9 21.9 %collective-permute-start.3 = (f32[192,128]{1,0:T(8,128)S(1)}, f32[192,128]{1,0:T(8,128)S(1)}, u32[]{:S(2)}, u32[]{:S(2)}) collective-permute-start(f32[192,128]{1,0:T(8,128)S(1)} %pad_maximum_fusion.refs_0_), channel_id=1, source_target_pairs={{0,6},{2,0},{4,2},{6,4},{1,7},{3,1},{5,3},{7,5},{8,14},{10,8},{12,... | collective-permute-start | bytes 294920 | tf_op jit(solution)/shard_map/ppermute | solution.py:21
  8.0 3.7 %collective-permute-start = (f32[3072]{0:T(1024)S(1)}, f32[3072]{0:T(1024)S(1)}, u32[]{:S(2)}, u32[]{:S(2)}) collective-permute-start(f32[3072]{0:T(1024)S(1)} %pad_maximum_fusion.2), channel_id=1, source_target_pairs={{0,1},{1,0},{2,3},{3,2},{4,5},{5,4},{6,7},{7,6},{8,9},{9,8},{10,11... | collective-permute-start | bytes 36872 | tf_op jit(solution)/shard_map/ppermute | solution.py:21
  9.6 46.6 %copy-start.4 = (s32[3]{0:T(128)}, s32[3]{0:T(128)S(1)}, u32[]{:S(2)}) copy-start(s32[3]{0:T(128)S(1)} %pad_add_fusion.where_ref) | copy-start | bytes 40
  11.8 64.5 %copy-start.14 = (s32[8]{0:T(128)S(1)}, s32[8]{0:T(128)}, u32[]{:S(2)}) copy-start(s32[8]{0:T(128)} %param.14) | copy-start | bytes 100
  11.8 72.3 %copy-start.7 = (f32[1024]{0:T(1024)S(1)}, f32[1024]{0:T(1024)}, u32[]{:S(2)}) copy-start(f32[1024]{0:T(1024)} %param.11) | copy-start | bytes 12292
  11.8 72.3 %copy-start.12 = (f32[1024]{0:T(1024)S(1)}, f32[1024]{0:T(1024)}, u32[]{:S(2)}) copy-start(f32[1024]{0:T(1024)} %param.12) | copy-start | bytes 12292
  11.8 72.3 %copy-start.13 = (f32[1024]{0:T(1024)S(1)}, f32[1024]{0:T(1024)}, u32[]{:S(2)}) copy-start(f32[1024]{0:T(1024)} %param.13) | copy-start | bytes 12292
  38.4 6.9 %collective-permute-start.4 = (f32[160,128]{1,0:T(8,128)S(1)}, f32[160,128]{1,0:T(8,128)S(1)}, u32[]{:S(2)}, u32[]{:S(2)}) collective-permute-start(f32[160,128]{1,0:T(8,128)S(1)} %get-tuple-element.6), channel_id=1, source_target_pairs={{0,8},{8,16},{16,24},{24,0},{1,9},{9,17},{17,25},{25,1},{2,10},{10... | collective-permute-start | bytes 245768 | tf_op jit(solution)/shard_map/ppermute | solution.py:21
  40.0 7.4 %collective-permute-start.5 = (f32[160,128]{1,0:T(8,128)S(1)}, f32[160,128]{1,0:T(8,128)S(1)}, u32[]{:S(2)}, u32[]{:S(2)}) collective-permute-start(f32[160,128]{1,0:T(8,128)S(1)} %get-tuple-element.8), channel_id=1, source_target_pairs={{0,16},{8,24},{16,0},{24,8},{1,17},{9,25},{17,1},{25,9},{2,18},{10... | collective-permute-start | bytes 245768 | tf_op jit(solution)/shard_map/ppermute | solution.py:21
  42.6 5.1 %collective-permute-start.6 = (f32[160,128]{1,0:T(8,128)S(1)}, f32[160,128]{1,0:T(8,128)S(1)}, u32[]{:S(2)}, u32[]{:S(2)}) collective-permute-start(f32[160,128]{1,0:T(8,128)S(1)} %get-tuple-element.7), channel_id=1, source_target_pairs={{0,24},{8,0},{16,8},{24,16},{1,25},{9,1},{17,9},{25,17},{2,26},{10... | collective-permute-start | bytes 245768 | tf_op jit(solution)/shard_map/ppermute | solution.py:21
  47.8 8.4 %copy-start.6 = (f32[64,128]{1,0:T(8,128)}, f32[64,128]{1,0:T(8,128)S(1)}, u32[]{:S(2)}) copy-start(f32[64,128]{1,0:T(8,128)S(1)} %fusion.4.refs_0_) | copy-start | bytes 98308
  47.8 4.3 %collective-permute-start.7 = (f32[64,128]{1,0:T(8,128)S(1)}, f32[64,128]{1,0:T(8,128)S(1)}, u32[]{:S(2)}, u32[]{:S(2)}) collective-permute-start(f32[64,128]{1,0:T(8,128)S(1)} %fusion.4.refs_0_), channel_id=1, source_target_pairs={{0,24},{8,0},{16,8},{24,16},{1,25},{9,1},{17,9},{25,17},{2,26},{10... | collective-permute-start | bytes 98312 | tf_op jit(solution)/shard_map/ppermute | solution.py:21
  50.5 4.8 %collective-permute-start.8 = (f32[64,128]{1,0:T(8,128)S(1)}, f32[64,128]{1,0:T(8,128)S(1)}, u32[]{:S(2)}, u32[]{:S(2)}) collective-permute-start(f32[64,128]{1,0:T(8,128)S(1)} %fusion.4.refs_0_), channel_id=1, source_target_pairs={{0,16},{8,24},{16,0},{24,8},{1,17},{9,25},{17,1},{25,9},{2,18},{10... | collective-permute-start | bytes 98312 | tf_op jit(solution)/shard_map/ppermute | solution.py:21
  50.5 5.7 %collective-permute-start.9 = (f32[64,128]{1,0:T(8,128)S(1)}, f32[64,128]{1,0:T(8,128)S(1)}, u32[]{:S(2)}, u32[]{:S(2)}) collective-permute-start(f32[64,128]{1,0:T(8,128)S(1)} %fusion.4.refs_0_), channel_id=1, source_target_pairs={{0,8},{8,16},{16,24},{24,0},{1,9},{9,17},{17,25},{25,1},{2,10},{10... | collective-permute-start | bytes 98312 | tf_op jit(solution)/shard_map/ppermute | solution.py:21
  52.1 4.1 %copy-start.9 = (f32[64,128]{1,0:T(8,128)}, f32[64,128]{1,0:T(8,128)S(1)}, u32[]{:S(2)}) copy-start(f32[64,128]{1,0:T(8,128)S(1)} %collective-permute-done.7.refs_1_) | copy-start | bytes 98308
  55.3 0.9 %copy-start.10 = (f32[64,128]{1,0:T(8,128)}, f32[64,128]{1,0:T(8,128)S(1)}, u32[]{:S(2)}) copy-start(f32[64,128]{1,0:T(8,128)S(1)} %collective-permute-done.8.refs_2_) | copy-start | bytes 98308
  56.2 0.6 copy-start.11
  58.3 0.8 copy-start
  59.1 0.8 copy-start.2
  60.0 0.7 copy-start.5
  60.6 15.6 %copy-start.3 = (f32[4,32,128]{2,1,0:T(8,128)S(1)}, f32[4,32,128]{2,1,0:T(8,128)}, u32[]{:S(2)}) copy-start(f32[4,32,128]{2,1,0:T(8,128)} %get-tuple-element.5) | copy-start | bytes 196612
  60.7 24.1 %copy-start.1 = (f32[4,32,128]{2,1,0:T(8,128)S(1)}, f32[4,32,128]{2,1,0:T(8,128)}, u32[]{:S(2)}) copy-start(f32[4,32,128]{2,1,0:T(8,128)} %get-tuple-element.4) | copy-start | bytes 196612
  74.7 3.7 %collective-permute-start.10 = (f32[1024]{0:T(1024)S(1)}, f32[1024]{0:T(1024)S(1)}, u32[]{:S(2)}, u32[]{:S(2)}) collective-permute-start(f32[1024]{0:T(1024)S(1)} %bitcast.42), channel_id=1, source_target_pairs={{0,1},{1,0},{2,3},{3,2},{4,5},{5,4},{6,7},{7,6},{8,9},{9,8},{10,11... | collective-permute-start | bytes 12296 | tf_op jit(solution)/shard_map/ppermute | solution.py:21
  76.3 8.4 %collective-permute-start.11 = (f32[128,128]{1,0:T(8,128)S(1)}, f32[128,128]{1,0:T(8,128)S(1)}, u32[]{:S(2)}, u32[]{:S(2)}) collective-permute-start(f32[128,128]{1,0:T(8,128)S(1)} %bitcast.38), channel_id=1, source_target_pairs={{0,1},{1,0},{2,3},{3,2},{4,5},{5,4},{6,7},{7,6},{8,9},{9,8},{10,11... | collective-permute-start | bytes 196616 | tf_op jit(solution)/shard_map/ppermute | solution.py:21

commit v2 on v0

v2 whole, which is shorter than its diff:
```python
import functools
import math

import jax
import jax.numpy as jnp
from jax import lax
from jax.experimental import pallas as pl
from jax.experimental.pallas import tpu as pltpu
from jax.sharding import PartitionSpec as P

BLOCK = 128
LANES = 128
SUBS = 64
SPAN_BITS = 14
CHUNK_ROWS = 16
TILE = 2048
F32 = jnp.float32
BF16 = jnp.bfloat16
NT = (((1,), (1,)), ((), ()))
VMEM = pl.BlockSpec(memory_space=pltpu.VMEM)
SMEM = pl.BlockSpec(memory_space=pltpu.SMEM)
ANY = pl.BlockSpec(memory_space=pl.ANY)


def permute(x, axis, size, shift):
    return lax.ppermute(x, axis, [(i, (i + shift) % size) for i in range(size)])


def tiled(x):
    return x.reshape(-1, LANES)


def prepare_kernel(live_ref, animal_ref, y_ref, bin_ref, e_ref, h_ref, raw_ref, mine_ref):
    rows = animal_ref.shape[0]
    slot = (
        lax.broadcasted_iota(jnp.int32, (rows, LANES), 0) * LANES
        + lax.broadcasted_iota(jnp.int32, (rows, LANES), 1)
    )
    first_bin = lax.axis_index("rec") * h_ref.shape[0] * LANES
    raw_ref[0:rows, :] = jnp.where(slot < live_ref[0], animal_ref[...], -1).astype(F32)
    raw_ref[rows : 2 * rows, :] = y_ref[...]
    raw_ref[2 * rows : 3 * rows, :] = (bin_ref[...] - first_bin).astype(F32)
    mine_ref[0 : e_ref.shape[0], :] = e_ref[...]
    mine_ref[e_ref.shape[0] :, :] = h_ref[...]


def prepare(live, animal, y, bins, e, h):
    rows = animal.shape[0]
    return pl.pallas_call(
        prepare_kernel,
        in_specs=[SMEM] + [VMEM] * 5,
        out_specs=[VMEM, VMEM],
        out_shape=[
            jax.ShapeDtypeStruct((3 * rows, LANES), F32),
            jax.ShapeDtypeStruct((e.shape[0] + h.shape[0], LANES), F32),
        ],
        name="prepare",
    )(live, animal, y, bins, e, h)


def up(x, k):
    return jnp.concatenate([x[k:], jnp.zeros((k,) + x.shape[1:], x.dtype)], axis=0)


def down(x, k):
    return jnp.concatenate([jnp.zeros((k,) + x.shape[1:], x.dtype), x[:-k]], axis=0)


def compact(srcs, base, key_s, y_s):
    src_rows = srcs[0].shape[0] // 3
    keys, ys = [], []
    for src in srcs:
        local = src[0:src_rows, :].astype(jnp.int32) - base
        which = src[2 * src_rows : 3 * src_rows, :].astype(jnp.int32)
        known = (local >= 0) & (local < (1 << SPAN_BITS))
        keys.append(jnp.where(known, (which << SPAN_BITS) + local, -1))
        ys.append(src[src_rows : 2 * src_rows, :])
    key = jnp.concatenate(keys, axis=0)
    y = jnp.concatenate(ys, axis=0)
    total = key.shape[0]
    gone = jnp.where(key < 0, 1, 0)
    left = gone
    k = 1
    while k < total:
        left = left + down(left, k)
        k *= 2
    most = total - jnp.min(left[total - 1 : total, :])
    left = left - gone
    k = 1
    while k < total:
        move = (key >= 0) & ((left & k) != 0)
        key_up = up(jnp.where(move, key, -1), k)
        key_up = jnp.concatenate([key_up[: total - k], jnp.full((k, LANES), -1, jnp.int32)], axis=0)
        come = key_up >= 0
        key = jnp.where(come, key_up, jnp.where(move, -1, key))
        y = jnp.where(come, up(y, k), y)
        left = jnp.where(come, up(left, k), left)
        k *= 2
    key_s[...] = key
    y_s[...] = y
    return most


def look_up(t, mine_ref, theirs_ref, first, key_s, y_s, lane_s, sub_s, v_s):
    for g in range(CHUNK_ROWS // 8):
        at = pl.ds(pl.multiple_of(t * CHUNK_ROWS + g * 8, 8), 8)
        key, y = key_s[at, :], y_s[at, :]
        local, which = key & ((1 << SPAN_BITS) - 1), key >> SPAN_BITS
        lane = (local & (LANES - 1)) | ((local >> 13) << 7)
        lane_s[at, :] = jnp.where(key >= 0, lane, -1).astype(F32)
        sub_s[at, :] = ((local >> 7) & (SUBS - 1)).astype(F32)
        low, high = which & (LANES - 1), which >> 7
        for ch, ref in enumerate((mine_ref, theirs_ref)):
            found = jnp.zeros((8, LANES), F32)
            for q in range(ref.shape[0] - first):
                row = jnp.broadcast_to(ref[first + q : first + q + 1, :], (8, LANES))
                got = jnp.take_along_axis(row, low, axis=1, mode="promise_in_bounds")
                found = jnp.where(high == q, got, found)
            value = y - found
            upper = value.astype(BF16).astype(F32)
            v_s[2 * ch, at, :] = upper
            v_s[2 * ch + 1, at, :] = value - upper


def spread(row, count):
    few = jnp.broadcast_to(row, (16, LANES)).astype(BF16)
    return jnp.broadcast_to(few[None], (count // 16, 16, LANES)).reshape(count, LANES)


def one_hots(t, lane_s, sub_s, v_s, lanes_iota, subs_iota):
    a_cols, b_cols = [], []
    one, zero = jnp.ones((), BF16), jnp.zeros((), BF16)
    for i in range(CHUNK_ROWS):
        at = pl.ds(t * CHUNK_ROWS + i, 1)
        a_cols.append(jnp.where(lanes_iota == spread(lane_s[at, :], 2 * LANES), one, zero))
        mask = subs_iota == spread(sub_s[at, :], SUBS)
        pieces = [jnp.where(mask, spread(v_s[p, at, :], SUBS), zero) for p in range(4)]
        pieces.append(jnp.where(mask, one, zero))
        b_cols.append(jnp.concatenate(pieces, axis=0))
    return jnp.concatenate(b_cols, axis=1), jnp.concatenate(a_cols, axis=1)


def front_kernel(n, n_src, mine_any, theirs_any, *refs):
    srcs_any, g_hbm, kept_ref = refs[:n_src], refs[n_src], refs[n_src + 1]
    outs = refs[n_src + 2 : n_src + 2 + n]
    key_s, y_s, lane_s, sub_s, v_s, acc, tab, gain, mine_ref, theirs_ref, src_s, sem, small_sem = refs[
        n_src + 2 + n :
    ]
    srcs = [src_s.at[k] for k in range(n_src)]
    half, markers = kept_ref.shape
    quarter = half // n
    tile = min(TILE, quarter)
    per = quarter // tile
    rows = quarter // LANES
    e_rows = markers // LANES
    chain, rec, ani = lax.axis_index("chain"), lax.axis_index("rec"), lax.axis_index("ani")

    def place(b):
        return pl.multiple_of(
            lax.rem(rec + b // per, n) * quarter + lax.rem(b, per) * tile, tile
        )

    def load(b):
        at = pl.ds(pl.multiple_of(chain * half + place(b), tile), tile)
        return pltpu.make_async_copy(
            g_hbm.at[at, :], kept_ref.at[pl.ds(place(b), tile), :], sem.at[b]
        )

    small = [
        pltpu.make_async_copy(a, b, small_sem.at[k])
        for k, (a, b) in enumerate(
            zip((*srcs_any, mine_any, theirs_any), (*srcs, mine_ref, theirs_ref))
        )
    ]
    for copy in small:
        copy.start()

    @pl.loop(0, n * per)
    def _(b):
        load(b).start()

    for copy in small:
        copy.wait()
    most = compact(srcs, ani * 2 * half + chain * half, key_s, y_s)
    acc[...] = jnp.zeros_like(acc)
    lanes_iota = lax.broadcasted_iota(jnp.int32, (2 * LANES, LANES), 0).astype(F32).astype(BF16)
    subs_iota = lax.broadcasted_iota(jnp.int32, (SUBS, LANES), 0).astype(F32).astype(BF16)

    @pl.loop(0, (most + CHUNK_ROWS - 1) // CHUNK_ROWS)
    def _(t):
        look_up(t, mine_ref, theirs_ref, e_rows, key_s, y_s, lane_s, sub_s, v_s)
        b, a = one_hots(t, lane_s, sub_s, v_s, lanes_iota, subs_iota)
        acc[...] += lax.dot_general(b, a, NT, preferred_element_type=F32)

    for q in range(n):
        wide, first = divmod(q * rows, SUBS)
        cols = slice(wide * LANES, (wide + 1) * LANES)
        window = lambda p: acc[p * SUBS + first : p * SUBS + first + rows, cols]
        tab[0, q] = window(0) + window(1)
        tab[1, q] = window(2) + window(3)
        tab[2, q] = window(4)
    for j in range(n):
        owner = lax.rem(rec + j, n)
        for p in range(3):
            outs[j][(2 + p) * rows : (3 + p) * rows, :] = tab[p, owner]

    e2 = jnp.concatenate(
        [
            jnp.concatenate([ref[i : i + 1, :] for i in range(e_rows)], axis=1)
            for ref in (mine_ref, theirs_ref)
        ]
        + [jnp.zeros((6, markers), F32)],
        axis=0,
    ).astype(BF16)

    @pl.loop(0, n * per)
    def _(b):
        load(b).wait()
        res = lax.dot_general(
            e2, kept_ref[pl.ds(place(b), tile), :], NT, preferred_element_type=F32
        )
        for i in range(tile // LANES):
            at = lax.rem(b, per) * (tile // LANES) + i
            gain[b // per, pl.ds(at, 1), :] = res[0:1, i * LANES : (i + 1) * LANES]
            gain[b // per, pl.ds(rows + at, 1), :] = res[1:2, i * LANES : (i + 1) * LANES]

    for j in range(n):
        outs[j][0 : 2 * rows, :] = gain[j]


def front(genotypes, mine, theirs, srcs, n):
    block, markers = genotypes.shape
    half = block // 2
    total = len(srcs) * srcs[0].shape[0] // 3
    rows = half // n // LANES
    tiles = half // min(TILE, half // n)
    return pl.pallas_call(
        functools.partial(front_kernel, n, len(srcs)),
        in_specs=[ANY] * (3 + len(srcs)),
        out_specs=[VMEM] * (1 + n),
        out_shape=[pltpu.VMEM((half, markers), BF16)]
        + [jax.ShapeDtypeStruct((5 * rows, LANES), F32)] * n,
        scratch_shapes=[
            pltpu.VMEM((total, LANES), jnp.int32),
            pltpu.VMEM((total, LANES), F32),
            pltpu.VMEM((total, LANES), F32),
            pltpu.VMEM((total, LANES), F32),
            pltpu.VMEM((4, total, LANES), F32),
            pltpu.VMEM((5 * SUBS, 2 * LANES), F32),
            pltpu.VMEM((3, n, rows, LANES), F32),
            pltpu.VMEM((n, 2 * rows, LANES), F32),
            pltpu.VMEM(mine.shape, F32),
            pltpu.VMEM(theirs.shape, F32),
            pltpu.VMEM((len(srcs),) + srcs[0].shape, F32),
            pltpu.SemaphoreType.DMA((tiles,)),
            pltpu.SemaphoreType.DMA((2 + len(srcs),)),
        ],
        compiler_params=pltpu.CompilerParams(vmem_limit_bytes=16 << 20),
        cost_estimate=pl.CostEstimate(
            flops=8 * half * markers, bytes_accessed=2 * half * markers, transcendentals=0
        ),
        name="front",
    )(*[pltpu.with_memory_space_constraint(x, pltpu.HBM) for x in (mine, theirs, *srcs)], genotypes)


def pinned(x):
    return pltpu.with_memory_space_constraint(x, pltpu.VMEM)


def combine_kernel(kept_ref, *refs):
    parts, out_ref = refs[:-1], refs[-1]
    rows = out_ref.shape[0] // 2
    total = parts[0][...]
    for part in parts[1:]:
        total = total + part[...]
    count = total[4 * rows :]
    for ch in range(2):
        gain = total[ch * rows : (ch + 1) * rows]
        out_ref[ch * rows : (ch + 1) * rows, :] = (
            total[(2 + ch) * rows : (3 + ch) * rows] - count * gain
        )


def combine(kept, parts):
    rows = parts[0].shape[0] // 5
    return pl.pallas_call(
        combine_kernel,
        in_specs=[VMEM] * (1 + len(parts)),
        out_specs=VMEM,
        out_shape=jax.ShapeDtypeStruct((2 * rows, LANES), F32),
        compiler_params=pltpu.CompilerParams(vmem_limit_bytes=16 << 20),
        cost_estimate=pl.CostEstimate(flops=1 << 16, bytes_accessed=1 << 16, transcendentals=0),
        name="combine",
    )(pinned(kept), *parts)


def product(kept_ref, parts, first, n):
    quarter = kept_ref.shape[0] // n
    rows = quarter // LANES
    rec = lax.axis_index("rec")
    total = jnp.zeros((8, kept_ref.shape[1]), F32)
    for j, part in enumerate(parts):
        cols = [
            jnp.concatenate(
                [part[i : i + 1, :], part[rows + i : rows + i + 1, :], jnp.zeros((6, LANES), F32)],
                axis=0,
            )
            for i in range(rows)
        ]
        lhs = jnp.concatenate(cols, axis=1).astype(BF16)
        at = pl.multiple_of(lax.rem(rec + first + j, n) * quarter, quarter)
        total = total + jnp.dot(
            lhs, kept_ref[pl.ds(at, quarter), :], preferred_element_type=F32
        )
    return total


def back_first_kernel(n, kept_ref, part_ref, out_ref):
    out_ref[...] = product(kept_ref, [part_ref], 0, n)


def back_first(kept, part, n):
    half, markers = kept.shape
    return pl.pallas_call(
        functools.partial(back_first_kernel, n),
        in_specs=[VMEM, VMEM],
        out_specs=VMEM,
        out_shape=jax.ShapeDtypeStruct((8, markers), F32),
        compiler_params=pltpu.CompilerParams(vmem_limit_bytes=16 << 20),
        cost_estimate=pl.CostEstimate(
            flops=4 * half // n * markers, bytes_accessed=2 * half // n * markers, transcendentals=0
        ),
        name="back_first",
    )(pinned(kept), part)


def back_rest_kernel(n, kept_ref, before_ref, *refs):
    parts, (own_ref, other_ref, theirs_ref) = refs[:n], refs[n:]
    rows = parts[0].shape[0] // 2
    for j in range(n):
        theirs_ref[j * rows : (j + 1) * rows, :] = parts[j][rows : 2 * rows, :]
    total = before_ref[...] + product(kept_ref, parts[1:], 1, n)
    for i in range(own_ref.shape[0]):
        own_ref[i : i + 1, :] = total[0:1, i * LANES : (i + 1) * LANES]
        other_ref[i : i + 1, :] = total[1:2, i * LANES : (i + 1) * LANES]


def back_rest(kept, before, parts, n):
    half, markers = kept.shape
    rows = half // n // LANES
    grad = jax.ShapeDtypeStruct((markers // LANES, LANES), F32)
    return pl.pallas_call(
        functools.partial(back_rest_kernel, n),
        in_specs=[VMEM] * (2 + n),
        out_specs=[VMEM] * 3,
        out_shape=[grad, grad, jax.ShapeDtypeStruct((n * rows, LANES), F32)],
        compiler_params=pltpu.CompilerParams(vmem_limit_bytes=16 << 20),
        cost_estimate=pl.CostEstimate(
            flops=4 * half * markers, bytes_accessed=2 * half * markers, transcendentals=0
        ),
        name="back_rest",
    )(pinned(kept), before, *parts)


def assemble_kernel(n, theirs_ref, *refs):
    parts, out_ref = refs[:n], refs[n]
    rows = parts[0].shape[0] // 2
    chain, rec = lax.axis_index("chain"), lax.axis_index("rec")
    for j in range(n):
        owner = lax.rem(rec + j, n)
        out_ref[chain * n + owner] = parts[j][0:rows, :]
        out_ref[(1 - chain) * n + owner] = theirs_ref[j * rows : (j + 1) * rows, :]


def assemble(theirs, parts, n):
    rows = parts[0].shape[0] // 2
    return pl.pallas_call(
        functools.partial(assemble_kernel, n),
        in_specs=[VMEM] * (1 + n),
        out_specs=VMEM,
        out_shape=jax.ShapeDtypeStruct((2 * n, rows, LANES), F32),
        name="assemble",
    )(theirs, *parts)


def on_device(
    n_rec,
    n_ani,
    genotypes,
    effects,
    gaussian_draw,
    prior_prec,
    accept,
    herd_effect,
    phenotype,
    record_animal,
    record_bin,
    live_records,
):
    step_size = 0.005
    rows = genotypes.shape[0] // 2 // n_rec // LANES

    raw, mine = prepare(
        live_records,
        tiled(record_animal),
        tiled(phenotype),
        tiled(record_bin),
        tiled(effects),
        tiled(herd_effect),
    )
    theirs = permute(mine, "chain", 2, 1)
    srcs = [raw] + [permute(raw, "ani", n_ani, k) for k in range(1, n_ani)]

    kept, *sums = front(genotypes, mine, theirs, srcs, n_rec)
    sums = [sums[0]] + [permute(sums[k], "rec", n_rec, k) for k in range(1, n_rec)]
    resid = combine(kept, sums)
    parts = [resid] + [permute(resid, "rec", n_rec, n_rec - k) for k in range(1, n_rec)]
    grads = back_first(kept, resid, n_rec)
    own, other, halves = back_rest(kept, grads, parts, n_rec)
    grad_part = (own + permute(other, "chain", 2, 1)).reshape(-1)
    swapped = permute(halves, "chain", 2, 1)
    resid_sum = assemble(swapped, parts, n_rec).reshape(-1)

    likelihood_grad = jnp.sum(lax.all_gather(grad_part, "ani"), axis=0)
    gradient = likelihood_grad - prior_prec * effects
    proposal = effects + step_size * gradient + math.sqrt(2.0 * step_size) * gaussian_draw
    accepted = jnp.repeat(accept, BLOCK) == 1
    return (jnp.where(accepted, proposal, effects), resid_sum)


def solution(mesh):
    return jax.shard_map(
        functools.partial(on_device, mesh.shape["rec"], mesh.shape["ani"]),
        mesh=mesh,
        in_specs=(
            P("ani", "rec"),
            P(("chain", "rec")),
            P(("chain", "rec")),
            P("rec"),
            P(("chain", "rec")),
            P(("chain", "rec")),
            P(("rec", "ani")),
            P(("rec", "ani")),
            P(("rec", "ani")),
            P(("rec", "ani")),
        ),
        out_specs=(P(("chain", "rec")), P(("chain", "ani"))),
        check_vma=False,
    )
```

time: 289 us -> 60.4 us (0.21)
  local copies, waits for them, and re-layouts: 94 us -> 1.93 us
  waiting for transfers between devices: 68.8 us -> 13 us
  matrix products: 49.6 us -> 0 us
  other arithmetic: 46.4 us -> 0.69 us
  Pallas kernels: 0 us -> 20.5 us
  starting transfers between devices: 0.12 us -> 17.2 us
  between operations: 15.2 us -> 1.42 us
  blocking collectives: 14.5 us -> 5.17 us
    gather x2 -> x0, local copies, waits for them, and re-layouts: 91.1 us -> none  [the longest x1 45.5 us: on_device(): herd_value = jnp.take(herd_effect, local_bin)]
    dot_general x2 -> x0, matrix products: 49.6 us -> none  [the longest x1 26.3 us: on_device(): jnp.dot(genotypes, effects_half, preferred_element_type=jnp.float32)]
    scatter-add x1 -> x0, other arithmetic: 44 us -> none  [on_device(): jax.ops.segment_sum(residual, record_animal, num_segments=animals)]
    psum x2 -> x0, waiting for transfers between devices: 35.9 us -> none  [the longest x1 35.9 us: on_device(): resid_sum = lax.psum(share, 'rec')]
    unnamed x4 -> x0, waiting for transfers between devices: 32.9 us -> none
    pallas_call x0 -> x6, Pallas kernels: none -> 20.5 us  [the longest x1 12.8 us: front(): pl.pallas_call(functools.partial(front_kernel, n, len(srcs)), in_specs=[A...]
    ppermute x0 -> x12, starting transfers between devices: none -> 17.2 us  [permute(): return lax.ppermute(x, axis, [(i, (i + shift) % size) for i in range(size)])]
    ppermute x0 -> x12, waiting for transfers between devices: none -> 13 us  [permute(): return lax.ppermute(x, axis, [(i, (i + shift) % size) for i in range(size)])]
  transfers between devices with their start and end apart: 3 -> 12, of which waited for: 2 -> 6; matrix products, arithmetic and copies ran while one was open for 16% -> 1% of each run, Pallas kernels for 0% -> 2%
where the time goes in v2:
time: 60.4 us; the launch traced here: 59.9 us
  Pallas kernels  20.5 us (34%)
  starting transfers between devices  17.2 us (28%)
  waiting for transfers between devices  13 us (22%)
  blocking collectives  5.17 us (9%)
  local copies, waits for them, and re-layouts  1.93 us (3%)
  between operations  1.42 us (2%)
  other arithmetic  0.69 us (1%)
    ppermute x12, starting transfers between devices, permute(): return lax.ppermute(x, axis, [(i, (i + shift) % size) for i in range(size)])  17.2 us
    ppermute x12, waiting for transfers between devices, permute(): return lax.ppermute(x, axis, [(i, (i + shift) % size) for i in range(size)])  13 us
    pallas_call x1, Pallas kernels, front(): pl.pallas_call(functools.partial(front_kernel, n, len(srcs)), in_specs=[A...  12.8 us
    all_gather x1, blocking collectives, on_device(): likelihood_grad = jnp.sum(lax.all_gather(grad_part, 'ani'), axis=0)  5.17 us
    pallas_call x1, Pallas kernels, back_rest(): pl.pallas_call(functools.partial(back_rest_kernel, n), in_specs=[VMEM] *...  3.4 us
    unnamed x26, local copies, waits for them, and re-layouts  1.93 us
    pallas_call x1, Pallas kernels, assemble(): pl.pallas_call(functools.partial(assemble_kernel, n), in_specs=[VMEM] * (...  1.55 us
    pallas_call x1, Pallas kernels, prepare(): pl.pallas_call(prepare_kernel, in_specs=[SMEM] + [VMEM] * 5, out_specs=[V...  1.47 us
  transfers between devices with their start and end apart: 12, of which 6 were waited for; matrix products, arithmetic and copies ran while one was open for 1% of the time, Pallas kernels for 2%

profile of v2, /device:TPU:0, one launch (start us, length us, event | category | flops | bytes accessed | tf_op | source)
XLA Modules:
  0.0 59.9 jit_solution(9660869883527256757)
XLA Ops:
  1.3 1.5 %prepare.1 = (f32[192,128]{1,0:T(8,128)}, f32[24,128]{1,0:T(8,128)}) custom-call(s32[1]{0:T(128)S(6)} %copy.12.live_ref, s32[64,128]{1,0:T(8,128)} %bitcast.10, f32[64,128]{1,0:T(8,128)} %bitcast.11, s32[64,128]{1,0:T(8,128)} %bitcast.12, f32[8,128]{1,0:T(8,128)} %bitcast.13, f32[16,128]{1,0:T(8,128)} %bitcast.15), custom_call_target="tpu_custom_call" | custom-call | tf_op jit(solution)/shard_map/prepare/pallas_call | solution.py:49
  2.7 0.5 collective-permute-start.1
  3.2 2.5 %collective-permute-start.2 = (f32[192,128]{1,0:T(8,128)}, f32[192,128]{1,0:T(8,128)S(1)}, u32[]{:S(2)}, u32[]{:S(2)}) collective-permute-start(f32[192,128]{1,0:T(8,128)} %get-tuple-element.13.refs_0_), channel_id=1, source_target_pairs={{0,4},{2,6},{4,0},{6,2},{1,5},{3,7},{5,1},{7,3},{8,12},{10,14},{12... | collective-permute-start | bytes 294920 | tf_op jit(solution)/shard_map/ppermute | solution.py:26
  5.7 1.4 %collective-permute-start.3 = (f32[192,128]{1,0:T(8,128)}, f32[192,128]{1,0:T(8,128)S(1)}, u32[]{:S(2)}, u32[]{:S(2)}) collective-permute-start(f32[192,128]{1,0:T(8,128)} %get-tuple-element.13.refs_0_), channel_id=1, source_target_pairs={{0,6},{2,0},{4,2},{6,4},{1,7},{3,1},{5,3},{7,5},{8,14},{10,8},{12,... | collective-permute-start | bytes 294920 | tf_op jit(solution)/shard_map/ppermute | solution.py:26
  7.2 1.5 %collective-permute-start = (f32[24,128]{1,0:T(8,128)}, f32[24,128]{1,0:T(8,128)S(1)}, u32[]{:S(2)}, u32[]{:S(2)}) collective-permute-start(f32[24,128]{1,0:T(8,128)} %get-tuple-element.12.mine_any), channel_id=1, source_target_pairs={{0,1},{1,0},{2,3},{3,2},{4,5},{5,4},{6,7},{7,6},{8,9},{9,8},{10,11... | collective-permute-start | bytes 36872 | tf_op jit(solution)/shard_map/ppermute | solution.py:26
  8.7 2.4 %collective-permute-done.theirs_any = f32[24,128]{1,0:T(8,128)S(1)} collective-permute-done((f32[24,128]{1,0:T(8,128)}, f32[24,128]{1,0:T(8,128)S(1)}, u32[]{:S(2)}, u32[]{:S(2)}) %collective-permute-start) | collective-permute-done | bytes 12320 | tf_op jit(solution)/shard_map/ppermute | solution.py:26
  11.1 0.6 copy-done.9
  11.7 0.0 copy-done.4
  11.7 0.0 copy-done.5
  11.7 0.6 %copy-done.6 = f32[192,128]{1,0:T(8,128)} copy-done((f32[192,128]{1,0:T(8,128)}, f32[192,128]{1,0:T(8,128)S(1)}, u32[]{:S(2)}) %copy-start.6) | copy-done | bytes 98328
  12.4 12.8 %front.1 = (bf16[16384,1024]{1,0:T(8,128)(2,1)S(1)}, f32[160,128]{1,0:T(8,128)S(1)}, f32[160,128]{1,0:T(8,128)S(1)}, f32[160,128]{1,0:T(8,128)S(1)}, f32[160,128]{1,0:T(8,128)S(1)}) custom-call(f32[24,128]{1,0:T(8,128)} %get-tuple-element.12.mine_any, f32[24,128]{1,0:T(8,128)} %copy-done.9, f32[192,128]{1,0:T(8,128)} %get-tuple-element.13.refs_0_, ...), custom_call_target="tpu_custom_call" | custom-call | flops 134217728 | bytes 33554432 | tf_op jit(solution)/shard_map/front/pallas_call | solution.py:237
  25.2 0.0 copy-start.12
  25.3 2.2 %collective-permute-start.4 = (f32[160,128]{1,0:T(8,128)S(1)}, f32[160,128]{1,0:T(8,128)S(1)}, u32[]{:S(2)}, u32[]{:S(2)}) collective-permute-start(f32[160,128]{1,0:T(8,128)S(1)} %get-tuple-element.16), channel_id=1, source_target_pairs={{0,8},{8,16},{16,24},{24,0},{1,9},{9,17},{17,25},{25,1},{2,10},{10... | collective-permute-start | bytes 245768 | tf_op jit(solution)/shard_map/ppermute | solution.py:26
  27.5 2.6 %collective-permute-start.5 = (f32[160,128]{1,0:T(8,128)S(1)}, f32[160,128]{1,0:T(8,128)S(1)}, u32[]{:S(2)}, u32[]{:S(2)}) collective-permute-start(f32[160,128]{1,0:T(8,128)S(1)} %get-tuple-element.17), channel_id=1, source_target_pairs={{0,16},{8,24},{16,0},{24,8},{1,17},{9,25},{17,1},{25,9},{2,18},{10... | collective-permute-start | bytes 245768 | tf_op jit(solution)/shard_map/ppermute | solution.py:26
  30.1 0.8 %collective-permute-start.6 = (f32[160,128]{1,0:T(8,128)S(1)}, f32[160,128]{1,0:T(8,128)S(1)}, u32[]{:S(2)}, u32[]{:S(2)}) collective-permute-start(f32[160,128]{1,0:T(8,128)S(1)} %get-tuple-element.18), channel_id=1, source_target_pairs={{0,24},{8,0},{16,8},{24,16},{1,25},{9,1},{17,9},{25,17},{2,26},{10... | collective-permute-start | bytes 245768 | tf_op jit(solution)/shard_map/ppermute | solution.py:26
  30.8 2.0 %collective-permute-done.4.refs_1_ = f32[160,128]{1,0:T(8,128)S(1)} collective-permute-done((f32[160,128]{1,0:T(8,128)S(1)}, f32[160,128]{1,0:T(8,128)S(1)}, u32[]{:S(2)}, u32[]{:S(2)}) %collective-permute-start.4) | collective-permute-done | bytes 81952 | tf_op jit(solution)/shard_map/ppermute | solution.py:26
  32.8 2.8 %collective-permute-done.5.refs_2_ = f32[160,128]{1,0:T(8,128)S(1)} collective-permute-done((f32[160,128]{1,0:T(8,128)S(1)}, f32[160,128]{1,0:T(8,128)S(1)}, u32[]{:S(2)}, u32[]{:S(2)}) %collective-permute-start.5) | collective-permute-done | bytes 81952 | tf_op jit(solution)/shard_map/ppermute | solution.py:26
  35.6 0.0 collective-permute-done.6.refs_3_
  35.7 3.0 %collective-permute-start.7 = (f32[64,128]{1,0:T(8,128)S(1)}, f32[64,128]{1,0:T(8,128)S(1)}, u32[]{:S(2)}, u32[]{:S(2)}) collective-permute-start(f32[64,128]{1,0:T(8,128)S(1)} %combine.1.part_ref.refs_0_), channel_id=1, source_target_pairs={{0,24},{8,0},{16,8},{24,16},{1,25},{9,1},{17,9},{25,17},{2,26},{10... | collective-permute-start | bytes 98312 | tf_op jit(solution)/shard_map/ppermute | solution.py:26
  38.6 0.4 collective-permute-start.8
  39.0 0.2 collective-permute-start.9
  39.3 1.2 %back_first.1.before_ref = f32[8,1024]{1,0:T(8,128)S(1)} custom-call(bf16[16384,1024]{1,0:T(8,128)(2,1)S(1)} %get-tuple-element.14.kept_ref, f32[64,128]{1,0:T(8,128)S(1)} %combine.1.part_ref.refs_0_), custom_call_target="tpu_custom_call" | custom-call | flops 16777216 | bytes 8388608 | tf_op jit(solution)/shard_map/back_first/pallas_call | solution.py:324
  40.4 3.0 %collective-permute-done.8.refs_2_ = f32[64,128]{1,0:T(8,128)S(1)} collective-permute-done((f32[64,128]{1,0:T(8,128)S(1)}, f32[64,128]{1,0:T(8,128)S(1)}, u32[]{:S(2)}, u32[]{:S(2)}) %collective-permute-start.8) | collective-permute-done | bytes 32800 | tf_op jit(solution)/shard_map/ppermute | solution.py:26
  43.4 1.3 %collective-permute-done.9.refs_3_ = f32[64,128]{1,0:T(8,128)S(1)} collective-permute-done((f32[64,128]{1,0:T(8,128)S(1)}, f32[64,128]{1,0:T(8,128)S(1)}, u32[]{:S(2)}, u32[]{:S(2)}) %collective-permute-start.9) | collective-permute-done | bytes 32800 | tf_op jit(solution)/shard_map/ppermute | solution.py:26
  44.8 3.4 %back_rest.1 = (f32[8,128]{1,0:T(8,128)S(1)}, f32[8,128]{1,0:T(8,128)S(1)}, f32[128,128]{1,0:T(8,128)S(1)}) custom-call(bf16[16384,1024]{1,0:T(8,128)(2,1)S(1)} %get-tuple-element.14.kept_ref, f32[8,1024]{1,0:T(8,128)S(1)} %back_first.1.before_ref, f32[64,128]{1,0:T(8,128)S(1)} %combine.1.part_ref.refs_0_, f32[64,128]{1,0:T(8,128)S(1)} %collective-permute-done.7.refs_1_, ...), custom_call_target="tpu_custom_call" | custom-call | flops 67108864 | bytes 33554432 | tf_op jit(solution)/shard_map/back_rest/pallas_call | solution.py:352
  48.2 2.1 %collective-permute-start.10 = (f32[8,128]{1,0:T(8,128)S(1)}, f32[8,128]{1,0:T(8,128)S(1)}, u32[]{:S(2)}, u32[]{:S(2)}) collective-permute-start(f32[8,128]{1,0:T(8,128)S(1)} %get-tuple-element.20), channel_id=1, source_target_pairs={{0,1},{1,0},{2,3},{3,2},{4,5},{5,4},{6,7},{7,6},{8,9},{9,8},{10,11... | collective-permute-start | bytes 12296 | tf_op jit(solution)/shard_map/ppermute | solution.py:26
  50.2 0.1 collective-permute-start.11
  50.3 1.5 %collective-permute-done.10 = f32[8,128]{1,0:T(8,128)S(1)} collective-permute-done((f32[8,128]{1,0:T(8,128)S(1)}, f32[8,128]{1,0:T(8,128)S(1)}, u32[]{:S(2)}, u32[]{:S(2)}) %collective-permute-start.10) | collective-permute-done | bytes 4128 | tf_op jit(solution)/shard_map/ppermute | solution.py:26
  51.8 5.2 %all-gather = f32[4,1,1024]{2,1,0:T(1,128)S(1)} all-gather(f32[1,1,1024]{2,1,0:T(1,128)S(1)} %bitcast.14), channel_id=1, replica_groups=mesh['rec'=4,'ani'=4,'chain'=2] {'ani'}, dimensions={0}, use_global_device_ids=true | all-gather | bytes 20480 | tf_op jit(solution)/shard_map/all_gather | solution.py:424
  57.0 0.7 %add_select_fusion = f32[1024]{0:T(1024)} fusion(f32[1024]{0:T(1024)S(1)} %copy-done.8, f32[1024]{0:T(1024)S(1)} %copy-done.10, f32[1024]{0:T(1024)S(1)} %reduce_sum.9, f32[1024]{0:T(1024)S(1)} %copy-done.11, pred[8]{0:T(512)(128)(4,1)S(1)} %broadcast_compare_fusion), kind=kLoop, calls=%fused_computation | loop fusion | flops 7168 | bytes 20488 | tf_op jit(solution)/shard_map/jit(_where)/select_n | solution.py:428
  57.7 0.6 %copy-done.7 = f32[128,128]{1,0:T(8,128)} copy-done((f32[128,128]{1,0:T(8,128)}, f32[128,128]{1,0:T(8,128)S(1)}, u32[]{:S(2)}) %copy-start.7) | copy-done | bytes 65560
  58.4 1.6 %assemble.1 = f32[8,32,128]{2,1,0:T(8,128)} custom-call(f32[128,128]{1,0:T(8,128)} %copy-done.7, f32[64,128]{1,0:T(8,128)} %copy-done, f32[64,128]{1,0:T(8,128)} %copy-done.1, f32[64,128]{1,0:T(8,128)} %copy-done.2, f32[64,128]{1,0:T(8,128)} %copy-done.3), custom_call_target="tpu_custom_call" | custom-call | tf_op jit(solution)/shard_map/assemble/pallas_call | solution.py:377
  (29 shorter events, 0.1 us)
Async XLA Ops:
  2.7 8.3 %collective-permute-start.1 = (f32[192,128]{1,0:T(8,128)}, f32[192,128]{1,0:T(8,128)S(1)}, u32[]{:S(2)}, u32[]{:S(2)}) collective-permute-start(f32[192,128]{1,0:T(8,128)} %get-tuple-element.13.refs_0_), channel_id=1, source_target_pairs={{0,2},{2,4},{4,6},{6,0},{1,3},{3,5},{5,7},{7,1},{8,10},{10,12},{12... | collective-permute-start | bytes 294920 | tf_op jit(solution)/shard_map/ppermute | solution.py:26
  3.2 7.9 %collective-permute-start.2 = (f32[192,128]{1,0:T(8,128)}, f32[192,128]{1,0:T(8,128)S(1)}, u32[]{:S(2)}, u32[]{:S(2)}) collective-permute-start(f32[192,128]{1,0:T(8,128)} %get-tuple-element.13.refs_0_), channel_id=1, source_target_pairs={{0,4},{2,6},{4,0},{6,2},{1,5},{3,7},{5,1},{7,3},{8,12},{10,14},{12... | collective-permute-start | bytes 294920 | tf_op jit(solution)/shard_map/ppermute | solution.py:26
  5.7 5.4 %collective-permute-start.3 = (f32[192,128]{1,0:T(8,128)}, f32[192,128]{1,0:T(8,128)S(1)}, u32[]{:S(2)}, u32[]{:S(2)}) collective-permute-start(f32[192,128]{1,0:T(8,128)} %get-tuple-element.13.refs_0_), channel_id=1, source_target_pairs={{0,6},{2,0},{4,2},{6,4},{1,7},{3,1},{5,3},{7,5},{8,14},{10,8},{12,... | collective-permute-start | bytes 294920 | tf_op jit(solution)/shard_map/ppermute | solution.py:26
  7.2 3.9 %collective-permute-start = (f32[24,128]{1,0:T(8,128)}, f32[24,128]{1,0:T(8,128)S(1)}, u32[]{:S(2)}, u32[]{:S(2)}) collective-permute-start(f32[24,128]{1,0:T(8,128)} %get-tuple-element.12.mine_any), channel_id=1, source_target_pairs={{0,1},{1,0},{2,3},{3,2},{4,5},{5,4},{6,7},{7,6},{8,9},{9,8},{10,11... | collective-permute-start | bytes 36872 | tf_op jit(solution)/shard_map/ppermute | solution.py:26
  11.1 0.6 copy-start.9
  11.1 0.6 %copy-start.4 = (f32[192,128]{1,0:T(8,128)}, f32[192,128]{1,0:T(8,128)S(1)}, u32[]{:S(2)}) copy-start(f32[192,128]{1,0:T(8,128)S(1)} %collective-permute-done.1.refs_1_) | copy-start | bytes 294916
  11.1 0.7 %copy-start.5 = (f32[192,128]{1,0:T(8,128)}, f32[192,128]{1,0:T(8,128)S(1)}, u32[]{:S(2)}) copy-start(f32[192,128]{1,0:T(8,128)S(1)} %collective-permute-done.2.refs_2_) | copy-start | bytes 294916
  11.7 0.6 %copy-start.6 = (f32[192,128]{1,0:T(8,128)}, f32[192,128]{1,0:T(8,128)S(1)}, u32[]{:S(2)}) copy-start(f32[192,128]{1,0:T(8,128)S(1)} %collective-permute-done.3.refs_3_) | copy-start | bytes 294916
  25.2 25.0 %copy-start.12 = (s32[8]{0:T(128)S(1)}, s32[8]{0:T(128)}, u32[]{:S(2)}) copy-start(s32[8]{0:T(128)} %param.14) | copy-start | bytes 100
  25.2 31.8 %copy-start.8 = (f32[1024]{0:T(1024)S(1)}, f32[1024]{0:T(1024)}, u32[]{:S(2)}) copy-start(f32[1024]{0:T(1024)} %param.11) | copy-start | bytes 12292
  25.2 31.8 %copy-start.10 = (f32[1024]{0:T(1024)S(1)}, f32[1024]{0:T(1024)}, u32[]{:S(2)}) copy-start(f32[1024]{0:T(1024)} %param.12) | copy-start | bytes 12292
  25.3 31.8 %copy-start.11 = (f32[1024]{0:T(1024)S(1)}, f32[1024]{0:T(1024)}, u32[]{:S(2)}) copy-start(f32[1024]{0:T(1024)} %param.13) | copy-start | bytes 12292
  25.3 7.5 %collective-permute-start.4 = (f32[160,128]{1,0:T(8,128)S(1)}, f32[160,128]{1,0:T(8,128)S(1)}, u32[]{:S(2)}, u32[]{:S(2)}) collective-permute-start(f32[160,128]{1,0:T(8,128)S(1)} %get-tuple-element.16), channel_id=1, source_target_pairs={{0,8},{8,16},{16,24},{24,0},{1,9},{9,17},{17,25},{25,1},{2,10},{10... | collective-permute-start | bytes 245768 | tf_op jit(solution)/shard_map/ppermute | solution.py:26
  27.5 8.1 %collective-permute-start.5 = (f32[160,128]{1,0:T(8,128)S(1)}, f32[160,128]{1,0:T(8,128)S(1)}, u32[]{:S(2)}, u32[]{:S(2)}) collective-permute-start(f32[160,128]{1,0:T(8,128)S(1)} %get-tuple-element.17), channel_id=1, source_target_pairs={{0,16},{8,24},{16,0},{24,8},{1,17},{9,25},{17,1},{25,9},{2,18},{10... | collective-permute-start | bytes 245768 | tf_op jit(solution)/shard_map/ppermute | solution.py:26
  30.1 5.5 %collective-permute-start.6 = (f32[160,128]{1,0:T(8,128)S(1)}, f32[160,128]{1,0:T(8,128)S(1)}, u32[]{:S(2)}, u32[]{:S(2)}) collective-permute-start(f32[160,128]{1,0:T(8,128)S(1)} %get-tuple-element.18), channel_id=1, source_target_pairs={{0,24},{8,0},{16,8},{24,16},{1,25},{9,1},{17,9},{25,17},{2,26},{10... | collective-permute-start | bytes 245768 | tf_op jit(solution)/shard_map/ppermute | solution.py:26
  35.6 22.1 %copy-start = (f32[64,128]{1,0:T(8,128)}, f32[64,128]{1,0:T(8,128)S(1)}, u32[]{:S(2)}) copy-start(f32[64,128]{1,0:T(8,128)S(1)} %combine.1.part_ref.refs_0_) | copy-start | bytes 98308
  35.7 4.8 %collective-permute-start.7 = (f32[64,128]{1,0:T(8,128)S(1)}, f32[64,128]{1,0:T(8,128)S(1)}, u32[]{:S(2)}, u32[]{:S(2)}) collective-permute-start(f32[64,128]{1,0:T(8,128)S(1)} %combine.1.part_ref.refs_0_), channel_id=1, source_target_pairs={{0,24},{8,0},{16,8},{24,16},{1,25},{9,1},{17,9},{25,17},{2,26},{10... | collective-permute-start | bytes 98312 | tf_op jit(solution)/shard_map/ppermute | solution.py:26
  38.6 4.8 %collective-permute-start.8 = (f32[64,128]{1,0:T(8,128)S(1)}, f32[64,128]{1,0:T(8,128)S(1)}, u32[]{:S(2)}, u32[]{:S(2)}) collective-permute-start(f32[64,128]{1,0:T(8,128)S(1)} %combine.1.part_ref.refs_0_), channel_id=1, source_target_pairs={{0,16},{8,24},{16,0},{24,8},{1,17},{9,25},{17,1},{25,9},{2,18},{10... | collective-permute-start | bytes 98312 | tf_op jit(solution)/shard_map/ppermute | solution.py:26
  39.0 5.7 %collective-permute-start.9 = (f32[64,128]{1,0:T(8,128)S(1)}, f32[64,128]{1,0:T(8,128)S(1)}, u32[]{:S(2)}, u32[]{:S(2)}) collective-permute-start(f32[64,128]{1,0:T(8,128)S(1)} %combine.1.part_ref.refs_0_), channel_id=1, source_target_pairs={{0,8},{8,16},{16,24},{24,0},{1,9},{9,17},{17,25},{25,1},{2,10},{10... | collective-permute-start | bytes 98312 | tf_op jit(solution)/shard_map/ppermute | solution.py:26
  40.4 17.3 %copy-start.1 = (f32[64,128]{1,0:T(8,128)}, f32[64,128]{1,0:T(8,128)S(1)}, u32[]{:S(2)}) copy-start(f32[64,128]{1,0:T(8,128)S(1)} %collective-permute-done.7.refs_1_) | copy-start | bytes 98308
  43.4 14.3 %copy-start.2 = (f32[64,128]{1,0:T(8,128)}, f32[64,128]{1,0:T(8,128)S(1)}, u32[]{:S(2)}) copy-start(f32[64,128]{1,0:T(8,128)S(1)} %collective-permute-done.8.refs_2_) | copy-start | bytes 98308
  44.8 13.0 %copy-start.3 = (f32[64,128]{1,0:T(8,128)}, f32[64,128]{1,0:T(8,128)S(1)}, u32[]{:S(2)}) copy-start(f32[64,128]{1,0:T(8,128)S(1)} %collective-permute-done.9.refs_3_) | copy-start | bytes 98308
  48.2 3.6 %collective-permute-start.10 = (f32[8,128]{1,0:T(8,128)S(1)}, f32[8,128]{1,0:T(8,128)S(1)}, u32[]{:S(2)}, u32[]{:S(2)}) collective-permute-start(f32[8,128]{1,0:T(8,128)S(1)} %get-tuple-element.20), channel_id=1, source_target_pairs={{0,1},{1,0},{2,3},{3,2},{4,5},{5,4},{6,7},{7,6},{8,9},{9,8},{10,11... | collective-permute-start | bytes 12296 | tf_op jit(solution)/shard_map/ppermute | solution.py:26
  50.2 7.5 %collective-permute-start.11 = (f32[128,128]{1,0:T(8,128)S(1)}, f32[128,128]{1,0:T(8,128)S(1)}, u32[]{:S(2)}, u32[]{:S(2)}) collective-permute-start(f32[128,128]{1,0:T(8,128)S(1)} %get-tuple-element.21), channel_id=1, source_target_pairs={{0,1},{1,0},{2,3},{3,2},{4,5},{5,4},{6,7},{7,6},{8,9},{9,8},{10,11... | collective-permute-start | bytes 196616 | tf_op jit(solution)/shard_map/ppermute | solution.py:26
  57.7 0.6 %copy-start.7 = (f32[128,128]{1,0:T(8,128)}, f32[128,128]{1,0:T(8,128)S(1)}, u32[]{:S(2)}) copy-start(f32[128,128]{1,0:T(8,128)S(1)} %collective-permute-done.11.theirs_ref) | copy-start | bytes 196612

commit v3 on v2

v3 whole, which is shorter than its diff:
```python
import functools
import math

import jax
import jax.numpy as jnp
from jax import lax
from jax.experimental import pallas as pl
from jax.experimental.pallas import tpu as pltpu
from jax.sharding import PartitionSpec as P

BLOCK = 128
LANES = 128
SUBS = 64
SPAN_BITS = 14
CHUNK_ROWS = 16
TILE = 1024
LIMIT = 14 << 20
F32 = jnp.float32
BF16 = jnp.bfloat16
NT = (((1,), (1,)), ((), ()))
VMEM = pl.BlockSpec(memory_space=pltpu.VMEM)
SMEM = pl.BlockSpec(memory_space=pltpu.SMEM)
ANY = pl.BlockSpec(memory_space=pl.ANY)


def swap(x, axis, size, j):
    return lax.ppermute(x, axis, [(i, i ^ j) for i in range(size)])


def tiled(x):
    return x.reshape(-1, LANES)


def prepare_kernel(bins, live_ref, animal_ref, y_ref, bin_ref, raw_ref):
    rows = animal_ref.shape[0]
    slot = (
        lax.broadcasted_iota(jnp.int32, (rows, LANES), 0) * LANES
        + lax.broadcasted_iota(jnp.int32, (rows, LANES), 1)
    )
    first_bin = lax.axis_index("rec") * bins
    raw_ref[0:rows, :] = jnp.where(slot < live_ref[...], animal_ref[...], -1).astype(F32)
    raw_ref[rows : 2 * rows, :] = y_ref[...]
    raw_ref[2 * rows : 3 * rows, :] = (bin_ref[...] - first_bin).astype(F32)


def prepare(bins, live, animal, y, which):
    rows = animal.shape[0]
    return pl.pallas_call(
        functools.partial(prepare_kernel, bins),
        in_specs=[VMEM] * 4,
        out_specs=VMEM,
        out_shape=pltpu.HBM((3 * rows, LANES), F32),
        name="prepare",
    )(live, animal, y, which)


def up(x, k):
    return jnp.concatenate([x[k:], jnp.zeros((k,) + x.shape[1:], x.dtype)], axis=0)


def down(x, k):
    return jnp.concatenate([jnp.zeros((k,) + x.shape[1:], x.dtype), x[:-k]], axis=0)


def compact(srcs, base, key_s, y_s):
    src_rows = srcs[0].shape[0] // 3
    keys, ys = [], []
    for src in srcs:
        local = src[0:src_rows, :].astype(jnp.int32) - base
        which = src[2 * src_rows : 3 * src_rows, :].astype(jnp.int32)
        known = (local >= 0) & (local < (1 << SPAN_BITS))
        keys.append(jnp.where(known, (which << SPAN_BITS) + local, -1))
        ys.append(src[src_rows : 2 * src_rows, :])
    key = jnp.concatenate(keys, axis=0)
    y = jnp.concatenate(ys, axis=0)
    total = key.shape[0]
    gone = jnp.where(key < 0, 1, 0)
    left = gone
    k = 1
    while k < total:
        left = left + down(left, k)
        k *= 2
    most = total - jnp.min(left[total - 1 : total, :])
    left = left - gone
    k = 1
    while k < total:
        move = (key >= 0) & ((left & k) != 0)
        key_up = up(jnp.where(move, key, -1), k)
        key_up = jnp.concatenate([key_up[: total - k], jnp.full((k, LANES), -1, jnp.int32)], axis=0)
        come = key_up >= 0
        key = jnp.where(come, key_up, jnp.where(move, -1, key))
        y = jnp.where(come, up(y, k), y)
        left = jnp.where(come, up(left, k), left)
        k *= 2
    key_s[...] = key
    y_s[...] = y
    return most


def look_up(t, herds, key_s, y_s, lane_s, sub_s, v_s):
    for g in range(CHUNK_ROWS // 8):
        at = pl.ds(pl.multiple_of(t * CHUNK_ROWS + g * 8, 8), 8)
        key, y = key_s[at, :], y_s[at, :]
        local, which = key & ((1 << SPAN_BITS) - 1), key >> SPAN_BITS
        lane = (local & (LANES - 1)) | ((local >> 13) << 7)
        lane_s[at, :] = jnp.where(key >= 0, lane, -1).astype(F32)
        sub_s[at, :] = ((local >> 7) & (SUBS - 1)).astype(F32)
        low, high = which & (LANES - 1), which >> 7
        for ch, ref in enumerate(herds):
            found = jnp.zeros((8, LANES), F32)
            for q in range(ref.shape[0]):
                row = jnp.broadcast_to(ref[q : q + 1, :], (8, LANES))
                got = jnp.take_along_axis(row, low, axis=1, mode="promise_in_bounds")
                found = jnp.where(high == q, got, found)
            value = y - found
            upper = value.astype(BF16).astype(F32)
            v_s[2 * ch, at, :] = upper
            v_s[2 * ch + 1, at, :] = value - upper


def spread(row, count):
    few = jnp.broadcast_to(row, (16, LANES)).astype(BF16)
    return jnp.broadcast_to(few[None], (count // 16, 16, LANES)).reshape(count, LANES)


def one_hots(t, lane_s, sub_s, v_s, lanes_iota, subs_iota):
    a_cols, b_cols = [], []
    one, zero = jnp.ones((), BF16), jnp.zeros((), BF16)
    for i in range(CHUNK_ROWS):
        at = pl.ds(t * CHUNK_ROWS + i, 1)
        a_cols.append(jnp.where(lanes_iota == spread(lane_s[at, :], 2 * LANES), one, zero))
        mask = subs_iota == spread(sub_s[at, :], SUBS)
        pieces = [jnp.where(mask, spread(v_s[p, at, :], SUBS), zero) for p in range(4)]
        pieces.append(jnp.where(mask, one, zero))
        b_cols.append(jnp.concatenate(pieces, axis=0))
    return jnp.concatenate(b_cols, axis=1), jnp.concatenate(a_cols, axis=1)


def gains(e2, kept_ref, at, count, out_ref, row, rows):
    res = lax.dot_general(e2, kept_ref[pl.ds(at, count), :], NT, preferred_element_type=F32)
    for i in range(count // LANES):
        for ch in range(2):
            out_ref[pl.ds(ch * rows + row + i, 1), :] = res[
                ch : ch + 1, i * LANES : (i + 1) * LANES
            ]


def front_a_kernel(n, own_any, other_any, g_hbm, kept_ref, gains_any, gain, own_s, other_s, sem, small_sem, out_sem):
    markers = kept_ref.shape[1]
    quarter = (kept_ref.shape[0] - 16) // (n // 2)
    chain, rec = lax.axis_index("chain"), lax.axis_index("rec")
    small = [
        pltpu.make_async_copy(a, b, small_sem.at[k])
        for k, (a, b) in enumerate([(own_any, own_s), (other_any, other_s)])
    ]
    for copy in small:
        copy.start()
    tile = min(TILE, quarter)
    per = quarter // tile
    rows = quarter // LANES

    def load(b):
        at = chain * quarter * n + (rec ^ (b // per)) * quarter + lax.rem(b, per) * tile
        return pltpu.make_async_copy(
            g_hbm.at[pl.ds(pl.multiple_of(at, tile), tile), :],
            kept_ref.at[pl.ds(pl.multiple_of(b * tile, tile), tile), :],
            sem.at[b],
        )

    @pl.loop(0, n // 2 * per)
    def _(b):
        load(b).start()

    for copy in small:
        copy.wait()
    e2 = jnp.concatenate(
        [
            jnp.concatenate([ref[i : i + 1, :] for i in range(markers // LANES)], axis=1)
            for ref in (own_s, other_s)
        ]
        + [jnp.zeros((14, markers), F32)],
        axis=0,
    ).astype(BF16)
    kept_ref[(n // 2) * quarter :, :] = e2

    @pl.loop(0, n // 2 * per)
    def _(b):
        load(b).wait()
        at = pl.multiple_of(b * tile, tile)
        gains(e2[:8], kept_ref, at, tile, gain.at[b // per], lax.rem(b, per) * (tile // LANES), rows)

    done = pltpu.make_async_copy(gain, gains_any, out_sem)
    done.start()
    done.wait()


def front_a(genotypes, effects, n):
    block, markers = genotypes.shape
    half = block // 2
    quarter = half // n
    rows = quarter // LANES
    tiles = n // 2 * (quarter // min(TILE, quarter))
    shape = (n // 2, 2 * rows, LANES)
    return pl.pallas_call(
        functools.partial(front_a_kernel, n),
        in_specs=[ANY] * 3,
        out_specs=[VMEM, ANY],
        out_shape=[pltpu.VMEM((n // 2 * quarter + 16, markers), BF16), pltpu.HBM(shape, F32)],
        scratch_shapes=[
            pltpu.VMEM(shape, F32),
            pltpu.VMEM(effects[0].shape, F32),
            pltpu.VMEM(effects[1].shape, F32),
            pltpu.SemaphoreType.DMA((tiles,)),
            pltpu.SemaphoreType.DMA((2,)),
            pltpu.SemaphoreType.DMA,
        ],
        compiler_params=pltpu.CompilerParams(vmem_limit_bytes=LIMIT),
        cost_estimate=pl.CostEstimate(
            flops=2 * half * markers, bytes_accessed=half * markers, transcendentals=0
        ),
        name="front_a",
    )(*[pltpu.with_memory_space_constraint(x, pltpu.HBM) for x in effects], genotypes)


def front_b_kernel(n, n_src, kept_a_ref, *refs):
    small_any, g_hbm, kept_ref = refs[: n_src + 3], refs[n_src + 3], refs[n_src + 4]
    outs = refs[n_src + 5 : n_src + 5 + n]
    key_s, y_s, lane_s, sub_s, v_s, acc, tab, *small_s, sem, small_sem = refs[n_src + 5 + n :]
    quarter = kept_ref.shape[0] // (n // 2)
    half = quarter * n
    rows = quarter // LANES
    chain, rec, ani = lax.axis_index("chain"), lax.axis_index("rec"), lax.axis_index("ani")

    small = [
        pltpu.make_async_copy(a, b, small_sem.at[k])
        for k, (a, b) in enumerate(zip(small_any, small_s))
    ]
    for copy in small:
        copy.start()
    big = []
    for slot in range(n // 2):
        at = pl.multiple_of(chain * half + (rec ^ (n // 2 + slot)) * quarter, quarter)
        big.append(
            pltpu.make_async_copy(
                g_hbm.at[pl.ds(at, quarter), :],
                kept_ref.at[slot * quarter : (slot + 1) * quarter, :],
                sem.at[slot],
            )
        )
        big[-1].start()
    for copy in small:
        copy.wait()
    srcs, (*herds, gain_a) = small_s[:n_src], small_s[n_src:]

    most = compact(srcs, ani * 2 * half + chain * half, key_s, y_s)
    acc[...] = jnp.zeros_like(acc)
    lanes_iota = lax.broadcasted_iota(jnp.int32, (2 * LANES, LANES), 0).astype(F32).astype(BF16)
    subs_iota = lax.broadcasted_iota(jnp.int32, (SUBS, LANES), 0).astype(F32).astype(BF16)

    @pl.loop(0, (most + CHUNK_ROWS - 1) // CHUNK_ROWS)
    def _(t):
        look_up(t, herds, key_s, y_s, lane_s, sub_s, v_s)
        b, a = one_hots(t, lane_s, sub_s, v_s, lanes_iota, subs_iota)
        acc[...] += lax.dot_general(b, a, NT, preferred_element_type=F32)

    for q in range(n):
        wide, first = divmod(q * rows, SUBS)
        cols = slice(wide * LANES, (wide + 1) * LANES)
        window = lambda p: acc[p * SUBS + first : p * SUBS + first + rows, cols]
        tab[q, 0:rows, :] = window(0) + window(1)
        tab[q, rows : 2 * rows, :] = window(2) + window(3)
        tab[q, 2 * rows : 3 * rows, :] = window(4)
    for j in range(n):
        outs[j][2 * rows : 5 * rows, :] = tab[rec ^ j]
    for j in range(n // 2):
        outs[j][0 : 2 * rows, :] = gain_a[j]
    e2 = kept_a_ref[n // 2 * quarter : n // 2 * quarter + 8, :]
    for slot in range(n // 2):
        big[slot].wait()
        gains(e2, kept_ref, slot * quarter, quarter, outs[n // 2 + slot], 0, rows)


def front_b(genotypes, kept_a, gain_a, herds, srcs, n):
    block, markers = genotypes.shape
    half = block // 2
    quarter = half // n
    total = len(srcs) * srcs[0].shape[0] // 3
    rows = quarter // LANES
    small = [*srcs, *herds, gain_a]
    return pl.pallas_call(
        functools.partial(front_b_kernel, n, len(srcs)),
        in_specs=[VMEM] + [ANY] * (1 + len(small)),
        out_specs=[VMEM] * (1 + n),
        out_shape=[pltpu.VMEM((n // 2 * quarter, markers), BF16)]
        + [jax.ShapeDtypeStruct((5 * rows, LANES), F32)] * n,
        scratch_shapes=[
            pltpu.VMEM((total, LANES), jnp.int32),
            pltpu.VMEM((total, LANES), F32),
            pltpu.VMEM((total, LANES), F32),
            pltpu.VMEM((total, LANES), F32),
            pltpu.VMEM((4, total, LANES), F32),
            pltpu.VMEM((5 * SUBS, 2 * LANES), F32),
            pltpu.VMEM((n, 3 * rows, LANES), F32),
        ]
        + [pltpu.VMEM(x.shape, F32) for x in small]
        + [pltpu.SemaphoreType.DMA((n // 2,)), pltpu.SemaphoreType.DMA((len(small),))],
        compiler_params=pltpu.CompilerParams(vmem_limit_bytes=LIMIT),
        cost_estimate=pl.CostEstimate(
            flops=4 * half * markers, bytes_accessed=half * markers, transcendentals=0
        ),
        name="front_b",
    )(
        pinned(kept_a),
        *[pltpu.with_memory_space_constraint(x, pltpu.HBM) for x in small],
        genotypes,
    )


def pinned(x):
    return pltpu.with_memory_space_constraint(x, pltpu.VMEM)


def combine_kernel(kept_a_ref, kept_b_ref, *refs):
    parts, out_ref = refs[:-1], refs[-1]
    rows = out_ref.shape[0] // 2
    total = parts[0][...]
    for part in parts[1:]:
        total = total + part[...]
    count = total[4 * rows :]
    for ch in range(2):
        gain = total[ch * rows : (ch + 1) * rows]
        out_ref[ch * rows : (ch + 1) * rows, :] = (
            total[(2 + ch) * rows : (3 + ch) * rows] - count * gain
        )


def combine(kept, parts):
    rows = parts[0].shape[0] // 5
    return pl.pallas_call(
        combine_kernel,
        in_specs=[VMEM] * (2 + len(parts)),
        out_specs=VMEM,
        out_shape=jax.ShapeDtypeStruct((2 * rows, LANES), F32),
        compiler_params=pltpu.CompilerParams(vmem_limit_bytes=LIMIT),
        cost_estimate=pl.CostEstimate(flops=1 << 16, bytes_accessed=1 << 16, transcendentals=0),
        name="combine",
    )(*map(pinned, kept), *parts)


def product(n, kept_refs, js, parts):
    quarter = kept_refs[1].shape[0] // (n // 2)
    rows = quarter // LANES
    total = jnp.zeros((8, kept_refs[1].shape[1]), F32)
    for j, part in zip(js, parts):
        cols = [
            jnp.concatenate(
                [part[i : i + 1, :], part[rows + i : rows + i + 1, :], jnp.zeros((6, LANES), F32)],
                axis=0,
            )
            for i in range(rows)
        ]
        lhs = jnp.concatenate(cols, axis=1).astype(BF16)
        late, slot = divmod(j, n // 2)
        total = total + jnp.dot(
            lhs,
            kept_refs[late][slot * quarter : (slot + 1) * quarter, :],
            preferred_element_type=F32,
        )
    return total


def back_kernel(n, js, kept_a_ref, kept_b_ref, *refs):
    parts, before, out_ref = refs[: len(js)], refs[len(js) : -1], refs[-1]
    total = product(n, (kept_a_ref, kept_b_ref), js, parts)
    out_ref[...] = total + before[0][...] if before else total


def back(kept, js, parts, n, *before):
    quarter, markers = kept[1].shape[0] // (n // 2), kept[1].shape[1]
    return pl.pallas_call(
        functools.partial(back_kernel, n, js),
        in_specs=[VMEM] * (2 + len(js) + len(before)),
        out_specs=VMEM,
        out_shape=jax.ShapeDtypeStruct((8, markers), F32),
        compiler_params=pltpu.CompilerParams(vmem_limit_bytes=LIMIT),
        cost_estimate=pl.CostEstimate(
            flops=4 * quarter * markers * len(js),
            bytes_accessed=2 * quarter * markers * len(js),
            transcendentals=0,
        ),
        name="back",
    )(*map(pinned, kept), *parts, *before)


def back_last_kernel(n, js, kept_a_ref, kept_b_ref, before_ref, *refs):
    parts, (own_ref, other_ref, theirs_ref) = refs[:n], refs[n:]
    rows = parts[0].shape[0] // 2
    for j in range(n):
        theirs_ref[j * rows : (j + 1) * rows, :] = parts[j][rows : 2 * rows, :]
    total = before_ref[...] + product(n, (kept_a_ref, kept_b_ref), js, [parts[j] for j in js])
    for i in range(own_ref.shape[0]):
        own_ref[i : i + 1, :] = total[0:1, i * LANES : (i + 1) * LANES]
        other_ref[i : i + 1, :] = total[1:2, i * LANES : (i + 1) * LANES]


def back_last(kept, js, parts, n, before):
    quarter, markers = kept[1].shape[0] // (n // 2), kept[1].shape[1]
    grad = jax.ShapeDtypeStruct((markers // LANES, LANES), F32)
    return pl.pallas_call(
        functools.partial(back_last_kernel, n, js),
        in_specs=[VMEM] * (3 + n),
        out_specs=[VMEM] * 3,
        out_shape=[grad, grad, jax.ShapeDtypeStruct((n * quarter // LANES, LANES), F32)],
        compiler_params=pltpu.CompilerParams(vmem_limit_bytes=LIMIT),
        cost_estimate=pl.CostEstimate(
            flops=4 * quarter * markers * len(js),
            bytes_accessed=2 * quarter * markers * len(js),
            transcendentals=0,
        ),
        name="back_last",
    )(*map(pinned, kept), before, *parts)


def assemble_kernel(n, theirs_ref, *refs):
    parts, out_ref = refs[:n], refs[n]
    rows = parts[0].shape[0] // 2
    chain, rec = lax.axis_index("chain"), lax.axis_index("rec")
    for j in range(n):
        owner = rec ^ j
        out_ref[chain * n + owner] = parts[j][0:rows, :]
        out_ref[(1 - chain) * n + owner] = theirs_ref[j * rows : (j + 1) * rows, :]


def assemble(theirs, parts, n):
    rows = parts[0].shape[0] // 2
    return pl.pallas_call(
        functools.partial(assemble_kernel, n),
        in_specs=[VMEM] * (1 + n),
        out_specs=VMEM,
        out_shape=jax.ShapeDtypeStruct((2 * n, rows, LANES), F32),
        cost_estimate=pl.CostEstimate(flops=1 << 16, bytes_accessed=1 << 18, transcendentals=0),
        name="assemble",
    )(theirs, *parts)


def on_device(
    n_rec,
    n_ani,
    genotypes,
    effects,
    gaussian_draw,
    prior_prec,
    accept,
    herd_effect,
    phenotype,
    record_animal,
    record_bin,
    live_records,
):
    step_size = 0.005
    n = n_rec

    effects_2d, herd_2d = tiled(effects), tiled(herd_effect)
    theirs = (swap(effects_2d, "chain", 2, 1), swap(herd_2d, "chain", 2, 1))
    raw = prepare(
        herd_effect.shape[0],
        live_records.reshape(1, 1),
        tiled(record_animal),
        tiled(phenotype),
        tiled(record_bin),
    )
    theirs, raw = lax.optimization_barrier((theirs, raw))
    srcs = [raw] + [swap(raw, "ani", n_ani, j) for j in range(1, n_ani)]

    kept_a, gain_a = front_a(genotypes, [effects_2d, theirs[0]], n)
    kept_b, *sums = front_b(genotypes, kept_a, gain_a, [herd_2d, theirs[1]], srcs, n)
    kept = (kept_a, kept_b)
    resid = combine(kept, [sums[0]] + [swap(sums[j], "rec", n, j) for j in range(1, n)])

    parts = [resid] + [swap(resid, "rec", n, j) for j in range(1, n)]
    grads = back(kept, [0], [resid], n)
    steps = [list(range(j, min(j + n // 4, n))) for j in range(1, n, n // 4)]
    for js in steps[:-1]:
        grads = back(kept, js, [parts[j] for j in js], n, grads)
    own, other, halves = back_last(kept, steps[-1], parts, n, grads)
    grad_part = own + swap(other, "chain", 2, 1)
    grad_part, swapped = lax.optimization_barrier((grad_part, swap(halves, "chain", 2, 1)))
    resid_sum = assemble(swapped, parts, n).reshape(-1)
    others = [swap(grad_part, "ani", n_ani, j) for j in range(1, n_ani)]

    likelihood_grad = grad_part
    for x in others:
        likelihood_grad = likelihood_grad + x
    likelihood_grad = likelihood_grad.reshape(-1)
    gradient = likelihood_grad - prior_prec * effects
    proposal = effects + step_size * gradient + math.sqrt(2.0 * step_size) * gaussian_draw
    accepted = jnp.repeat(accept, BLOCK) == 1
    return (jnp.where(accepted, proposal, effects), resid_sum)


def solution(mesh):
    return jax.shard_map(
        functools.partial(on_device, mesh.shape["rec"], mesh.shape["ani"]),
        mesh=mesh,
        in_specs=(
            P("ani", "rec"),
            P(("chain", "rec")),
            P(("chain", "rec")),
            P("rec"),
            P(("chain", "rec")),
            P(("chain", "rec")),
            P(("rec", "ani")),
            P(("rec", "ani")),
            P(("rec", "ani")),
            P(("rec", "ani")),
        ),
        out_specs=(P(("chain", "rec")), P(("chain", "ani"))),
        check_vma=False,
    )
```

time: 60.4 us -> 57.6 us (0.954)
  blocking collectives: 5.17 us -> 0 us
  Pallas kernels: 20.5 us -> 23.9 us
  local copies, waits for them, and re-layouts: 1.93 us -> 0.72 us
  starting transfers between devices: 17.2 us -> 17.9 us
    all_gather x1 -> x0, blocking collectives: 5.17 us -> none  [on_device(): likelihood_grad = jnp.sum(lax.all_gather(grad_part, 'ani'), axis=0)]
    pallas_call x5 -> x8, Pallas kernels: 18.9 us -> 22.4 us  [the longest x1 8.42 us: front_b(): pl.pallas_call(functools.partial(front_b_kernel, n, len(srcs)), in_specs=...]
    unnamed x26 -> x28, local copies, waits for them, and re-layouts: 1.93 us -> 0.72 us
    ppermute x12 -> x16, starting transfers between devices: 17.2 us -> 17.9 us  [swap(): return lax.ppermute(x, axis, [(i, i ^ j) for i in range(size)])]
    ppermute x12 -> x16, waiting for transfers between devices: 13 us -> 12.7 us  [swap(): return lax.ppermute(x, axis, [(i, i ^ j) for i in range(size)])]
  transfers between devices with their start and end apart: 12 -> 16, of which waited for: 6 -> 8; matrix products, arithmetic and copies ran while one was open for 1% -> 0% of each run, Pallas kernels for 2% -> 25%
where the time goes in v3:
time: 57.6 us; the launch traced here: 57.4 us
  Pallas kernels  23.9 us (41%)
  starting transfers between devices  17.9 us (31%)
  waiting for transfers between devices  12.7 us (22%)
  between operations  1.43 us (2%)
  local copies, waits for them, and re-layouts  0.72 us (1%)
  other arithmetic  0.67 us (1%)
    ppermute x16, starting transfers between devices, swap(): return lax.ppermute(x, axis, [(i, i ^ j) for i in range(size)])  17.9 us
    ppermute x16, waiting for transfers between devices, swap(): return lax.ppermute(x, axis, [(i, i ^ j) for i in range(size)])  12.7 us
    pallas_call x1, Pallas kernels, front_b(): pl.pallas_call(functools.partial(front_b_kernel, n, len(srcs)), in_specs=...  8.42 us
    pallas_call x1, Pallas kernels, front_a(): pl.pallas_call(functools.partial(front_a_kernel, n), in_specs=[ANY] * 3,...  7.63 us
    pallas_call x3, Pallas kernels, back(): pl.pallas_call(functools.partial(back_kernel, n, js), in_specs=[VMEM] * (...  3.56 us
    pallas_call x1, Pallas kernels, assemble(): pl.pallas_call(functools.partial(assemble_kernel, n), in_specs=[VMEM] * (...  1.55 us
    pallas_call x1, Pallas kernels, prepare(): pl.pallas_call(functools.partial(prepare_kernel, bins), in_specs=[VMEM] *...  1.51 us
    pallas_call x1, Pallas kernels, back_last(): pl.pallas_call(functools.partial(back_last_kernel, n, js), in_specs=[VMEM...  1.22 us
  transfers between devices with their start and end apart: 16, of which 8 were waited for; matrix products, arithmetic and copies ran while one was open for 0% of the time, Pallas kernels for 25%

profile of v3, /device:TPU:0, one launch (start us, length us, event | category | flops | bytes accessed | tf_op | source)
XLA Modules:
  0.0 57.4 jit_solution(2014310525798840935)
XLA Ops:
  0.6 3.0 %collective-permute-start.1 = (f32[16,128]{1,0:T(8,128)}, f32[16,128]{1,0:T(8,128)S(1)}, u32[]{:S(2)}, u32[]{:S(2)}) collective-permute-start(f32[16,128]{1,0:T(8,128)} %bitcast.26), channel_id=1, source_target_pairs={{0,1},{1,0},{2,3},{3,2},{4,5},{5,4},{6,7},{7,6},{8,9},{9,8},{10,11... | collective-permute-start | bytes 24584 | tf_op jit(solution)/shard_map/ppermute | solution.py:27
  3.7 0.1 collective-permute-start
  4.4 1.5 %prepare.1.refs_0_ = f32[192,128]{1,0:T(8,128)} custom-call(s32[1,1]{1,0:T(1,128)} %bitcast.19.live_ref, s32[64,128]{1,0:T(8,128)} %bitcast.21, f32[64,128]{1,0:T(8,128)} %bitcast.22, s32[64,128]{1,0:T(8,128)} %bitcast.23), custom_call_target="tpu_custom_call" | custom-call | tf_op jit(solution)/shard_map/prepare/pallas_call | solution.py:48
  5.9 1.6 %collective-permute-done.other_any = f32[8,128]{1,0:T(8,128)S(1)} collective-permute-done((f32[8,128]{1,0:T(8,128)}, f32[8,128]{1,0:T(8,128)S(1)}, u32[]{:S(2)}, u32[]{:S(2)}) %collective-permute-start) | collective-permute-done | bytes 4128 | tf_op jit(solution)/shard_map/ppermute | solution.py:27
  7.6 1.6 %collective-permute-start.3 = (f32[192,128]{1,0:T(8,128)}, f32[192,128]{1,0:T(8,128)S(1)}, u32[]{:S(2)}, u32[]{:S(2)}) collective-permute-start(f32[192,128]{1,0:T(8,128)} %prepare.1.refs_0_), channel_id=1, source_target_pairs={{0,4},{2,6},{4,0},{6,2},{1,5},{3,7},{5,1},{7,3},{8,12},{10,14},{12... | collective-permute-start | bytes 294920 | tf_op jit(solution)/shard_map/ppermute | solution.py:27
  9.1 0.3 collective-permute-start.4
  9.4 7.6 %front_a.1 = (bf16[8208,1024]{1,0:T(8,128)(2,1)S(1)}, f32[2,64,128]{2,1,0:T(8,128)}) custom-call(f32[8,128]{1,0:T(8,128)} %bitcast.25, f32[8,128]{1,0:T(8,128)} %copy-done.10, bf16[32768,1024]{1,0:T(8,128)(2,1)} %refs_7_.1), custom_call_target="tpu_custom_call" | custom-call | flops 33554432 | bytes 16777216 | tf_op jit(solution)/shard_map/front_a/pallas_call | solution.py:204
  17.1 0.6 %copy-done.4 = f32[192,128]{1,0:T(8,128)} copy-done((f32[192,128]{1,0:T(8,128)}, f32[192,128]{1,0:T(8,128)S(1)}, u32[]{:S(2)}) %copy-start.4) | copy-done | bytes 98328
  17.8 8.4 %front_b.1 = (bf16[8192,1024]{1,0:T(8,128)(2,1)S(1)}, f32[160,128]{1,0:T(8,128)S(1)}, f32[160,128]{1,0:T(8,128)S(1)}, f32[160,128]{1,0:T(8,128)S(1)}, f32[160,128]{1,0:T(8,128)S(1)}) custom-call(bf16[8208,1024]{1,0:T(8,128)(2,1)S(1)} %get-tuple-element.18.kept_a_ref, f32[192,128]{1,0:T(8,128)} %prepare.1.refs_0_, f32[192,128]{1,0:T(8,128)} %copy-done.4, ...), custom_call_target="tpu_custom_call" | custom-call | flops 67108864 | bytes 16777216 | tf_op jit(solution)/shard_map/front_b/pallas_call | solution.py:290
  26.2 1.6 %collective-permute-start.5 = (f32[160,128]{1,0:T(8,128)S(1)}, f32[160,128]{1,0:T(8,128)S(1)}, u32[]{:S(2)}, u32[]{:S(2)}) collective-permute-start(f32[160,128]{1,0:T(8,128)S(1)} %get-tuple-element.24), channel_id=1, source_target_pairs={{0,8},{8,0},{16,24},{24,16},{1,9},{9,1},{17,25},{25,17},{2,10},{10... | collective-permute-start | bytes 245768 | tf_op jit(solution)/shard_map/ppermute | solution.py:27
  27.9 2.6 %collective-permute-start.6 = (f32[160,128]{1,0:T(8,128)S(1)}, f32[160,128]{1,0:T(8,128)S(1)}, u32[]{:S(2)}, u32[]{:S(2)}) collective-permute-start(f32[160,128]{1,0:T(8,128)S(1)} %get-tuple-element.25), channel_id=1, source_target_pairs={{0,16},{8,24},{16,0},{24,8},{1,17},{9,25},{17,1},{25,9},{2,18},{10... | collective-permute-start | bytes 245768 | tf_op jit(solution)/shard_map/ppermute | solution.py:27
  30.5 0.2 collective-permute-start.7
  30.7 0.3 collective-permute-done.5.refs_1_
  31.0 6.4 %collective-permute-done.6.refs_2_ = f32[160,128]{1,0:T(8,128)S(1)} collective-permute-done((f32[160,128]{1,0:T(8,128)S(1)}, f32[160,128]{1,0:T(8,128)S(1)}, u32[]{:S(2)}, u32[]{:S(2)}) %collective-permute-start.6) | collective-permute-done | bytes 81952 | tf_op jit(solution)/shard_map/ppermute | solution.py:27
  37.4 1.8 %collective-permute-start.9 = (f32[64,128]{1,0:T(8,128)S(1)}, f32[64,128]{1,0:T(8,128)S(1)}, u32[]{:S(2)}, u32[]{:S(2)}) collective-permute-start(f32[64,128]{1,0:T(8,128)S(1)} %combine.1.refs_0_), channel_id=1, source_target_pairs={{0,8},{8,0},{16,24},{24,16},{1,9},{9,1},{17,25},{25,17},{2,10},{10... | collective-permute-start | bytes 98312 | tf_op jit(solution)/shard_map/ppermute | solution.py:27
  39.1 1.6 %collective-permute-start.8 = (f32[64,128]{1,0:T(8,128)S(1)}, f32[64,128]{1,0:T(8,128)S(1)}, u32[]{:S(2)}, u32[]{:S(2)}) collective-permute-start(f32[64,128]{1,0:T(8,128)S(1)} %combine.1.refs_0_), channel_id=1, source_target_pairs={{0,16},{8,24},{16,0},{24,8},{1,17},{9,25},{17,1},{25,9},{2,18},{10... | collective-permute-start | bytes 98312 | tf_op jit(solution)/shard_map/ppermute | solution.py:27
  40.7 1.1 %collective-permute-start.10 = (f32[64,128]{1,0:T(8,128)S(1)}, f32[64,128]{1,0:T(8,128)S(1)}, u32[]{:S(2)}, u32[]{:S(2)}) collective-permute-start(f32[64,128]{1,0:T(8,128)S(1)} %combine.1.refs_0_), channel_id=1, source_target_pairs={{0,24},{8,16},{16,8},{24,0},{1,25},{9,17},{17,9},{25,1},{2,26},{10... | collective-permute-start | bytes 98312 | tf_op jit(solution)/shard_map/ppermute | solution.py:27
  41.8 1.2 %back.3.refs_1_ = f32[8,1024]{1,0:T(8,128)S(1)} custom-call(bf16[8208,1024]{1,0:T(8,128)(2,1)S(1)} %get-tuple-element.18.kept_a_ref, bf16[8192,1024]{1,0:T(8,128)(2,1)S(1)} %get-tuple-element.22.kept_b_ref, f32[64,128]{1,0:T(8,128)S(1)} %combine.1.refs_0_), custom_call_target="tpu_custom_call" | custom-call | flops 16777216 | bytes 8388608 | tf_op jit(solution)/shard_map/back/pallas_call | solution.py:380
  43.0 1.2 %back.4.refs_1_ = f32[8,1024]{1,0:T(8,128)S(1)} custom-call(bf16[8208,1024]{1,0:T(8,128)(2,1)S(1)} %get-tuple-element.18.kept_a_ref, bf16[8192,1024]{1,0:T(8,128)(2,1)S(1)} %get-tuple-element.22.kept_b_ref, f32[64,128]{1,0:T(8,128)S(1)} %collective-permute-done.9.refs_0_.refs_1_, f32[8,1024]{1,0:T(8,128)S(1)} %back.3.refs_1_), custom_call_target="tpu_custom_call" | custom-call | flops 16777216 | bytes 8388608 | tf_op jit(solution)/shard_map/back/pallas_call | solution.py:380
  44.2 0.2 collective-permute-done.8.refs_0_.refs_2_
  44.5 1.2 %back.5.before_ref = f32[8,1024]{1,0:T(8,128)S(1)} custom-call(bf16[8208,1024]{1,0:T(8,128)(2,1)S(1)} %get-tuple-element.18.kept_a_ref, bf16[8192,1024]{1,0:T(8,128)(2,1)S(1)} %get-tuple-element.22.kept_b_ref, f32[64,128]{1,0:T(8,128)S(1)} %collective-permute-done.8.refs_0_.refs_2_, f32[8,1024]{1,0:T(8,128)S(1)} %back.4.refs_1_), custom_call_target="tpu_custom_call" | custom-call | flops 16777216 | bytes 8388608 | tf_op jit(solution)/shard_map/back/pallas_call | solution.py:380
  45.7 0.7 %collective-permute-done.10.refs_3_ = f32[64,128]{1,0:T(8,128)S(1)} collective-permute-done((f32[64,128]{1,0:T(8,128)S(1)}, f32[64,128]{1,0:T(8,128)S(1)}, u32[]{:S(2)}, u32[]{:S(2)}) %collective-permute-start.10) | collective-permute-done | bytes 32800 | tf_op jit(solution)/shard_map/ppermute | solution.py:27
  46.4 1.2 %back_last.1 = (f32[8,128]{1,0:T(8,128)S(1)}, f32[8,128]{1,0:T(8,128)S(1)}, f32[128,128]{1,0:T(8,128)S(1)}) custom-call(bf16[8208,1024]{1,0:T(8,128)(2,1)S(1)} %get-tuple-element.18.kept_a_ref, bf16[8192,1024]{1,0:T(8,128)(2,1)S(1)} %get-tuple-element.22.kept_b_ref, f32[8,1024]{1,0:T(8,128)S(1)} %back.5.before_ref, f32[64,128]{1,0:T(8,128)S(1)} %combine.1.refs_0_, ...), custom_call_target="tpu_custom_call" | custom-call | flops 16777216 | bytes 8388608 | tf_op jit(solution)/shard_map/back_last/pallas_call | solution.py:409
  47.7 0.5 collective-permute-start.12
  48.2 1.5 %collective-permute-start.11 = (f32[8,128]{1,0:T(8,128)S(1)}, f32[8,128]{1,0:T(8,128)S(1)}, u32[]{:S(2)}, u32[]{:S(2)}) collective-permute-start(f32[8,128]{1,0:T(8,128)S(1)} %get-tuple-element.28), channel_id=1, source_target_pairs={{0,1},{1,0},{2,3},{3,2},{4,5},{5,4},{6,7},{7,6},{8,9},{9,8},{10,11... | collective-permute-start | bytes 12296 | tf_op jit(solution)/shard_map/ppermute | solution.py:27
  49.7 2.3 %collective-permute-done.11 = f32[8,128]{1,0:T(8,128)S(1)} collective-permute-done((f32[8,128]{1,0:T(8,128)S(1)}, f32[8,128]{1,0:T(8,128)S(1)}, u32[]{:S(2)}, u32[]{:S(2)}) %collective-permute-start.11) | collective-permute-done | bytes 4128 | tf_op jit(solution)/shard_map/ppermute | solution.py:27
  52.1 1.6 %collective-permute-start.14 = (f32[8,128]{1,0:T(8,128)S(1)}, f32[8,128]{1,0:T(8,128)S(1)}, u32[]{:S(2)}, u32[]{:S(2)}) collective-permute-start(f32[8,128]{1,0:T(8,128)S(1)} %add.18), channel_id=1, source_target_pairs={{0,4},{2,6},{4,0},{6,2},{1,5},{3,7},{5,1},{7,3},{8,12},{10,14},{12... | collective-permute-start | bytes 12296 | tf_op jit(solution)/shard_map/ppermute | solution.py:27
  53.7 0.3 collective-permute-start.15
  54.0 1.6 %assemble.1 = f32[8,32,128]{2,1,0:T(8,128)} custom-call(f32[128,128]{1,0:T(8,128)} %copy-done.7, f32[64,128]{1,0:T(8,128)} %copy-done, f32[64,128]{1,0:T(8,128)} %copy-done.1, f32[64,128]{1,0:T(8,128)} %copy-done.2, f32[64,128]{1,0:T(8,128)} %copy-done.3), custom_call_target="tpu_custom_call" | custom-call | flops 65536 | bytes 262144 | tf_op jit(solution)/shard_map/assemble/pallas_call | solution.py:436
  55.5 0.2 collective-permute-done.14
  55.8 0.9 %collective-permute-done.15 = f32[8,128]{1,0:T(8,128)S(1)} collective-permute-done((f32[8,128]{1,0:T(8,128)S(1)}, f32[8,128]{1,0:T(8,128)S(1)}, u32[]{:S(2)}, u32[]{:S(2)}) %collective-permute-start.15) | collective-permute-done | bytes 4128 | tf_op jit(solution)/shard_map/ppermute | solution.py:27
  56.7 0.7 %fusion.3 = f32[1024]{0:T(1024)} fusion(f32[1024]{0:T(1024)S(1)} %copy-done.8, f32[1024]{0:T(1024)S(1)} %copy-done.11, f32[1024]{0:T(1024)S(1)} %copy-done.12, f32[8,128]{1,0:T(8,128)S(1)} %collective-permute-done.15, f32[8,128]{1,0:T(8,128)S(1)} %collective-permute-done.14, f32[8,128]{1,0:T(8,128)S(1)} %add.18, f32[8,128]{1,0:T(8,128)S(1)} %collective-permute-done.13, ...), kind=kLoop, calls=%fused_computation.4 | loop fusion | flops 10240 | bytes 32776 | tf_op jit(solution)/shard_map/jit(_where)/select_n | solution.py:498
  (40 shorter events, 0.3 us)
Async XLA Ops:
  0.6 6.9 %collective-permute-start.1 = (f32[16,128]{1,0:T(8,128)}, f32[16,128]{1,0:T(8,128)S(1)}, u32[]{:S(2)}, u32[]{:S(2)}) collective-permute-start(f32[16,128]{1,0:T(8,128)} %bitcast.26), channel_id=1, source_target_pairs={{0,1},{1,0},{2,3},{3,2},{4,5},{5,4},{6,7},{7,6},{8,9},{9,8},{10,11... | collective-permute-start | bytes 24584 | tf_op jit(solution)/shard_map/ppermute | solution.py:27
  3.7 3.8 %collective-permute-start = (f32[8,128]{1,0:T(8,128)}, f32[8,128]{1,0:T(8,128)S(1)}, u32[]{:S(2)}, u32[]{:S(2)}) collective-permute-start(f32[8,128]{1,0:T(8,128)} %bitcast.24), channel_id=1, source_target_pairs={{0,1},{1,0},{2,3},{3,2},{4,5},{5,4},{6,7},{7,6},{8,9},{9,8},{10,11... | collective-permute-start | bytes 12296 | tf_op jit(solution)/shard_map/ppermute | solution.py:27
  7.5 1.9 %copy-start.10 = (f32[8,128]{1,0:T(8,128)}, f32[8,128]{1,0:T(8,128)S(1)}, u32[]{:S(2)}) copy-start(f32[8,128]{1,0:T(8,128)S(1)} %collective-permute-done.other_any) | copy-start | bytes 12292
  7.5 9.6 %copy-start.9 = (f32[16,128]{1,0:T(8,128)}, f32[16,128]{1,0:T(8,128)S(1)}, u32[]{:S(2)}) copy-start(f32[16,128]{1,0:T(8,128)S(1)} %collective-permute-done.1.refs_5_) | copy-start | bytes 24580
  7.5 9.6 %collective-permute-start.2 = (f32[192,128]{1,0:T(8,128)}, f32[192,128]{1,0:T(8,128)S(1)}, u32[]{:S(2)}, u32[]{:S(2)}) collective-permute-start(f32[192,128]{1,0:T(8,128)} %prepare.1.refs_0_), channel_id=1, source_target_pairs={{0,2},{2,0},{4,6},{6,4},{1,3},{3,1},{5,7},{7,5},{8,10},{10,8},{12,... | collective-permute-start | bytes 294920 | tf_op jit(solution)/shard_map/ppermute | solution.py:27
  7.6 9.5 %collective-permute-start.3 = (f32[192,128]{1,0:T(8,128)}, f32[192,128]{1,0:T(8,128)S(1)}, u32[]{:S(2)}, u32[]{:S(2)}) collective-permute-start(f32[192,128]{1,0:T(8,128)} %prepare.1.refs_0_), channel_id=1, source_target_pairs={{0,4},{2,6},{4,0},{6,2},{1,5},{3,7},{5,1},{7,3},{8,12},{10,14},{12... | collective-permute-start | bytes 294920 | tf_op jit(solution)/shard_map/ppermute | solution.py:27
  9.1 8.0 %collective-permute-start.4 = (f32[192,128]{1,0:T(8,128)}, f32[192,128]{1,0:T(8,128)S(1)}, u32[]{:S(2)}, u32[]{:S(2)}) collective-permute-start(f32[192,128]{1,0:T(8,128)} %prepare.1.refs_0_), channel_id=1, source_target_pairs={{0,6},{2,4},{4,2},{6,0},{1,7},{3,5},{5,3},{7,1},{8,14},{10,12},{12... | collective-permute-start | bytes 294920 | tf_op jit(solution)/shard_map/ppermute | solution.py:27
  17.1 0.6 %copy-start.4 = (f32[192,128]{1,0:T(8,128)}, f32[192,128]{1,0:T(8,128)S(1)}, u32[]{:S(2)}) copy-start(f32[192,128]{1,0:T(8,128)S(1)} %collective-permute-done.2.refs_1_) | copy-start | bytes 294916
  17.1 0.7 %copy-start.5 = (f32[192,128]{1,0:T(8,128)}, f32[192,128]{1,0:T(8,128)S(1)}, u32[]{:S(2)}) copy-start(f32[192,128]{1,0:T(8,128)S(1)} %collective-permute-done.3.refs_2_) | copy-start | bytes 294916
  17.1 0.7 %copy-start.6 = (f32[192,128]{1,0:T(8,128)}, f32[192,128]{1,0:T(8,128)S(1)}, u32[]{:S(2)}) copy-start(f32[192,128]{1,0:T(8,128)S(1)} %collective-permute-done.4.refs_3_) | copy-start | bytes 294916
  26.2 4.8 %collective-permute-start.5 = (f32[160,128]{1,0:T(8,128)S(1)}, f32[160,128]{1,0:T(8,128)S(1)}, u32[]{:S(2)}, u32[]{:S(2)}) collective-permute-start(f32[160,128]{1,0:T(8,128)S(1)} %get-tuple-element.24), channel_id=1, source_target_pairs={{0,8},{8,0},{16,24},{24,16},{1,9},{9,1},{17,25},{25,17},{2,10},{10... | collective-permute-start | bytes 245768 | tf_op jit(solution)/shard_map/ppermute | solution.py:27
  27.9 9.5 %collective-permute-start.6 = (f32[160,128]{1,0:T(8,128)S(1)}, f32[160,128]{1,0:T(8,128)S(1)}, u32[]{:S(2)}, u32[]{:S(2)}) collective-permute-start(f32[160,128]{1,0:T(8,128)S(1)} %get-tuple-element.25), channel_id=1, source_target_pairs={{0,16},{8,24},{16,0},{24,8},{1,17},{9,25},{17,1},{25,9},{2,18},{10... | collective-permute-start | bytes 245768 | tf_op jit(solution)/shard_map/ppermute | solution.py:27
  30.5 6.9 %collective-permute-start.7 = (f32[160,128]{1,0:T(8,128)S(1)}, f32[160,128]{1,0:T(8,128)S(1)}, u32[]{:S(2)}, u32[]{:S(2)}) collective-permute-start(f32[160,128]{1,0:T(8,128)S(1)} %get-tuple-element.26), channel_id=1, source_target_pairs={{0,24},{8,16},{16,8},{24,0},{1,25},{9,17},{17,9},{25,1},{2,26},{10... | collective-permute-start | bytes 245768 | tf_op jit(solution)/shard_map/ppermute | solution.py:27
  37.4 9.1 %copy-start = (f32[64,128]{1,0:T(8,128)}, f32[64,128]{1,0:T(8,128)S(1)}, u32[]{:S(2)}) copy-start(f32[64,128]{1,0:T(8,128)S(1)} %combine.1.refs_0_) | copy-start | bytes 98308
  37.4 5.6 %collective-permute-start.9 = (f32[64,128]{1,0:T(8,128)S(1)}, f32[64,128]{1,0:T(8,128)S(1)}, u32[]{:S(2)}, u32[]{:S(2)}) collective-permute-start(f32[64,128]{1,0:T(8,128)S(1)} %combine.1.refs_0_), channel_id=1, source_target_pairs={{0,8},{8,0},{16,24},{24,16},{1,9},{9,1},{17,25},{25,17},{2,10},{10... | collective-permute-start | bytes 98312 | tf_op jit(solution)/shard_map/ppermute | solution.py:27
  39.1 5.3 %collective-permute-start.8 = (f32[64,128]{1,0:T(8,128)S(1)}, f32[64,128]{1,0:T(8,128)S(1)}, u32[]{:S(2)}, u32[]{:S(2)}) collective-permute-start(f32[64,128]{1,0:T(8,128)S(1)} %combine.1.refs_0_), channel_id=1, source_target_pairs={{0,16},{8,24},{16,0},{24,8},{1,17},{9,25},{17,1},{25,9},{2,18},{10... | collective-permute-start | bytes 98312 | tf_op jit(solution)/shard_map/ppermute | solution.py:27
  40.7 5.7 %collective-permute-start.10 = (f32[64,128]{1,0:T(8,128)S(1)}, f32[64,128]{1,0:T(8,128)S(1)}, u32[]{:S(2)}, u32[]{:S(2)}) collective-permute-start(f32[64,128]{1,0:T(8,128)S(1)} %combine.1.refs_0_), channel_id=1, source_target_pairs={{0,24},{8,16},{16,8},{24,0},{1,25},{9,17},{17,9},{25,1},{2,26},{10... | collective-permute-start | bytes 98312 | tf_op jit(solution)/shard_map/ppermute | solution.py:27
  43.0 3.4 %copy-start.1 = (f32[64,128]{1,0:T(8,128)}, f32[64,128]{1,0:T(8,128)S(1)}, u32[]{:S(2)}) copy-start(f32[64,128]{1,0:T(8,128)S(1)} %collective-permute-done.9.refs_0_.refs_1_) | copy-start | bytes 98308
  44.5 2.0 %copy-start.2 = (f32[64,128]{1,0:T(8,128)}, f32[64,128]{1,0:T(8,128)S(1)}, u32[]{:S(2)}) copy-start(f32[64,128]{1,0:T(8,128)S(1)} %collective-permute-done.8.refs_0_.refs_2_) | copy-start | bytes 98308
  45.7 8.3 %copy-start.13 = (s32[8]{0:T(128)S(1)}, s32[8]{0:T(128)}, u32[]{:S(2)}) copy-start(s32[8]{0:T(128)} %param.14) | copy-start | bytes 100
  45.7 11.0 %copy-start.8 = (f32[1024]{0:T(1024)S(1)}, f32[1024]{0:T(1024)}, u32[]{:S(2)}) copy-start(f32[1024]{0:T(1024)} %param.11) | copy-start | bytes 12292
  45.7 11.0 %copy-start.11 = (f32[1024]{0:T(1024)S(1)}, f32[1024]{0:T(1024)}, u32[]{:S(2)}) copy-start(f32[1024]{0:T(1024)} %param.12) | copy-start | bytes 12292
  45.7 11.0 %copy-start.12 = (f32[1024]{0:T(1024)S(1)}, f32[1024]{0:T(1024)}, u32[]{:S(2)}) copy-start(f32[1024]{0:T(1024)} %param.13) | copy-start | bytes 12292
  46.4 1.2 %copy-start.3 = (f32[64,128]{1,0:T(8,128)}, f32[64,128]{1,0:T(8,128)S(1)}, u32[]{:S(2)}) copy-start(f32[64,128]{1,0:T(8,128)S(1)} %collective-permute-done.10.refs_3_) | copy-start | bytes 98308
  47.7 4.4 %collective-permute-start.12 = (f32[128,128]{1,0:T(8,128)S(1)}, f32[128,128]{1,0:T(8,128)S(1)}, u32[]{:S(2)}, u32[]{:S(2)}) collective-permute-start(f32[128,128]{1,0:T(8,128)S(1)} %get-tuple-element.29), channel_id=1, source_target_pairs={{0,1},{1,0},{2,3},{3,2},{4,5},{5,4},{6,7},{7,6},{8,9},{9,8},{10,11... | collective-permute-start | bytes 196616 | tf_op jit(solution)/shard_map/ppermute | solution.py:27
  48.2 3.8 %collective-permute-start.11 = (f32[8,128]{1,0:T(8,128)S(1)}, f32[8,128]{1,0:T(8,128)S(1)}, u32[]{:S(2)}, u32[]{:S(2)}) collective-permute-start(f32[8,128]{1,0:T(8,128)S(1)} %get-tuple-element.28), channel_id=1, source_target_pairs={{0,1},{1,0},{2,3},{3,2},{4,5},{5,4},{6,7},{7,6},{8,9},{9,8},{10,11... | collective-permute-start | bytes 12296 | tf_op jit(solution)/shard_map/ppermute | solution.py:27
  52.0 2.0 %copy-start.7 = (f32[128,128]{1,0:T(8,128)}, f32[128,128]{1,0:T(8,128)S(1)}, u32[]{:S(2)}) copy-start(f32[128,128]{1,0:T(8,128)S(1)} %collective-permute-done.12.theirs_ref) | copy-start | bytes 196612
  52.0 3.5 %collective-permute-start.13 = (f32[8,128]{1,0:T(8,128)S(1)}, f32[8,128]{1,0:T(8,128)S(1)}, u32[]{:S(2)}, u32[]{:S(2)}) collective-permute-start(f32[8,128]{1,0:T(8,128)S(1)} %add.18), channel_id=1, source_target_pairs={{0,2},{2,0},{4,6},{6,4},{1,3},{3,1},{5,7},{7,5},{8,10},{10,8},{12,... | collective-permute-start | bytes 12296 | tf_op jit(solution)/shard_map/ppermute | solution.py:27
  52.1 3.7 %collective-permute-start.14 = (f32[8,128]{1,0:T(8,128)S(1)}, f32[8,128]{1,0:T(8,128)S(1)}, u32[]{:S(2)}, u32[]{:S(2)}) collective-permute-start(f32[8,128]{1,0:T(8,128)S(1)} %add.18), channel_id=1, source_target_pairs={{0,4},{2,6},{4,0},{6,2},{1,5},{3,7},{5,1},{7,3},{8,12},{10,14},{12... | collective-permute-start | bytes 12296 | tf_op jit(solution)/shard_map/ppermute | solution.py:27
  53.7 3.0 %collective-permute-start.15 = (f32[8,128]{1,0:T(8,128)S(1)}, f32[8,128]{1,0:T(8,128)S(1)}, u32[]{:S(2)}, u32[]{:S(2)}) collective-permute-start(f32[8,128]{1,0:T(8,128)S(1)} %add.18), channel_id=1, source_target_pairs={{0,6},{2,4},{4,2},{6,0},{1,7},{3,5},{5,3},{7,1},{8,14},{10,12},{12... | collective-permute-start | bytes 12296 | tf_op jit(solution)/shard_map/ppermute | solution.py:27

commit v4 on v3

--- a/solution.py
+++ b/solution.py
@@ -25,6 +25,10 @@
 
 def swap(x, axis, size, j):
     return lax.ppermute(x, axis, [(i, i ^ j) for i in range(size)])
+
+
+def shift(x, axis, size, j):
+    return lax.ppermute(x, axis, [(i, (i + j) % size) for i in range(size)])
 
 
 def tiled(x):
@@ -160,7 +164,8 @@
     rows = quarter // LANES
 
     def load(b):
-        at = chain * quarter * n + (rec ^ (b // per)) * quarter + lax.rem(b, per) * tile
+        owner = rec ^ (2 * (b // per) + 1)
+        at = chain * quarter * n + owner * quarter + lax.rem(b, per) * tile
         return pltpu.make_async_copy(
             g_hbm.at[pl.ds(pl.multiple_of(at, tile), tile), :],
             kept_ref.at[pl.ds(pl.multiple_of(b * tile, tile), tile), :],
@@ -183,7 +188,7 @@
     ).astype(BF16)
     kept_ref[(n // 2) * quarter :, :] = e2
 
-    @pl.loop(0, n // 2 * per)
+    @pl.loop(0, n // 4 * per)
     def _(b):
         load(b).wait()
         at = pl.multiple_of(b * tile, tile)
@@ -191,6 +196,11 @@
 
     done = pltpu.make_async_copy(gain, gains_any, out_sem)
     done.start()
+
+    @pl.loop(n // 4 * per, n // 2 * per)
+    def _(b):
+        load(b).wait()
+
     done.wait()
 
 
@@ -200,7 +210,7 @@
     quarter = half // n
     rows = quarter // LANES
     tiles = n // 2 * (quarter // min(TILE, quarter))
-    shape = (n // 2, 2 * rows, LANES)
+    shape = (n // 4, 2 * rows, LANES)
     return pl.pallas_call(
         functools.partial(front_a_kernel, n),
         in_specs=[ANY] * 3,
@@ -223,9 +233,9 @@
 
 
 def front_b_kernel(n, n_src, kept_a_ref, *refs):
-    small_any, g_hbm, kept_ref = refs[: n_src + 3], refs[n_src + 3], refs[n_src + 4]
-    outs = refs[n_src + 5 : n_src + 5 + n]
-    key_s, y_s, lane_s, sub_s, v_s, acc, tab, *small_s, sem, small_sem = refs[n_src + 5 + n :]
+    small_any, g_hbm = refs[: n_src + 3], refs[n_src + 3]
+    kept_ref, odd, rest = refs[n_src + 4 : n_src + 7]
+    key_s, y_s, lane_s, sub_s, v_s, acc, tab, *small_s, sem, small_sem = refs[n_src + 7 :]
     quarter = kept_ref.shape[0] // (n // 2)
     half = quarter * n
     rows = quarter // LANES
@@ -239,7 +249,7 @@
         copy.start()
     big = []
     for slot in range(n // 2):
-        at = pl.multiple_of(chain * half + (rec ^ (n // 2 + slot)) * quarter, quarter)
+        at = pl.multiple_of(chain * half + (rec ^ (2 * slot)) * quarter, quarter)
         big.append(
             pltpu.make_async_copy(
                 g_hbm.at[pl.ds(at, quarter), :],
@@ -270,14 +280,16 @@
         tab[q, 0:rows, :] = window(0) + window(1)
         tab[q, rows : 2 * rows, :] = window(2) + window(3)
         tab[q, 2 * rows : 3 * rows, :] = window(4)
-    for j in range(n):
-        outs[j][2 * rows : 5 * rows, :] = tab[rec ^ j]
-    for j in range(n // 2):
-        outs[j][0 : 2 * rows, :] = gain_a[j]
+    for i in range(n // 2):
+        rest[i] = tab[rec ^ (2 * i)]
+        odd[i, 2 * rows : 5 * rows, :] = tab[rec ^ (2 * i + 1)]
+    for i in range(n // 4):
+        odd[i, 0 : 2 * rows, :] = gain_a[i]
     e2 = kept_a_ref[n // 2 * quarter : n // 2 * quarter + 8, :]
-    for slot in range(n // 2):
-        big[slot].wait()
-        gains(e2, kept_ref, slot * quarter, quarter, outs[n // 2 + slot], 0, rows)
+    for i in range(n // 4, n // 2):
+        gains(e2, kept_a_ref, i * quarter, quarter, odd.at[i], 0, rows)
+    for copy in big:
+        copy.wait()
 
 
 def front_b(genotypes, kept_a, gain_a, herds, srcs, n):
@@ -290,9 +302,12 @@
     return pl.pallas_call(
         functools.partial(front_b_kernel, n, len(srcs)),
         in_specs=[VMEM] + [ANY] * (1 + len(small)),
-        out_specs=[VMEM] * (1 + n),
-        out_shape=[pltpu.VMEM((n // 2 * quarter, markers), BF16)]
-        + [jax.ShapeDtypeStruct((5 * rows, LANES), F32)] * n,
+        out_specs=[VMEM] * 3,
+        out_shape=[
+            pltpu.VMEM((n // 2 * quarter, markers), BF16),
+            jax.ShapeDtypeStruct((n // 2, 5 * rows, LANES), F32),
+            jax.ShapeDtypeStruct((n // 2, 3 * rows, LANES), F32),
+        ],
         scratch_shapes=[
             pltpu.VMEM((total, LANES), jnp.int32),
             pltpu.VMEM((total, LANES), F32),
@@ -320,11 +335,54 @@
     return pltpu.with_memory_space_constraint(x, pltpu.VMEM)
 
 
-def combine_kernel(kept_a_ref, kept_b_ref, *refs):
+def front_c_kernel(n, kept_a_ref, kept_b_ref, rest_ref, *outs):
+    quarter = kept_b_ref.shape[0] // (n // 2)
+    rows = quarter // LANES
+    e2 = kept_a_ref[n // 2 * quarter : n // 2 * quarter + 8, :]
+    for i in range(n // 2):
+        outs[i][2 * rows : 5 * rows, :] = rest_ref[i]
+        gains(e2, kept_b_ref, i * quarter, quarter, outs[i], 0, rows)
+
+
+def front_c(kept, rest, n):
+    quarter, markers = kept[1].shape[0] // (n // 2), kept[1].shape[1]
+    piece = jax.ShapeDtypeStruct((5 * quarter // LANES, LANES), F32)
+    return pl.pallas_call(
+        functools.partial(front_c_kernel, n),
+        in_specs=[VMEM] * 3,
+        out_specs=[VMEM] * (n // 2),
+        out_shape=[piece] * (n // 2),
+        compiler_params=pltpu.CompilerParams(vmem_limit_bytes=LIMIT),
+        cost_estimate=pl.CostEstimate(
+            flops=2 * n * quarter * markers, bytes_accessed=n * quarter * markers, transcendentals=0
+        ),
+        name="front_c",
+    )(*map(pinned, kept), rest)
+
+
+def merge_kernel(kept_a_ref, kept_b_ref, came_ref, *refs):
+    count = len(refs) // 2
+    for i in range(count):
+        refs[count + i][...] = refs[i][...] + came_ref[i + 1]
+
+
+def merge(kept, came, pieces):
+    return pl.pallas_call(
+        merge_kernel,
+        in_specs=[VMEM] * (3 + len(pieces)),
+        out_specs=[VMEM] * len(pieces),
+        out_shape=[jax.ShapeDtypeStruct(x.shape, F32) for x in pieces],
+        compiler_params=pltpu.CompilerParams(vmem_limit_bytes=LIMIT),
+        cost_estimate=pl.CostEstimate(flops=1 << 16, bytes_accessed=1 << 16, transcendentals=0),
+        name="merge",
+    )(*map(pinned, kept), came, *pieces)
+
+
+def combine_kernel(kept_a_ref, kept_b_ref, came_ref, *refs):
     parts, out_ref = refs[:-1], refs[-1]
     rows = out_ref.shape[0] // 2
-    total = parts[0][...]
-    for part in parts[1:]:
+    total = came_ref[0]
+    for part in parts:
         total = total + part[...]
     count = total[4 * rows :]
     for ch in range(2):
@@ -334,17 +392,17 @@
         )
 
 
-def combine(kept, parts):
+def combine(kept, came, parts):
     rows = parts[0].shape[0] // 5
     return pl.pallas_call(
         combine_kernel,
-        in_specs=[VMEM] * (2 + len(parts)),
+        in_specs=[VMEM] * (3 + len(parts)),
         out_specs=VMEM,
         out_shape=jax.ShapeDtypeStruct((2 * rows, LANES), F32),
         compiler_params=pltpu.CompilerParams(vmem_limit_bytes=LIMIT),
         cost_estimate=pl.CostEstimate(flops=1 << 16, bytes_accessed=1 << 16, transcendentals=0),
         name="combine",
-    )(*map(pinned, kept), *parts)
+    )(*map(pinned, kept), came, *parts)
 
 
 def product(n, kept_refs, js, parts):
@@ -360,7 +418,7 @@
             for i in range(rows)
         ]
         lhs = jnp.concatenate(cols, axis=1).astype(BF16)
-        late, slot = divmod(j, n // 2)
+        late, slot = 1 - j % 2, j // 2
         total = total + jnp.dot(
             lhs,
             kept_refs[late][slot * quarter : (slot + 1) * quarter, :],
@@ -473,9 +531,12 @@
     srcs = [raw] + [swap(raw, "ani", n_ani, j) for j in range(1, n_ani)]
 
     kept_a, gain_a = front_a(genotypes, [effects_2d, theirs[0]], n)
-    kept_b, *sums = front_b(genotypes, kept_a, gain_a, [herd_2d, theirs[1]], srcs, n)
+    kept_b, odd, rest = front_b(genotypes, kept_a, gain_a, [herd_2d, theirs[1]], srcs, n)
     kept = (kept_a, kept_b)
-    resid = combine(kept, [sums[0]] + [swap(sums[j], "rec", n, j) for j in range(1, n)])
+    came = swap(odd, "rec", n, 1)
+    mine, *even = front_c(kept, rest, n)
+    even = merge(kept, came, even)
+    resid = combine(kept, came, [mine] + [swap(x, "rec", n, 2 * i + 2) for i, x in enumerate(even)])
 
     parts = [resid] + [swap(resid, "rec", n, j) for j in range(1, n)]
     grads = back(kept, [0], [resid], n)
@@ -486,7 +547,7 @@
     grad_part = own + swap(other, "chain", 2, 1)
     grad_part, swapped = lax.optimization_barrier((grad_part, swap(halves, "chain", 2, 1)))
     resid_sum = assemble(swapped, parts, n).reshape(-1)
-    others = [swap(grad_part, "ani", n_ani, j) for j in range(1, n_ani)]
+    others = [shift(grad_part, "ani", n_ani, j) for j in range(1, n_ani)]
 
     likelihood_grad = grad_part
     for x in others:

time: 57.6 us -> 56.5 us (0.981)
  waiting for transfers between devices: 12.7 us -> 10.1 us
  starting transfers between devices: 17.9 us -> 18.9 us
    pallas_call x1 -> x3, Pallas kernels: 0.02 us -> 4.46 us  [the longest x1 4.44 us: front_c(): pl.pallas_call(functools.partial(front_c_kernel, n), in_specs=[VMEM] * 3,...]
    ppermute x0 -> x3, starting transfers between devices: none -> 3 us  [shift(): return lax.ppermute(x, axis, [(i, (i + j) % size) for i in range(size)])]
    ppermute x16 -> x12, waiting for transfers between devices: 12.7 us -> 10.1 us  [swap(): return lax.ppermute(x, axis, [(i, i ^ j) for i in range(size)])]
    pallas_call x1, Pallas kernels: 8.42 us -> 6.12 us  [front_b(): pl.pallas_call(functools.partial(front_b_kernel, n, len(srcs)), in_specs=...]
    ppermute x16 -> x12, starting transfers between devices: 17.9 us -> 15.9 us  [swap(): return lax.ppermute(x, axis, [(i, i ^ j) for i in range(size)])]
    pallas_call x1, Pallas kernels: 7.63 us -> 5.99 us  [front_a(): pl.pallas_call(functools.partial(front_a_kernel, n), in_specs=[ANY] * 3,...]
  transfers between devices with their start and end apart: 16 -> 15, of which waited for: 8 -> 5; matrix products, arithmetic and copies ran while one was open for 0% -> 0% of each run, Pallas kernels for 25% -> 30%
where the time goes in v4:
time: 56.5 us; the launch traced here: 56.3 us
  Pallas kernels  24.4 us (43%)
  starting transfers between devices  18.9 us (33%)
  waiting for transfers between devices  10.1 us (18%)
  between operations  1.46 us (3%)
  local copies, waits for them, and re-layouts  0.72 us (1%)
  other arithmetic  0.67 us (1%)
    ppermute x12, starting transfers between devices, swap(): return lax.ppermute(x, axis, [(i, i ^ j) for i in range(size)])  15.9 us
    ppermute x12, waiting for transfers between devices, swap(): return lax.ppermute(x, axis, [(i, i ^ j) for i in range(size)])  10.1 us
    pallas_call x1, Pallas kernels, front_b(): pl.pallas_call(functools.partial(front_b_kernel, n, len(srcs)), in_specs=...  6.12 us
    pallas_call x1, Pallas kernels, front_a(): pl.pallas_call(functools.partial(front_a_kernel, n), in_specs=[ANY] * 3,...  5.99 us
    pallas_call x1, Pallas kernels, front_c(): pl.pallas_call(functools.partial(front_c_kernel, n), in_specs=[VMEM] * 3,...  4.44 us
    pallas_call x3, Pallas kernels, back(): pl.pallas_call(functools.partial(back_kernel, n, js), in_specs=[VMEM] * (...  3.58 us
    ppermute x3, starting transfers between devices, shift(): return lax.ppermute(x, axis, [(i, (i + j) % size) for i in range(size)])  3 us
    pallas_call x1, Pallas kernels, assemble(): pl.pallas_call(functools.partial(assemble_kernel, n), in_specs=[VMEM] * (...  1.55 us
  transfers between devices with their start and end apart: 15, of which 5 were waited for; matrix products, arithmetic and copies ran while one was open for 0% of the time, Pallas kernels for 30%

profile of v4, /device:TPU:0, one launch (start us, length us, event | category | flops | bytes accessed | tf_op | source)
XLA Modules:
  0.0 56.3 jit_solution(4934333635908598075)
XLA Ops:
  0.6 3.0 %collective-permute-start.1 = (f32[16,128]{1,0:T(8,128)}, f32[16,128]{1,0:T(8,128)S(1)}, u32[]{:S(2)}, u32[]{:S(2)}) collective-permute-start(f32[16,128]{1,0:T(8,128)} %bitcast.26), channel_id=1, source_target_pairs={{0,1},{1,0},{2,3},{3,2},{4,5},{5,4},{6,7},{7,6},{8,9},{9,8},{10,11... | collective-permute-start | bytes 24584 | tf_op jit(solution)/shard_map/ppermute | solution.py:27
  3.7 0.1 collective-permute-start
  4.4 1.5 %prepare.1.refs_0_ = f32[192,128]{1,0:T(8,128)} custom-call(s32[1,1]{1,0:T(1,128)} %bitcast.19.live_ref, s32[64,128]{1,0:T(8,128)} %bitcast.21, f32[64,128]{1,0:T(8,128)} %bitcast.22, s32[64,128]{1,0:T(8,128)} %bitcast.23), custom_call_target="tpu_custom_call" | custom-call | tf_op jit(solution)/shard_map/prepare/pallas_call | solution.py:52
  5.9 1.6 %collective-permute-done.other_any = f32[8,128]{1,0:T(8,128)S(1)} collective-permute-done((f32[8,128]{1,0:T(8,128)}, f32[8,128]{1,0:T(8,128)S(1)}, u32[]{:S(2)}, u32[]{:S(2)}) %collective-permute-start) | collective-permute-done | bytes 4128 | tf_op jit(solution)/shard_map/ppermute | solution.py:27
  7.5 0.1 collective-permute-start.2
  7.6 1.6 %collective-permute-start.3 = (f32[192,128]{1,0:T(8,128)}, f32[192,128]{1,0:T(8,128)S(1)}, u32[]{:S(2)}, u32[]{:S(2)}) collective-permute-start(f32[192,128]{1,0:T(8,128)} %prepare.1.refs_0_), channel_id=1, source_target_pairs={{0,4},{2,6},{4,0},{6,2},{1,5},{3,7},{5,1},{7,3},{8,12},{10,14},{12... | collective-permute-start | bytes 294920 | tf_op jit(solution)/shard_map/ppermute | solution.py:27
  9.1 0.3 collective-permute-start.4
  9.4 6.0 %front_a.1 = (bf16[8208,1024]{1,0:T(8,128)(2,1)S(1)}, f32[1,64,128]{2,1,0:T(8,128)}) custom-call(f32[8,128]{1,0:T(8,128)} %bitcast.25, f32[8,128]{1,0:T(8,128)} %copy-done.10, bf16[32768,1024]{1,0:T(8,128)(2,1)} %refs_7_.1), custom_call_target="tpu_custom_call" | custom-call | flops 33554432 | bytes 16777216 | tf_op jit(solution)/shard_map/front_a/pallas_call | solution.py:214
  15.5 0.6 %copy-done.4 = f32[192,128]{1,0:T(8,128)} copy-done((f32[192,128]{1,0:T(8,128)}, f32[192,128]{1,0:T(8,128)S(1)}, u32[]{:S(2)}) %copy-start.4) | copy-done | bytes 98328
  16.1 0.0 copy-done.5
  16.2 6.1 %front_b.1 = (bf16[8192,1024]{1,0:T(8,128)(2,1)S(1)}, f32[2,160,128]{2,1,0:T(8,128)S(1)}, f32[2,96,128]{2,1,0:T(8,128)S(1)}) custom-call(bf16[8208,1024]{1,0:T(8,128)(2,1)S(1)} %get-tuple-element.18.kept_a_ref, f32[192,128]{1,0:T(8,128)} %prepare.1.refs_0_, f32[192,128]{1,0:T(8,128)} %copy-done.4, f32[192,128]{1,0:T(8,128)} %copy-done.5, ...), custom_call_target="tpu_custom_call" | custom-call | flops 67108864 | bytes 16777216 | tf_op jit(solution)/shard_map/front_b/pallas_call | solution.py:302
  22.3 1.6 %collective-permute-start.5 = (f32[2,160,128]{2,1,0:T(8,128)S(1)}, f32[2,160,128]{2,1,0:T(8,128)S(1)}, u32[]{:S(2)}, u32[]{:S(2)}) collective-permute-start(f32[2,160,128]{2,1,0:T(8,128)S(1)} %get-tuple-element.23), channel_id=1, source_target_pairs={{0,8},{8,0},{16,24},{24,16},{1,9},{9,1},{17,25},{25,17},{2,10},{10... | collective-permute-start | bytes 491528 | tf_op jit(solution)/shard_map/ppermute | solution.py:27
  23.9 4.4 %front_c.1 = (f32[160,128]{1,0:T(8,128)S(1)}, f32[160,128]{1,0:T(8,128)S(1)}) custom-call(bf16[8208,1024]{1,0:T(8,128)(2,1)S(1)} %get-tuple-element.18.kept_a_ref, bf16[8192,1024]{1,0:T(8,128)(2,1)S(1)} %get-tuple-element.22.kept_b_ref, f32[2,96,128]{2,1,0:T(8,128)S(1)} %get-tuple-element.24.rest_ref), custom_call_target="tpu_custom_call" | custom-call | flops 33554432 | bytes 16777216 | tf_op jit(solution)/shard_map/front_c/pallas_call | solution.py:350
  28.4 0.4 collective-permute-done.5.came_ref
  28.8 2.7 %collective-permute-start.6 = (f32[160,128]{1,0:T(8,128)S(1)}, f32[160,128]{1,0:T(8,128)S(1)}, u32[]{:S(2)}, u32[]{:S(2)}) collective-permute-start(f32[160,128]{1,0:T(8,128)S(1)} %merge.1), channel_id=1, source_target_pairs={{0,16},{8,24},{16,0},{24,8},{1,17},{9,25},{17,1},{25,9},{2,18},{10... | collective-permute-start | bytes 245768 | tf_op jit(solution)/shard_map/ppermute | solution.py:27
  31.5 4.1 %collective-permute-done.6.refs_1_ = f32[160,128]{1,0:T(8,128)S(1)} collective-permute-done((f32[160,128]{1,0:T(8,128)S(1)}, f32[160,128]{1,0:T(8,128)S(1)}, u32[]{:S(2)}, u32[]{:S(2)}) %collective-permute-start.6) | collective-permute-done | bytes 81952 | tf_op jit(solution)/shard_map/ppermute | solution.py:27
  35.6 0.7 %collective-permute-start.8 = (f32[64,128]{1,0:T(8,128)S(1)}, f32[64,128]{1,0:T(8,128)S(1)}, u32[]{:S(2)}, u32[]{:S(2)}) collective-permute-start(f32[64,128]{1,0:T(8,128)S(1)} %combine.1.refs_0_), channel_id=1, source_target_pairs={{0,8},{8,0},{16,24},{24,16},{1,9},{9,1},{17,25},{25,17},{2,10},{10... | collective-permute-start | bytes 98312 | tf_op jit(solution)/shard_map/ppermute | solution.py:27
  36.3 3.4 %collective-permute-start.7 = (f32[64,128]{1,0:T(8,128)S(1)}, f32[64,128]{1,0:T(8,128)S(1)}, u32[]{:S(2)}, u32[]{:S(2)}) collective-permute-start(f32[64,128]{1,0:T(8,128)S(1)} %combine.1.refs_0_), channel_id=1, source_target_pairs={{0,16},{8,24},{16,0},{24,8},{1,17},{9,25},{17,1},{25,9},{2,18},{10... | collective-permute-start | bytes 98312 | tf_op jit(solution)/shard_map/ppermute | solution.py:27
  39.7 0.4 collective-permute-start.9
  40.0 1.2 %back.3.refs_1_ = f32[8,1024]{1,0:T(8,128)S(1)} custom-call(bf16[8208,1024]{1,0:T(8,128)(2,1)S(1)} %get-tuple-element.18.kept_a_ref, bf16[8192,1024]{1,0:T(8,128)(2,1)S(1)} %get-tuple-element.22.kept_b_ref, f32[64,128]{1,0:T(8,128)S(1)} %combine.1.refs_0_), custom_call_target="tpu_custom_call" | custom-call | flops 16777216 | bytes 8388608 | tf_op jit(solution)/shard_map/back/pallas_call | solution.py:438
  41.2 1.2 %back.4.refs_1_ = f32[8,1024]{1,0:T(8,128)S(1)} custom-call(bf16[8208,1024]{1,0:T(8,128)(2,1)S(1)} %get-tuple-element.18.kept_a_ref, bf16[8192,1024]{1,0:T(8,128)(2,1)S(1)} %get-tuple-element.22.kept_b_ref, f32[64,128]{1,0:T(8,128)S(1)} %collective-permute-done.8.refs_0_.refs_1_, f32[8,1024]{1,0:T(8,128)S(1)} %back.3.refs_1_), custom_call_target="tpu_custom_call" | custom-call | flops 16777216 | bytes 8388608 | tf_op jit(solution)/shard_map/back/pallas_call | solution.py:438
  42.4 1.2 %back.5.before_ref = f32[8,1024]{1,0:T(8,128)S(1)} custom-call(bf16[8208,1024]{1,0:T(8,128)(2,1)S(1)} %get-tuple-element.18.kept_a_ref, bf16[8192,1024]{1,0:T(8,128)(2,1)S(1)} %get-tuple-element.22.kept_b_ref, f32[64,128]{1,0:T(8,128)S(1)} %collective-permute-done.7.refs_0_.refs_2_, f32[8,1024]{1,0:T(8,128)S(1)} %back.4.refs_1_), custom_call_target="tpu_custom_call" | custom-call | flops 16777216 | bytes 8388608 | tf_op jit(solution)/shard_map/back/pallas_call | solution.py:438
  43.7 1.7 %collective-permute-done.9.refs_3_ = f32[64,128]{1,0:T(8,128)S(1)} collective-permute-done((f32[64,128]{1,0:T(8,128)S(1)}, f32[64,128]{1,0:T(8,128)S(1)}, u32[]{:S(2)}, u32[]{:S(2)}) %collective-permute-start.9) | collective-permute-done | bytes 32800 | tf_op jit(solution)/shard_map/ppermute | solution.py:27
  45.4 1.2 %back_last.1 = (f32[8,128]{1,0:T(8,128)S(1)}, f32[8,128]{1,0:T(8,128)S(1)}, f32[128,128]{1,0:T(8,128)S(1)}) custom-call(bf16[8208,1024]{1,0:T(8,128)(2,1)S(1)} %get-tuple-element.18.kept_a_ref, bf16[8192,1024]{1,0:T(8,128)(2,1)S(1)} %get-tuple-element.22.kept_b_ref, f32[8,1024]{1,0:T(8,128)S(1)} %back.5.before_ref, f32[64,128]{1,0:T(8,128)S(1)} %combine.1.refs_0_, ...), custom_call_target="tpu_custom_call" | custom-call | flops 16777216 | bytes 8388608 | tf_op jit(solution)/shard_map/back_last/pallas_call | solution.py:467
  46.6 0.5 collective-permute-start.11
  47.2 1.5 %collective-permute-start.10 = (f32[8,128]{1,0:T(8,128)S(1)}, f32[8,128]{1,0:T(8,128)S(1)}, u32[]{:S(2)}, u32[]{:S(2)}) collective-permute-start(f32[8,128]{1,0:T(8,128)S(1)} %get-tuple-element.28), channel_id=1, source_target_pairs={{0,1},{1,0},{2,3},{3,2},{4,5},{5,4},{6,7},{7,6},{8,9},{9,8},{10,11... | collective-permute-start | bytes 12296 | tf_op jit(solution)/shard_map/ppermute | solution.py:27
  48.7 2.3 %collective-permute-done.10 = f32[8,128]{1,0:T(8,128)S(1)} collective-permute-done((f32[8,128]{1,0:T(8,128)S(1)}, f32[8,128]{1,0:T(8,128)S(1)}, u32[]{:S(2)}, u32[]{:S(2)}) %collective-permute-start.10) | collective-permute-done | bytes 4128 | tf_op jit(solution)/shard_map/ppermute | solution.py:27
  51.0 0.1 collective-permute-start.12
  51.1 1.6 %collective-permute-start.13 = (f32[8,128]{1,0:T(8,128)S(1)}, f32[8,128]{1,0:T(8,128)S(1)}, u32[]{:S(2)}, u32[]{:S(2)}) collective-permute-start(f32[8,128]{1,0:T(8,128)S(1)} %add.18), channel_id=1, source_target_pairs={{0,4},{2,6},{4,0},{6,2},{1,5},{3,7},{5,1},{7,3},{8,12},{10,14},{12... | collective-permute-start | bytes 12296 | tf_op jit(solution)/shard_map/ppermute | solution.py:31
  52.6 1.4 %collective-permute-start.14 = (f32[8,128]{1,0:T(8,128)S(1)}, f32[8,128]{1,0:T(8,128)S(1)}, u32[]{:S(2)}, u32[]{:S(2)}) collective-permute-start(f32[8,128]{1,0:T(8,128)S(1)} %add.18), channel_id=1, source_target_pairs={{0,6},{2,0},{4,2},{6,4},{1,7},{3,1},{5,3},{7,5},{8,14},{10,8},{12,... | collective-permute-start | bytes 12296 | tf_op jit(solution)/shard_map/ppermute | solution.py:31
  54.0 1.6 %assemble.1 = f32[8,32,128]{2,1,0:T(8,128)} custom-call(f32[128,128]{1,0:T(8,128)} %copy-done.7, f32[64,128]{1,0:T(8,128)} %copy-done, f32[64,128]{1,0:T(8,128)} %copy-done.1, f32[64,128]{1,0:T(8,128)} %copy-done.2, f32[64,128]{1,0:T(8,128)} %copy-done.3), custom_call_target="tpu_custom_call" | custom-call | flops 65536 | bytes 262144 | tf_op jit(solution)/shard_map/assemble/pallas_call | solution.py:494
  55.6 0.7 %fusion.3 = f32[1024]{0:T(1024)} fusion(f32[1024]{0:T(1024)S(1)} %copy-done.8, f32[1024]{0:T(1024)S(1)} %copy-done.11, f32[1024]{0:T(1024)S(1)} %copy-done.12, f32[8,128]{1,0:T(8,128)S(1)} %collective-permute-done.14, f32[8,128]{1,0:T(8,128)S(1)} %collective-permute-done.13, f32[8,128]{1,0:T(8,128)S(1)} %add.18, f32[8,128]{1,0:T(8,128)S(1)} %collective-permute-done.12, ...), kind=kLoop, calls=%fused_computation.4 | loop fusion | flops 10240 | bytes 32776 | tf_op jit(solution)/shard_map/jit(_where)/select_n | solution.py:559
  (40 shorter events, 0.2 us)
Async XLA Ops:
  0.6 6.9 %collective-permute-start.1 = (f32[16,128]{1,0:T(8,128)}, f32[16,128]{1,0:T(8,128)S(1)}, u32[]{:S(2)}, u32[]{:S(2)}) collective-permute-start(f32[16,128]{1,0:T(8,128)} %bitcast.26), channel_id=1, source_target_pairs={{0,1},{1,0},{2,3},{3,2},{4,5},{5,4},{6,7},{7,6},{8,9},{9,8},{10,11... | collective-permute-start | bytes 24584 | tf_op jit(solution)/shard_map/ppermute | solution.py:27
  3.7 3.8 %collective-permute-start = (f32[8,128]{1,0:T(8,128)}, f32[8,128]{1,0:T(8,128)S(1)}, u32[]{:S(2)}, u32[]{:S(2)}) collective-permute-start(f32[8,128]{1,0:T(8,128)} %bitcast.24), channel_id=1, source_target_pairs={{0,1},{1,0},{2,3},{3,2},{4,5},{5,4},{6,7},{7,6},{8,9},{9,8},{10,11... | collective-permute-start | bytes 12296 | tf_op jit(solution)/shard_map/ppermute | solution.py:27
  7.5 1.9 %copy-start.10 = (f32[8,128]{1,0:T(8,128)}, f32[8,128]{1,0:T(8,128)S(1)}, u32[]{:S(2)}) copy-start(f32[8,128]{1,0:T(8,128)S(1)} %collective-permute-done.other_any) | copy-start | bytes 12292
  7.5 7.9 %copy-start.9 = (f32[16,128]{1,0:T(8,128)}, f32[16,128]{1,0:T(8,128)S(1)}, u32[]{:S(2)}) copy-start(f32[16,128]{1,0:T(8,128)S(1)} %collective-permute-done.1.refs_5_) | copy-start | bytes 24580
  7.5 7.9 %collective-permute-start.2 = (f32[192,128]{1,0:T(8,128)}, f32[192,128]{1,0:T(8,128)S(1)}, u32[]{:S(2)}, u32[]{:S(2)}) collective-permute-start(f32[192,128]{1,0:T(8,128)} %prepare.1.refs_0_), channel_id=1, source_target_pairs={{0,2},{2,0},{4,6},{6,4},{1,3},{3,1},{5,7},{7,5},{8,10},{10,8},{12,... | collective-permute-start | bytes 294920 | tf_op jit(solution)/shard_map/ppermute | solution.py:27
  7.6 7.9 %collective-permute-start.3 = (f32[192,128]{1,0:T(8,128)}, f32[192,128]{1,0:T(8,128)S(1)}, u32[]{:S(2)}, u32[]{:S(2)}) collective-permute-start(f32[192,128]{1,0:T(8,128)} %prepare.1.refs_0_), channel_id=1, source_target_pairs={{0,4},{2,6},{4,0},{6,2},{1,5},{3,7},{5,1},{7,3},{8,12},{10,14},{12... | collective-permute-start | bytes 294920 | tf_op jit(solution)/shard_map/ppermute | solution.py:27
  9.1 6.4 %collective-permute-start.4 = (f32[192,128]{1,0:T(8,128)}, f32[192,128]{1,0:T(8,128)S(1)}, u32[]{:S(2)}, u32[]{:S(2)}) collective-permute-start(f32[192,128]{1,0:T(8,128)} %prepare.1.refs_0_), channel_id=1, source_target_pairs={{0,6},{2,4},{4,2},{6,0},{1,7},{3,5},{5,3},{7,1},{8,14},{10,12},{12... | collective-permute-start | bytes 294920 | tf_op jit(solution)/shard_map/ppermute | solution.py:27
  15.4 0.6 %copy-start.4 = (f32[192,128]{1,0:T(8,128)}, f32[192,128]{1,0:T(8,128)S(1)}, u32[]{:S(2)}) copy-start(f32[192,128]{1,0:T(8,128)S(1)} %collective-permute-done.2.refs_1_) | copy-start | bytes 294916
  15.5 0.7 %copy-start.5 = (f32[192,128]{1,0:T(8,128)}, f32[192,128]{1,0:T(8,128)S(1)}, u32[]{:S(2)}) copy-start(f32[192,128]{1,0:T(8,128)S(1)} %collective-permute-done.3.refs_2_) | copy-start | bytes 294916
  15.5 0.7 %copy-start.6 = (f32[192,128]{1,0:T(8,128)}, f32[192,128]{1,0:T(8,128)S(1)}, u32[]{:S(2)}) copy-start(f32[192,128]{1,0:T(8,128)S(1)} %collective-permute-done.4.refs_3_) | copy-start | bytes 294916
  22.3 6.5 %collective-permute-start.5 = (f32[2,160,128]{2,1,0:T(8,128)S(1)}, f32[2,160,128]{2,1,0:T(8,128)S(1)}, u32[]{:S(2)}, u32[]{:S(2)}) collective-permute-start(f32[2,160,128]{2,1,0:T(8,128)S(1)} %get-tuple-element.23), channel_id=1, source_target_pairs={{0,8},{8,0},{16,24},{24,16},{1,9},{9,1},{17,25},{25,17},{2,10},{10... | collective-permute-start | bytes 491528 | tf_op jit(solution)/shard_map/ppermute | solution.py:27
  28.8 6.7 %collective-permute-start.6 = (f32[160,128]{1,0:T(8,128)S(1)}, f32[160,128]{1,0:T(8,128)S(1)}, u32[]{:S(2)}, u32[]{:S(2)}) collective-permute-start(f32[160,128]{1,0:T(8,128)S(1)} %merge.1), channel_id=1, source_target_pairs={{0,16},{8,24},{16,0},{24,8},{1,17},{9,25},{17,1},{25,9},{2,18},{10... | collective-permute-start | bytes 245768 | tf_op jit(solution)/shard_map/ppermute | solution.py:27
  35.6 9.8 %copy-start = (f32[64,128]{1,0:T(8,128)}, f32[64,128]{1,0:T(8,128)S(1)}, u32[]{:S(2)}) copy-start(f32[64,128]{1,0:T(8,128)S(1)} %combine.1.refs_0_) | copy-start | bytes 98308
  35.6 5.6 %collective-permute-start.8 = (f32[64,128]{1,0:T(8,128)S(1)}, f32[64,128]{1,0:T(8,128)S(1)}, u32[]{:S(2)}, u32[]{:S(2)}) collective-permute-start(f32[64,128]{1,0:T(8,128)S(1)} %combine.1.refs_0_), channel_id=1, source_target_pairs={{0,8},{8,0},{16,24},{24,16},{1,9},{9,1},{17,25},{25,17},{2,10},{10... | collective-permute-start | bytes 98312 | tf_op jit(solution)/shard_map/ppermute | solution.py:27
  36.3 6.1 %collective-permute-start.7 = (f32[64,128]{1,0:T(8,128)S(1)}, f32[64,128]{1,0:T(8,128)S(1)}, u32[]{:S(2)}, u32[]{:S(2)}) collective-permute-start(f32[64,128]{1,0:T(8,128)S(1)} %combine.1.refs_0_), channel_id=1, source_target_pairs={{0,16},{8,24},{16,0},{24,8},{1,17},{9,25},{17,1},{25,9},{2,18},{10... | collective-permute-start | bytes 98312 | tf_op jit(solution)/shard_map/ppermute | solution.py:27
  39.7 5.7 %collective-permute-start.9 = (f32[64,128]{1,0:T(8,128)S(1)}, f32[64,128]{1,0:T(8,128)S(1)}, u32[]{:S(2)}, u32[]{:S(2)}) collective-permute-start(f32[64,128]{1,0:T(8,128)S(1)} %combine.1.refs_0_), channel_id=1, source_target_pairs={{0,24},{8,16},{16,8},{24,0},{1,25},{9,17},{17,9},{25,1},{2,26},{10... | collective-permute-start | bytes 98312 | tf_op jit(solution)/shard_map/ppermute | solution.py:27
  41.2 4.2 %copy-start.1 = (f32[64,128]{1,0:T(8,128)}, f32[64,128]{1,0:T(8,128)S(1)}, u32[]{:S(2)}) copy-start(f32[64,128]{1,0:T(8,128)S(1)} %collective-permute-done.8.refs_0_.refs_1_) | copy-start | bytes 98308
  42.4 3.0 %copy-start.2 = (f32[64,128]{1,0:T(8,128)}, f32[64,128]{1,0:T(8,128)S(1)}, u32[]{:S(2)}) copy-start(f32[64,128]{1,0:T(8,128)S(1)} %collective-permute-done.7.refs_0_.refs_2_) | copy-start | bytes 98308
  43.6 10.4 %copy-start.13 = (s32[8]{0:T(128)S(1)}, s32[8]{0:T(128)}, u32[]{:S(2)}) copy-start(s32[8]{0:T(128)} %param.14) | copy-start | bytes 100
  43.6 12.0 %copy-start.8 = (f32[1024]{0:T(1024)S(1)}, f32[1024]{0:T(1024)}, u32[]{:S(2)}) copy-start(f32[1024]{0:T(1024)} %param.11) | copy-start | bytes 12292
  43.6 12.0 %copy-start.11 = (f32[1024]{0:T(1024)S(1)}, f32[1024]{0:T(1024)}, u32[]{:S(2)}) copy-start(f32[1024]{0:T(1024)} %param.12) | copy-start | bytes 12292
  43.6 12.0 %copy-start.12 = (f32[1024]{0:T(1024)S(1)}, f32[1024]{0:T(1024)}, u32[]{:S(2)}) copy-start(f32[1024]{0:T(1024)} %param.13) | copy-start | bytes 12292
  45.4 1.2 %copy-start.3 = (f32[64,128]{1,0:T(8,128)}, f32[64,128]{1,0:T(8,128)S(1)}, u32[]{:S(2)}) copy-start(f32[64,128]{1,0:T(8,128)S(1)} %collective-permute-done.9.refs_3_) | copy-start | bytes 98308
  46.6 4.4 %collective-permute-start.11 = (f32[128,128]{1,0:T(8,128)S(1)}, f32[128,128]{1,0:T(8,128)S(1)}, u32[]{:S(2)}, u32[]{:S(2)}) collective-permute-start(f32[128,128]{1,0:T(8,128)S(1)} %get-tuple-element.29), channel_id=1, source_target_pairs={{0,1},{1,0},{2,3},{3,2},{4,5},{5,4},{6,7},{7,6},{8,9},{9,8},{10,11... | collective-permute-start | bytes 196616 | tf_op jit(solution)/shard_map/ppermute | solution.py:27
  47.2 3.8 %collective-permute-start.10 = (f32[8,128]{1,0:T(8,128)S(1)}, f32[8,128]{1,0:T(8,128)S(1)}, u32[]{:S(2)}, u32[]{:S(2)}) collective-permute-start(f32[8,128]{1,0:T(8,128)S(1)} %get-tuple-element.28), channel_id=1, source_target_pairs={{0,1},{1,0},{2,3},{3,2},{4,5},{5,4},{6,7},{7,6},{8,9},{9,8},{10,11... | collective-permute-start | bytes 12296 | tf_op jit(solution)/shard_map/ppermute | solution.py:27
  51.0 3.0 %copy-start.7 = (f32[128,128]{1,0:T(8,128)}, f32[128,128]{1,0:T(8,128)S(1)}, u32[]{:S(2)}) copy-start(f32[128,128]{1,0:T(8,128)S(1)} %collective-permute-done.11.theirs_ref) | copy-start | bytes 196612
  51.0 4.6 %collective-permute-start.12 = (f32[8,128]{1,0:T(8,128)S(1)}, f32[8,128]{1,0:T(8,128)S(1)}, u32[]{:S(2)}, u32[]{:S(2)}) collective-permute-start(f32[8,128]{1,0:T(8,128)S(1)} %add.18), channel_id=1, source_target_pairs={{0,2},{2,4},{4,6},{6,0},{1,3},{3,5},{5,7},{7,1},{8,10},{10,12},{12... | collective-permute-start | bytes 12296 | tf_op jit(solution)/shard_map/ppermute | solution.py:31
  51.1 4.5 %collective-permute-start.13 = (f32[8,128]{1,0:T(8,128)S(1)}, f32[8,128]{1,0:T(8,128)S(1)}, u32[]{:S(2)}, u32[]{:S(2)}) collective-permute-start(f32[8,128]{1,0:T(8,128)S(1)} %add.18), channel_id=1, source_target_pairs={{0,4},{2,6},{4,0},{6,2},{1,5},{3,7},{5,1},{7,3},{8,12},{10,14},{12... | collective-permute-start | bytes 12296 | tf_op jit(solution)/shard_map/ppermute | solution.py:31
  52.6 3.0 %collective-permute-start.14 = (f32[8,128]{1,0:T(8,128)S(1)}, f32[8,128]{1,0:T(8,128)S(1)}, u32[]{:S(2)}, u32[]{:S(2)}) collective-permute-start(f32[8,128]{1,0:T(8,128)S(1)} %add.18), channel_id=1, source_target_pairs={{0,6},{2,0},{4,2},{6,4},{1,7},{3,1},{5,3},{7,5},{8,14},{10,8},{12,... | collective-permute-start | bytes 12296 | tf_op jit(solution)/shard_map/ppermute | solution.py:31

commit v5 on v4

--- a/solution.py
+++ b/solution.py
@@ -13,7 +13,6 @@
 SUBS = 64
 SPAN_BITS = 14
 CHUNK_ROWS = 16
-TILE = 1024
 LIMIT = 14 << 20
 F32 = jnp.float32
 BF16 = jnp.bfloat16
@@ -35,27 +34,82 @@
     return x.reshape(-1, LANES)
 
 
-def prepare_kernel(bins, live_ref, animal_ref, y_ref, bin_ref, raw_ref):
-    rows = animal_ref.shape[0]
+def locate(j, n):
+    i = j // 2
+    if j % 2:
+        return (0, i) if i < n // 4 else (1, i - n // 4)
+    return (1, n // 4 + i) if i < n // 4 else (2, i - n // 4)
+
+
+def load(j, n, g_hbm, kept_ref, sem):
+    chain, rec = lax.axis_index("chain"), lax.axis_index("rec")
+    half = g_hbm.shape[0] // 2
+    quarter = half // n
+    slot = locate(j, n)[1]
+    at = pl.multiple_of(chain * half + (rec ^ j) * quarter, quarter)
+    return pltpu.make_async_copy(
+        g_hbm.at[pl.ds(at, quarter), :],
+        kept_ref.at[slot * quarter : (slot + 1) * quarter, :],
+        sem.at[slot],
+    )
+
+
+def prepare_kernel(bins, n, live_ref, animal_any, y_any, bin_any, g_hbm, kept_ref, raw_any, *scratch):
+    *small_s, raw_s, sem, small_sem, raw_sem = scratch
+    small = [
+        pltpu.make_async_copy(a, b, small_sem.at[k])
+        for k, (a, b) in enumerate(zip((animal_any, y_any, bin_any), small_s))
+    ]
+    for copy in small:
+        copy.start()
+    big = [load(2 * i + 1, n, g_hbm, kept_ref, sem) for i in range(n // 4)]
+    for copy in big:
+        copy.start()
+    for copy in small:
+        copy.wait()
+    animal, y, which = small_s
+    rows = animal.shape[0]
     slot = (
         lax.broadcasted_iota(jnp.int32, (rows, LANES), 0) * LANES
         + lax.broadcasted_iota(jnp.int32, (rows, LANES), 1)
     )
-    first_bin = lax.axis_index("rec") * bins
-    raw_ref[0:rows, :] = jnp.where(slot < live_ref[...], animal_ref[...], -1).astype(F32)
-    raw_ref[rows : 2 * rows, :] = y_ref[...]
-    raw_ref[2 * rows : 3 * rows, :] = (bin_ref[...] - first_bin).astype(F32)
-
-
-def prepare(bins, live, animal, y, which):
+    raw_s[0:rows, :] = jnp.where(slot < live_ref[0], animal[...], -1).astype(F32)
+    raw_s[rows : 2 * rows, :] = y[...]
+    raw_s[2 * rows : 3 * rows, :] = (which[...] - lax.axis_index("rec") * bins).astype(F32)
+    out = pltpu.make_async_copy(raw_s, raw_any, raw_sem)
+    out.start()
+    for copy in big:
+        copy.wait()
+    out.wait()
+
+
+def in_hbm(arrays):
+    return [pltpu.with_memory_space_constraint(x, pltpu.HBM) for x in arrays]
+
+
+def prepare(genotypes, bins, n, live, animal, y, which):
     rows = animal.shape[0]
-    return pl.pallas_call(
-        functools.partial(prepare_kernel, bins),
-        in_specs=[VMEM] * 4,
-        out_specs=VMEM,
-        out_shape=pltpu.HBM((3 * rows, LANES), F32),
+    block, markers = genotypes.shape
+    return pl.pallas_call(
+        functools.partial(prepare_kernel, bins, n),
+        in_specs=[SMEM] + [ANY] * 4,
+        out_specs=[VMEM, ANY],
+        out_shape=[pltpu.VMEM((block // 8, markers), BF16), pltpu.HBM((3 * rows, LANES), F32)],
+        scratch_shapes=[
+            pltpu.VMEM((rows, LANES), jnp.int32),
+            pltpu.VMEM((rows, LANES), F32),
+            pltpu.VMEM((rows, LANES), jnp.int32),
+            pltpu.VMEM((3 * rows, LANES), F32),
+            pltpu.SemaphoreType.DMA((n // 4,)),
+            pltpu.SemaphoreType.DMA((3,)),
+            pltpu.SemaphoreType.DMA,
+        ],
+        compiler_params=pltpu.CompilerParams(vmem_limit_bytes=LIMIT),
+        cost_estimate=pl.CostEstimate(
+            flops=1 << 16, bytes_accessed=block * markers // 4, transcendentals=0
+        ),
         name="prepare",
-    )(live, animal, y, which)
+    )(live, *in_hbm([animal, y, which]), genotypes)
 
 
 def up(x, k):
@@ -149,33 +203,20 @@
             ]
 
 
-def front_a_kernel(n, own_any, other_any, g_hbm, kept_ref, gains_any, gain, own_s, other_s, sem, small_sem, out_sem):
+def front_a_kernel(n, kept_0_ref, own_any, other_any, g_hbm, kept_ref, gains_any, gain, own_s, other_s, sem, small_sem, out_sem):
     markers = kept_ref.shape[1]
     quarter = (kept_ref.shape[0] - 16) // (n // 2)
-    chain, rec = lax.axis_index("chain"), lax.axis_index("rec")
+    rows = quarter // LANES
     small = [
         pltpu.make_async_copy(a, b, small_sem.at[k])
         for k, (a, b) in enumerate([(own_any, own_s), (other_any, other_s)])
     ]
     for copy in small:
         copy.start()
-    tile = min(TILE, quarter)
-    per = quarter // tile
-    rows = quarter // LANES
-
-    def load(b):
-        owner = rec ^ (2 * (b // per) + 1)
-        at = chain * quarter * n + owner * quarter + lax.rem(b, per) * tile
-        return pltpu.make_async_copy(
-            g_hbm.at[pl.ds(pl.multiple_of(at, tile), tile), :],
-            kept_ref.at[pl.ds(pl.multiple_of(b * tile, tile), tile), :],
-            sem.at[b],
-        )
-
-    @pl.loop(0, n // 2 * per)
-    def _(b):
-        load(b).start()
-
+    odd = [load(2 * i + 1, n, g_hbm, kept_ref, sem) for i in range(n // 4, n // 2)]
+    even = [load(2 * i, n, g_hbm, kept_ref, sem) for i in range(n // 4)]
+    for copy in odd + even:
+        copy.start()
     for copy in small:
         copy.wait()
     e2 = jnp.concatenate(
@@ -187,40 +228,34 @@
         axis=0,
     ).astype(BF16)
     kept_ref[(n // 2) * quarter :, :] = e2
-
-    @pl.loop(0, n // 4 * per)
-    def _(b):
-        load(b).wait()
-        at = pl.multiple_of(b * tile, tile)
-        gains(e2[:8], kept_ref, at, tile, gain.at[b // per], lax.rem(b, per) * (tile // LANES), rows)
-
+    for i in range(n // 4):
+        gains(e2[:8], kept_0_ref, i * quarter, quarter, gain.at[i], 0, rows)
+    for i in range(n // 4):
+        odd[i].wait()
+        gains(e2[:8], kept_ref, i * quarter, quarter, gain.at[n // 4 + i], 0, rows)
     done = pltpu.make_async_copy(gain, gains_any, out_sem)
     done.start()
-
-    @pl.loop(n // 4 * per, n // 2 * per)
-    def _(b):
-        load(b).wait()
-
+    for copy in even:
+        copy.wait()
     done.wait()
 
 
-def front_a(genotypes, effects, n):
+def front_a(genotypes, kept_0, effects, n):
     block, markers = genotypes.shape
     half = block // 2
     quarter = half // n
     rows = quarter // LANES
-    tiles = n // 2 * (quarter // min(TILE, quarter))
-    shape = (n // 4, 2 * rows, LANES)
+    shape = (n // 2, 2 * rows, LANES)
     return pl.pallas_call(
         functools.partial(front_a_kernel, n),
-        in_specs=[ANY] * 3,
+        in_specs=[VMEM] + [ANY] * 3,
         out_specs=[VMEM, ANY],
         out_shape=[pltpu.VMEM((n // 2 * quarter + 16, markers), BF16), pltpu.HBM(shape, F32)],
         scratch_shapes=[
             pltpu.VMEM(shape, F32),
             pltpu.VMEM(effects[0].shape, F32),
             pltpu.VMEM(effects[1].shape, F32),
-            pltpu.SemaphoreType.DMA((tiles,)),
+            pltpu.SemaphoreType.DMA((n // 2,)),
             pltpu.SemaphoreType.DMA((2,)),
             pltpu.SemaphoreType.DMA,
         ],
@@ -229,14 +264,14 @@
             flops=2 * half * markers, bytes_accessed=half * markers, transcendentals=0
         ),
         name="front_a",
-    )(*[pltpu.with_memory_space_constraint(x, pltpu.HBM) for x in effects], genotypes)
-
-
-def front_b_kernel(n, n_src, kept_a_ref, *refs):
+    )(pinned(kept_0), *in_hbm(effects), genotypes)
+
+
+def front_b_kernel(n, n_src, kept_0_ref, kept_a_ref, *refs):
     small_any, g_hbm = refs[: n_src + 3], refs[n_src + 3]
     kept_ref, odd, rest = refs[n_src + 4 : n_src + 7]
     key_s, y_s, lane_s, sub_s, v_s, acc, tab, *small_s, sem, small_sem = refs[n_src + 7 :]
-    quarter = kept_ref.shape[0] // (n // 2)
+    quarter = kept_ref.shape[0] // (n // 4)
     half = quarter * n
     rows = quarter // LANES
     chain, rec, ani = lax.axis_index("chain"), lax.axis_index("rec"), lax.axis_index("ani")
@@ -247,17 +282,9 @@
     ]
     for copy in small:
         copy.start()
-    big = []
-    for slot in range(n // 2):
-        at = pl.multiple_of(chain * half + (rec ^ (2 * slot)) * quarter, quarter)
-        big.append(
-            pltpu.make_async_copy(
-                g_hbm.at[pl.ds(at, quarter), :],
-                kept_ref.at[slot * quarter : (slot + 1) * quarter, :],
-                sem.at[slot],
-            )
-        )
-        big[-1].start()
+    big = [load(2 * i, n, g_hbm, kept_ref, sem) for i in range(n // 4, n // 2)]
+    for copy in big:
+        copy.start()
     for copy in small:
         copy.wait()
     srcs, (*herds, gain_a) = small_s[:n_src], small_s[n_src:]
@@ -283,16 +310,12 @@
     for i in range(n // 2):
         rest[i] = tab[rec ^ (2 * i)]
         odd[i, 2 * rows : 5 * rows, :] = tab[rec ^ (2 * i + 1)]
-    for i in range(n // 4):
         odd[i, 0 : 2 * rows, :] = gain_a[i]
-    e2 = kept_a_ref[n // 2 * quarter : n // 2 * quarter + 8, :]
-    for i in range(n // 4, n // 2):
-        gains(e2, kept_a_ref, i * quarter, quarter, odd.at[i], 0, rows)
     for copy in big:
         copy.wait()
 
 
-def front_b(genotypes, kept_a, gain_a, herds, srcs, n):
+def front_b(genotypes, kept, gain_a, herds, srcs, n):
     block, markers = genotypes.shape
     half = block // 2
     quarter = half // n
@@ -301,10 +324,10 @@
     small = [*srcs, *herds, gain_a]
     return pl.pallas_call(
         functools.partial(front_b_kernel, n, len(srcs)),
-        in_specs=[VMEM] + [ANY] * (1 + len(small)),
+        in_specs=[VMEM] * 2 + [ANY] * (1 + len(small)),
         out_specs=[VMEM] * 3,
         out_shape=[
-            pltpu.VMEM((n // 2 * quarter, markers), BF16),
+            pltpu.VMEM((n // 4 * quarter, markers), BF16),
             jax.ShapeDtypeStruct((n // 2, 5 * rows, LANES), F32),
             jax.ShapeDtypeStruct((n // 2, 3 * rows, LANES), F32),
         ],
@@ -318,15 +341,15 @@
             pltpu.VMEM((n, 3 * rows, LANES), F32),
         ]
         + [pltpu.VMEM(x.shape, F32) for x in small]
-        + [pltpu.SemaphoreType.DMA((n // 2,)), pltpu.SemaphoreType.DMA((len(small),))],
+        + [pltpu.SemaphoreType.DMA((n // 4,)), pltpu.SemaphoreType.DMA((len(small),))],
         compiler_params=pltpu.CompilerParams(vmem_limit_bytes=LIMIT),
         cost_estimate=pl.CostEstimate(
             flops=4 * half * markers, bytes_accessed=half * markers, transcendentals=0
         ),
         name="front_b",
     )(
-        pinned(kept_a),
-        *[pltpu.with_memory_space_constraint(x, pltpu.HBM) for x in small],
+        *map(pinned, kept),
+        *in_hbm(small),
         genotypes,
     )
 
@@ -335,21 +358,23 @@
     return pltpu.with_memory_space_constraint(x, pltpu.VMEM)
 
 
-def front_c_kernel(n, kept_a_ref, kept_b_ref, rest_ref, *outs):
-    quarter = kept_b_ref.shape[0] // (n // 2)
+def front_c_kernel(n, kept_0_ref, kept_a_ref, kept_b_ref, rest_ref, *outs):
+    quarter = kept_b_ref.shape[0] // (n // 4)
     rows = quarter // LANES
     e2 = kept_a_ref[n // 2 * quarter : n // 2 * quarter + 8, :]
     for i in range(n // 2):
         outs[i][2 * rows : 5 * rows, :] = rest_ref[i]
-        gains(e2, kept_b_ref, i * quarter, quarter, outs[i], 0, rows)
+        late, slot = locate(2 * i, n)
+        kept_ref = (kept_0_ref, kept_a_ref, kept_b_ref)[late]
+        gains(e2, kept_ref, slot * quarter, quarter, outs[i], 0, rows)
 
 
 def front_c(kept, rest, n):
-    quarter, markers = kept[1].shape[0] // (n // 2), kept[1].shape[1]
+    quarter, markers = kept[2].shape[0] // (n // 4), kept[2].shape[1]
     piece = jax.ShapeDtypeStruct((5 * quarter // LANES, LANES), F32)
     return pl.pallas_call(
         functools.partial(front_c_kernel, n),
-        in_specs=[VMEM] * 3,
+        in_specs=[VMEM] * 4,
         out_specs=[VMEM] * (n // 2),
         out_shape=[piece] * (n // 2),
         compiler_params=pltpu.CompilerParams(vmem_limit_bytes=LIMIT),
@@ -360,7 +385,7 @@
     )(*map(pinned, kept), rest)
 
 
-def merge_kernel(kept_a_ref, kept_b_ref, came_ref, *refs):
+def merge_kernel(kept_0_ref, kept_a_ref, kept_b_ref, came_ref, *refs):
     count = len(refs) // 2
     for i in range(count):
         refs[count + i][...] = refs[i][...] + came_ref[i + 1]
@@ -369,7 +394,7 @@
 def merge(kept, came, pieces):
     return pl.pallas_call(
         merge_kernel,
-        in_specs=[VMEM] * (3 + len(pieces)),
+        in_specs=[VMEM] * (4 + len(pieces)),
         out_specs=[VMEM] * len(pieces),
         out_shape=[jax.ShapeDtypeStruct(x.shape, F32) for x in pieces],
         compiler_params=pltpu.CompilerParams(vmem_limit_bytes=LIMIT),
@@ -378,7 +403,7 @@
     )(*map(pinned, kept), came, *pieces)
 
 
-def combine_kernel(kept_a_ref, kept_b_ref, came_ref, *refs):
+def combine_kernel(kept_0_ref, kept_a_ref, kept_b_ref, came_ref, *refs):
     parts, out_ref = refs[:-1], refs[-1]
     rows = out_ref.shape[0] // 2
     total = came_ref[0]
@@ -396,7 +421,7 @@
     rows = parts[0].shape[0] // 5
     return pl.pallas_call(
         combine_kernel,
-        in_specs=[VMEM] * (3 + len(parts)),
+        in_specs=[VMEM] * (4 + len(parts)),
         out_specs=VMEM,
         out_shape=jax.ShapeDtypeStruct((2 * rows, LANES), F32),
         compiler_params=pltpu.CompilerParams(vmem_limit_bytes=LIMIT),
@@ -406,7 +431,7 @@
 
 
 def product(n, kept_refs, js, parts):
-    quarter = kept_refs[1].shape[0] // (n // 2)
+    quarter = kept_refs[2].shape[0] // (n // 4)
     rows = quarter // LANES
     total = jnp.zeros((8, kept_refs[1].shape[1]), F32)
     for j, part in zip(js, parts):
@@ -418,7 +443,7 @@
             for i in range(rows)
         ]
         lhs = jnp.concatenate(cols, axis=1).astype(BF16)
-        late, slot = 1 - j % 2, j // 2
+        late, slot = locate(j, n)
         total = total + jnp.dot(
             lhs,
             kept_refs[late][slot * quarter : (slot + 1) * quarter, :],
@@ -427,17 +452,17 @@
     return total
 
 
-def back_kernel(n, js, kept_a_ref, kept_b_ref, *refs):
+def back_kernel(n, js, kept_0_ref, kept_a_ref, kept_b_ref, *refs):
     parts, before, out_ref = refs[: len(js)], refs[len(js) : -1], refs[-1]
-    total = product(n, (kept_a_ref, kept_b_ref), js, parts)
+    total = product(n, (kept_0_ref, kept_a_ref, kept_b_ref), js, parts)
     out_ref[...] = total + before[0][...] if before else total
 
 
 def back(kept, js, parts, n, *before):
-    quarter, markers = kept[1].shape[0] // (n // 2), kept[1].shape[1]
+    quarter, markers = kept[2].shape[0] // (n // 4), kept[2].shape[1]
     return pl.pallas_call(
         functools.partial(back_kernel, n, js),
-        in_specs=[VMEM] * (2 + len(js) + len(before)),
+        in_specs=[VMEM] * (3 + len(js) + len(before)),
         out_specs=VMEM,
         out_shape=jax.ShapeDtypeStruct((8, markers), F32),
         compiler_params=pltpu.CompilerParams(vmem_limit_bytes=LIMIT),
@@ -450,23 +475,23 @@
     )(*map(pinned, kept), *parts, *before)
 
 
-def back_last_kernel(n, js, kept_a_ref, kept_b_ref, before_ref, *refs):
+def back_last_kernel(n, js, kept_0_ref, kept_a_ref, kept_b_ref, before_ref, *refs):
     parts, (own_ref, other_ref, theirs_ref) = refs[:n], refs[n:]
     rows = parts[0].shape[0] // 2
     for j in range(n):
         theirs_ref[j * rows : (j + 1) * rows, :] = parts[j][rows : 2 * rows, :]
-    total = before_ref[...] + product(n, (kept_a_ref, kept_b_ref), js, [parts[j] for j in js])
+    total = before_ref[...] + product(n, (kept_0_ref, kept_a_ref, kept_b_ref), js, [parts[j] for j in js])
     for i in range(own_ref.shape[0]):
         own_ref[i : i + 1, :] = total[0:1, i * LANES : (i + 1) * LANES]
         other_ref[i : i + 1, :] = total[1:2, i * LANES : (i + 1) * LANES]
 
 
 def back_last(kept, js, parts, n, before):
-    quarter, markers = kept[1].shape[0] // (n // 2), kept[1].shape[1]
+    quarter, markers = kept[2].shape[0] // (n // 4), kept[2].shape[1]
     grad = jax.ShapeDtypeStruct((markers // LANES, LANES), F32)
     return pl.pallas_call(
         functools.partial(back_last_kernel, n, js),
-        in_specs=[VMEM] * (3 + n),
+        in_specs=[VMEM] * (4 + n),
         out_specs=[VMEM] * 3,
         out_shape=[grad, grad, jax.ShapeDtypeStruct((n * quarter // LANES, LANES), F32)],
         compiler_params=pltpu.CompilerParams(vmem_limit_bytes=LIMIT),
@@ -520,9 +545,11 @@
 
     effects_2d, herd_2d = tiled(effects), tiled(herd_effect)
     theirs = (swap(effects_2d, "chain", 2, 1), swap(herd_2d, "chain", 2, 1))
-    raw = prepare(
+    kept_0, raw = prepare(
+        genotypes,
         herd_effect.shape[0],
-        live_records.reshape(1, 1),
+        n,
+        live_records,
         tiled(record_animal),
         tiled(phenotype),
         tiled(record_bin),
@@ -530,9 +557,9 @@
     theirs, raw = lax.optimization_barrier((theirs, raw))
     srcs = [raw] + [swap(raw, "ani", n_ani, j) for j in range(1, n_ani)]
 
-    kept_a, gain_a = front_a(genotypes, [effects_2d, theirs[0]], n)
-    kept_b, odd, rest = front_b(genotypes, kept_a, gain_a, [herd_2d, theirs[1]], srcs, n)
-    kept = (kept_a, kept_b)
+    kept_a, gain_a = front_a(genotypes, kept_0, [effects_2d, theirs[0]], n)
+    kept_b, odd, rest = front_b(genotypes, (kept_0, kept_a), gain_a, [herd_2d, theirs[1]], srcs, n)
+    kept = (kept_0, kept_a, kept_b)
     came = swap(odd, "rec", n, 1)
     mine, *even = front_c(kept, rest, n)
     even = merge(kept, came, even)

time: 56.5 us -> 56.2 us (level)
  waiting for transfers between devices: 10.1 us -> 9.31 us
    pallas_call x5, Pallas kernels: 12 us -> 14.3 us  [the longest x1 6.36 us: front_a(): pl.pallas_call(functools.partial(front_a_kernel, n), in_specs=[VMEM] + [A...]
    pallas_call x1, Pallas kernels: 6.12 us -> 3.74 us  [front_b(): pl.pallas_call(functools.partial(front_b_kernel, n, len(srcs)), in_specs=...]
    ppermute x12, waiting for transfers between devices: 10.1 us -> 9.3 us  [swap(): return lax.ppermute(x, axis, [(i, i ^ j) for i in range(size)])]
    ppermute x12, starting transfers between devices: 15.9 us -> 16.4 us  [swap(): return lax.ppermute(x, axis, [(i, i ^ j) for i in range(size)])]
  transfers between devices with their start and end apart: 15 -> 15, of which waited for: 5 -> 4; matrix products, arithmetic and copies ran while one was open for 0% -> 0% of each run, Pallas kernels for 30% -> 35%
where the time goes in v5:
time: 56.2 us; the launch traced here: 56 us
  Pallas kernels  24.4 us (43%)
  starting transfers between devices  19.4 us (35%)
  waiting for transfers between devices  9.31 us (17%)
  between operations  1.5 us (3%)
  local copies, waits for them, and re-layouts  0.72 us (1%)
  other arithmetic  0.67 us (1%)
    ppermute x12, starting transfers between devices, swap(): return lax.ppermute(x, axis, [(i, i ^ j) for i in range(size)])  16.4 us
    ppermute x12, waiting for transfers between devices, swap(): return lax.ppermute(x, axis, [(i, i ^ j) for i in range(size)])  9.3 us
    pallas_call x1, Pallas kernels, front_a(): pl.pallas_call(functools.partial(front_a_kernel, n), in_specs=[VMEM] + [A...  6.36 us
    pallas_call x1, Pallas kernels, front_c(): pl.pallas_call(functools.partial(front_c_kernel, n), in_specs=[VMEM] * 4,...  4.44 us
    pallas_call x1, Pallas kernels, front_b(): pl.pallas_call(functools.partial(front_b_kernel, n, len(srcs)), in_specs=...  3.74 us
    pallas_call x3, Pallas kernels, back(): pl.pallas_call(functools.partial(back_kernel, n, js), in_specs=[VMEM] * (...  3.58 us
    pallas_call x1, Pallas kernels, prepare(): pl.pallas_call(functools.partial(prepare_kernel, bins, n), in_specs=[SMEM...  3.52 us
    ppermute x3, starting transfers between devices, shift(): return lax.ppermute(x, axis, [(i, (i + j) % size) for i in range(size)])  2.96 us
  transfers between devices with their start and end apart: 15, of which 4 were waited for; matrix products, arithmetic and copies ran while one was open for 0% of the time, Pallas kernels for 35%

profile of v5, /device:TPU:0, one launch (start us, length us, event | category | flops | bytes accessed | tf_op | source)
XLA Modules:
  0.0 56.0 jit_solution(13559506151794686318)
XLA Ops:
  0.6 3.0 %collective-permute-start.1 = (f32[16,128]{1,0:T(8,128)}, f32[16,128]{1,0:T(8,128)S(1)}, u32[]{:S(2)}, u32[]{:S(2)}) collective-permute-start(f32[16,128]{1,0:T(8,128)} %bitcast.24), channel_id=1, source_target_pairs={{0,1},{1,0},{2,3},{3,2},{4,5},{5,4},{6,7},{7,6},{8,9},{9,8},{10,11... | collective-permute-start | bytes 24584 | tf_op jit(solution)/shard_map/ppermute | solution.py:26
  3.7 0.1 collective-permute-start
  4.4 3.5 %prepare.1 = (bf16[4096,1024]{1,0:T(8,128)(2,1)S(1)}, f32[192,128]{1,0:T(8,128)}) custom-call(s32[1]{0:T(128)S(6)} %copy.12.live_ref, s32[64,128]{1,0:T(8,128)} %bitcast.19, f32[64,128]{1,0:T(8,128)} %bitcast.20, s32[64,128]{1,0:T(8,128)} %bitcast.21, bf16[32768,1024]{1,0:T(8,128)(2,1)} %refs_7_.1), custom_call_target="tpu_custom_call" | custom-call | flops 65536 | bytes 8388608 | tf_op jit(solution)/shard_map/prepare/pallas_call | solution.py:93
  8.0 0.1 collective-permute-start.2
  8.0 2.0 %collective-permute-start.3 = (f32[192,128]{1,0:T(8,128)}, f32[192,128]{1,0:T(8,128)S(1)}, u32[]{:S(2)}, u32[]{:S(2)}) collective-permute-start(f32[192,128]{1,0:T(8,128)} %get-tuple-element.23.refs_0_), channel_id=1, source_target_pairs={{0,4},{2,6},{4,0},{6,2},{1,5},{3,7},{5,1},{7,3},{8,12},{10,14},{12... | collective-permute-start | bytes 294920 | tf_op jit(solution)/shard_map/ppermute | solution.py:26
  10.0 0.1 collective-permute-start.4
  10.1 6.4 %front_a.1 = (bf16[8208,1024]{1,0:T(8,128)(2,1)S(1)}, f32[2,64,128]{2,1,0:T(8,128)}) custom-call(bf16[4096,1024]{1,0:T(8,128)(2,1)S(1)} %get-tuple-element.19.kept_0_ref, f32[8,128]{1,0:T(8,128)} %bitcast.23, f32[8,128]{1,0:T(8,128)} %copy-done.10, bf16[32768,1024]{1,0:T(8,128)(2,1)} %refs_7_.1), custom_call_target="tpu_custom_call" | custom-call | flops 33554432 | bytes 16777216 | tf_op jit(solution)/shard_map/front_a/pallas_call | solution.py:249
  16.5 0.6 %copy-done.4 = f32[192,128]{1,0:T(8,128)} copy-done((f32[192,128]{1,0:T(8,128)}, f32[192,128]{1,0:T(8,128)S(1)}, u32[]{:S(2)}) %copy-start.4) | copy-done | bytes 98328
  17.1 0.0 copy-done.5
  17.2 0.0 copy-done.6
  17.2 3.7 %front_b.1 = (bf16[4096,1024]{1,0:T(8,128)(2,1)S(1)}, f32[2,160,128]{2,1,0:T(8,128)S(1)}, f32[2,96,128]{2,1,0:T(8,128)S(1)}) custom-call(bf16[4096,1024]{1,0:T(8,128)(2,1)S(1)} %get-tuple-element.19.kept_0_ref, bf16[8208,1024]{1,0:T(8,128)(2,1)S(1)} %get-tuple-element.22.kept_a_ref, f32[192,128]{1,0:T(8,128)} %get-tuple-element.23.refs_0_, ...), custom_call_target="tpu_custom_call" | custom-call | flops 67108864 | bytes 16777216 | tf_op jit(solution)/shard_map/front_b/pallas_call | solution.py:325
  20.9 1.9 %collective-permute-start.5 = (f32[2,160,128]{2,1,0:T(8,128)S(1)}, f32[2,160,128]{2,1,0:T(8,128)S(1)}, u32[]{:S(2)}, u32[]{:S(2)}) collective-permute-start(f32[2,160,128]{2,1,0:T(8,128)S(1)} %get-tuple-element.27), channel_id=1, source_target_pairs={{0,8},{8,0},{16,24},{24,16},{1,9},{9,1},{17,25},{25,17},{2,10},{10... | collective-permute-start | bytes 491528 | tf_op jit(solution)/shard_map/ppermute | solution.py:26
  22.8 4.4 %front_c.1 = (f32[160,128]{1,0:T(8,128)S(1)}, f32[160,128]{1,0:T(8,128)S(1)}) custom-call(bf16[4096,1024]{1,0:T(8,128)(2,1)S(1)} %get-tuple-element.19.kept_0_ref, bf16[8208,1024]{1,0:T(8,128)(2,1)S(1)} %get-tuple-element.22.kept_a_ref, bf16[4096,1024]{1,0:T(8,128)(2,1)S(1)} %get-tuple-element.26.kept_b_ref, f32[2,96,128]{2,1,0:T(8,128)S(1)} %get-tuple-element.28.rest_ref), custom_call_target="tpu_custom_call" | custom-call | flops 33554432 | bytes 16777216 | tf_op jit(solution)/shard_map/front_c/pallas_call | solution.py:375
  27.3 0.3 collective-permute-done.5.came_ref
  27.5 2.8 %collective-permute-start.6 = (f32[160,128]{1,0:T(8,128)S(1)}, f32[160,128]{1,0:T(8,128)S(1)}, u32[]{:S(2)}, u32[]{:S(2)}) collective-permute-start(f32[160,128]{1,0:T(8,128)S(1)} %merge.1), channel_id=1, source_target_pairs={{0,16},{8,24},{16,0},{24,8},{1,17},{9,25},{17,1},{25,9},{2,18},{10... | collective-permute-start | bytes 245768 | tf_op jit(solution)/shard_map/ppermute | solution.py:26
  30.4 4.1 %collective-permute-done.6.refs_1_ = f32[160,128]{1,0:T(8,128)S(1)} collective-permute-done((f32[160,128]{1,0:T(8,128)S(1)}, f32[160,128]{1,0:T(8,128)S(1)}, u32[]{:S(2)}, u32[]{:S(2)}) %collective-permute-start.6) | collective-permute-done | bytes 81952 | tf_op jit(solution)/shard_map/ppermute | solution.py:26
  34.5 0.8 %collective-permute-start.8 = (f32[64,128]{1,0:T(8,128)S(1)}, f32[64,128]{1,0:T(8,128)S(1)}, u32[]{:S(2)}, u32[]{:S(2)}) collective-permute-start(f32[64,128]{1,0:T(8,128)S(1)} %combine.1.refs_0_), channel_id=1, source_target_pairs={{0,8},{8,0},{16,24},{24,16},{1,9},{9,1},{17,25},{25,17},{2,10},{10... | collective-permute-start | bytes 98312 | tf_op jit(solution)/shard_map/ppermute | solution.py:26
  35.2 3.4 %collective-permute-start.7 = (f32[64,128]{1,0:T(8,128)S(1)}, f32[64,128]{1,0:T(8,128)S(1)}, u32[]{:S(2)}, u32[]{:S(2)}) collective-permute-start(f32[64,128]{1,0:T(8,128)S(1)} %combine.1.refs_0_), channel_id=1, source_target_pairs={{0,16},{8,24},{16,0},{24,8},{1,17},{9,25},{17,1},{25,9},{2,18},{10... | collective-permute-start | bytes 98312 | tf_op jit(solution)/shard_map/ppermute | solution.py:26
  38.6 0.3 collective-permute-start.9
  38.9 1.2 %back.3.refs_1_ = f32[8,1024]{1,0:T(8,128)S(1)} custom-call(bf16[4096,1024]{1,0:T(8,128)(2,1)S(1)} %get-tuple-element.19.kept_0_ref, bf16[8208,1024]{1,0:T(8,128)(2,1)S(1)} %get-tuple-element.22.kept_a_ref, bf16[4096,1024]{1,0:T(8,128)(2,1)S(1)} %get-tuple-element.26.kept_b_ref, f32[64,128]{1,0:T(8,128)S(1)} %combine.1.refs_0_), custom_call_target="tpu_custom_call" | custom-call | flops 16777216 | bytes 8388608 | tf_op jit(solution)/shard_map/back/pallas_call | solution.py:463
  40.1 1.2 %back.4.refs_1_ = f32[8,1024]{1,0:T(8,128)S(1)} custom-call(bf16[4096,1024]{1,0:T(8,128)(2,1)S(1)} %get-tuple-element.19.kept_0_ref, bf16[8208,1024]{1,0:T(8,128)(2,1)S(1)} %get-tuple-element.22.kept_a_ref, bf16[4096,1024]{1,0:T(8,128)(2,1)S(1)} %get-tuple-element.26.kept_b_ref, f32[64,128]{1,0:T(8,128)S(1)} %collective-permute-done.8.refs_0_.refs_1_, ...), custom_call_target="tpu_custom_call" | custom-call | flops 16777216 | bytes 8388608 | tf_op jit(solution)/shard_map/back/pallas_call | solution.py:463
  41.3 1.2 %back.5.before_ref = f32[8,1024]{1,0:T(8,128)S(1)} custom-call(bf16[4096,1024]{1,0:T(8,128)(2,1)S(1)} %get-tuple-element.19.kept_0_ref, bf16[8208,1024]{1,0:T(8,128)(2,1)S(1)} %get-tuple-element.22.kept_a_ref, bf16[4096,1024]{1,0:T(8,128)(2,1)S(1)} %get-tuple-element.26.kept_b_ref, f32[64,128]{1,0:T(8,128)S(1)} %collective-permute-done.7.refs_0_.refs_2_, ...), custom_call_target="tpu_custom_call" | custom-call | flops 16777216 | bytes 8388608 | tf_op jit(solution)/shard_map/back/pallas_call | solution.py:463
  42.6 1.8 %collective-permute-done.9.refs_3_ = f32[64,128]{1,0:T(8,128)S(1)} collective-permute-done((f32[64,128]{1,0:T(8,128)S(1)}, f32[64,128]{1,0:T(8,128)S(1)}, u32[]{:S(2)}, u32[]{:S(2)}) %collective-permute-start.9) | collective-permute-done | bytes 32800 | tf_op jit(solution)/shard_map/ppermute | solution.py:26
  44.4 1.2 %back_last.1 = (f32[8,128]{1,0:T(8,128)S(1)}, f32[8,128]{1,0:T(8,128)S(1)}, f32[128,128]{1,0:T(8,128)S(1)}) custom-call(bf16[4096,1024]{1,0:T(8,128)(2,1)S(1)} %get-tuple-element.19.kept_0_ref, bf16[8208,1024]{1,0:T(8,128)(2,1)S(1)} %get-tuple-element.22.kept_a_ref, bf16[4096,1024]{1,0:T(8,128)(2,1)S(1)} %get-tuple-element.26.kept_b_ref, ...), custom_call_target="tpu_custom_call" | custom-call | flops 16777216 | bytes 8388608 | tf_op jit(solution)/shard_map/back_last/pallas_call | solution.py:492
  45.6 1.6 %collective-permute-start.11 = (f32[128,128]{1,0:T(8,128)S(1)}, f32[128,128]{1,0:T(8,128)S(1)}, u32[]{:S(2)}, u32[]{:S(2)}) collective-permute-start(f32[128,128]{1,0:T(8,128)S(1)} %get-tuple-element.33), channel_id=1, source_target_pairs={{0,1},{1,0},{2,3},{3,2},{4,5},{5,4},{6,7},{7,6},{8,9},{9,8},{10,11... | collective-permute-start | bytes 196616 | tf_op jit(solution)/shard_map/ppermute | solution.py:26
  47.2 0.5 collective-permute-start.10
  47.7 3.1 %collective-permute-done.10 = f32[8,128]{1,0:T(8,128)S(1)} collective-permute-done((f32[8,128]{1,0:T(8,128)S(1)}, f32[8,128]{1,0:T(8,128)S(1)}, u32[]{:S(2)}, u32[]{:S(2)}) %collective-permute-start.10) | collective-permute-done | bytes 4128 | tf_op jit(solution)/shard_map/ppermute | solution.py:26
  50.8 0.1 collective-permute-start.12
  50.9 1.5 %collective-permute-start.13 = (f32[8,128]{1,0:T(8,128)S(1)}, f32[8,128]{1,0:T(8,128)S(1)}, u32[]{:S(2)}, u32[]{:S(2)}) collective-permute-start(f32[8,128]{1,0:T(8,128)S(1)} %add.18), channel_id=1, source_target_pairs={{0,4},{2,6},{4,0},{6,2},{1,5},{3,7},{5,1},{7,3},{8,12},{10,14},{12... | collective-permute-start | bytes 12296 | tf_op jit(solution)/shard_map/ppermute | solution.py:30
  52.4 1.4 %collective-permute-start.14 = (f32[8,128]{1,0:T(8,128)S(1)}, f32[8,128]{1,0:T(8,128)S(1)}, u32[]{:S(2)}, u32[]{:S(2)}) collective-permute-start(f32[8,128]{1,0:T(8,128)S(1)} %add.18), channel_id=1, source_target_pairs={{0,6},{2,0},{4,2},{6,4},{1,7},{3,1},{5,3},{7,5},{8,14},{10,8},{12,... | collective-permute-start | bytes 12296 | tf_op jit(solution)/shard_map/ppermute | solution.py:30
  53.8 1.6 %assemble.1 = f32[8,32,128]{2,1,0:T(8,128)} custom-call(f32[128,128]{1,0:T(8,128)} %copy-done.7, f32[64,128]{1,0:T(8,128)} %copy-done, f32[64,128]{1,0:T(8,128)} %copy-done.1, f32[64,128]{1,0:T(8,128)} %copy-done.2, f32[64,128]{1,0:T(8,128)} %copy-done.3), custom_call_target="tpu_custom_call" | custom-call | flops 65536 | bytes 262144 | tf_op jit(solution)/shard_map/assemble/pallas_call | solution.py:519
  55.4 0.7 %fusion.3 = f32[1024]{0:T(1024)} fusion(f32[1024]{0:T(1024)S(1)} %copy-done.8, f32[1024]{0:T(1024)S(1)} %copy-done.11, f32[1024]{0:T(1024)S(1)} %copy-done.12, f32[8,128]{1,0:T(8,128)S(1)} %collective-permute-done.14, f32[8,128]{1,0:T(8,128)S(1)} %collective-permute-done.13, f32[8,128]{1,0:T(8,128)S(1)} %add.18, f32[8,128]{1,0:T(8,128)S(1)} %collective-permute-done.12, ...), kind=kLoop, calls=%fused_computation.4 | loop fusion | flops 10240 | bytes 32776 | tf_op jit(solution)/shard_map/jit(_where)/select_n | solution.py:586
  (40 shorter events, 0.1 us)
Async XLA Ops:
  0.6 7.3 %collective-permute-start.1 = (f32[16,128]{1,0:T(8,128)}, f32[16,128]{1,0:T(8,128)S(1)}, u32[]{:S(2)}, u32[]{:S(2)}) collective-permute-start(f32[16,128]{1,0:T(8,128)} %bitcast.24), channel_id=1, source_target_pairs={{0,1},{1,0},{2,3},{3,2},{4,5},{5,4},{6,7},{7,6},{8,9},{9,8},{10,11... | collective-permute-start | bytes 24584 | tf_op jit(solution)/shard_map/ppermute | solution.py:26
  3.7 4.3 %collective-permute-start = (f32[8,128]{1,0:T(8,128)}, f32[8,128]{1,0:T(8,128)S(1)}, u32[]{:S(2)}, u32[]{:S(2)}) collective-permute-start(f32[8,128]{1,0:T(8,128)} %bitcast.22), channel_id=1, source_target_pairs={{0,1},{1,0},{2,3},{3,2},{4,5},{5,4},{6,7},{7,6},{8,9},{9,8},{10,11... | collective-permute-start | bytes 12296 | tf_op jit(solution)/shard_map/ppermute | solution.py:26
  7.9 2.2 %copy-start.10 = (f32[8,128]{1,0:T(8,128)}, f32[8,128]{1,0:T(8,128)S(1)}, u32[]{:S(2)}) copy-start(f32[8,128]{1,0:T(8,128)S(1)} %collective-permute-done.other_any) | copy-start | bytes 12292
  8.0 8.5 %copy-start.9 = (f32[16,128]{1,0:T(8,128)}, f32[16,128]{1,0:T(8,128)S(1)}, u32[]{:S(2)}) copy-start(f32[16,128]{1,0:T(8,128)S(1)} %collective-permute-done.1.refs_5_) | copy-start | bytes 24580
  8.0 8.5 %collective-permute-start.2 = (f32[192,128]{1,0:T(8,128)}, f32[192,128]{1,0:T(8,128)S(1)}, u32[]{:S(2)}, u32[]{:S(2)}) collective-permute-start(f32[192,128]{1,0:T(8,128)} %get-tuple-element.23.refs_0_), channel_id=1, source_target_pairs={{0,2},{2,0},{4,6},{6,4},{1,3},{3,1},{5,7},{7,5},{8,10},{10,8},{12,... | collective-permute-start | bytes 294920 | tf_op jit(solution)/shard_map/ppermute | solution.py:26
  8.0 8.5 %collective-permute-start.3 = (f32[192,128]{1,0:T(8,128)}, f32[192,128]{1,0:T(8,128)S(1)}, u32[]{:S(2)}, u32[]{:S(2)}) collective-permute-start(f32[192,128]{1,0:T(8,128)} %get-tuple-element.23.refs_0_), channel_id=1, source_target_pairs={{0,4},{2,6},{4,0},{6,2},{1,5},{3,7},{5,1},{7,3},{8,12},{10,14},{12... | collective-permute-start | bytes 294920 | tf_op jit(solution)/shard_map/ppermute | solution.py:26
  10.0 6.5 %collective-permute-start.4 = (f32[192,128]{1,0:T(8,128)}, f32[192,128]{1,0:T(8,128)S(1)}, u32[]{:S(2)}, u32[]{:S(2)}) collective-permute-start(f32[192,128]{1,0:T(8,128)} %get-tuple-element.23.refs_0_), channel_id=1, source_target_pairs={{0,6},{2,4},{4,2},{6,0},{1,7},{3,5},{5,3},{7,1},{8,14},{10,12},{12... | collective-permute-start | bytes 294920 | tf_op jit(solution)/shard_map/ppermute | solution.py:26
  16.5 0.6 %copy-start.4 = (f32[192,128]{1,0:T(8,128)}, f32[192,128]{1,0:T(8,128)S(1)}, u32[]{:S(2)}) copy-start(f32[192,128]{1,0:T(8,128)S(1)} %collective-permute-done.2.refs_1_) | copy-start | bytes 294916
  16.5 0.7 %copy-start.5 = (f32[192,128]{1,0:T(8,128)}, f32[192,128]{1,0:T(8,128)S(1)}, u32[]{:S(2)}) copy-start(f32[192,128]{1,0:T(8,128)S(1)} %collective-permute-done.3.refs_2_) | copy-start | bytes 294916
  16.5 0.7 %copy-start.6 = (f32[192,128]{1,0:T(8,128)}, f32[192,128]{1,0:T(8,128)S(1)}, u32[]{:S(2)}) copy-start(f32[192,128]{1,0:T(8,128)S(1)} %collective-permute-done.4.refs_3_) | copy-start | bytes 294916
  20.9 6.6 %collective-permute-start.5 = (f32[2,160,128]{2,1,0:T(8,128)S(1)}, f32[2,160,128]{2,1,0:T(8,128)S(1)}, u32[]{:S(2)}, u32[]{:S(2)}) collective-permute-start(f32[2,160,128]{2,1,0:T(8,128)S(1)} %get-tuple-element.27), channel_id=1, source_target_pairs={{0,8},{8,0},{16,24},{24,16},{1,9},{9,1},{17,25},{25,17},{2,10},{10... | collective-permute-start | bytes 491528 | tf_op jit(solution)/shard_map/ppermute | solution.py:26
  27.5 6.9 %collective-permute-start.6 = (f32[160,128]{1,0:T(8,128)S(1)}, f32[160,128]{1,0:T(8,128)S(1)}, u32[]{:S(2)}, u32[]{:S(2)}) collective-permute-start(f32[160,128]{1,0:T(8,128)S(1)} %merge.1), channel_id=1, source_target_pairs={{0,16},{8,24},{16,0},{24,8},{1,17},{9,25},{17,1},{25,9},{2,18},{10... | collective-permute-start | bytes 245768 | tf_op jit(solution)/shard_map/ppermute | solution.py:26
  34.5 9.9 %copy-start = (f32[64,128]{1,0:T(8,128)}, f32[64,128]{1,0:T(8,128)S(1)}, u32[]{:S(2)}) copy-start(f32[64,128]{1,0:T(8,128)S(1)} %combine.1.refs_0_) | copy-start | bytes 98308
  34.5 5.6 %collective-permute-start.8 = (f32[64,128]{1,0:T(8,128)S(1)}, f32[64,128]{1,0:T(8,128)S(1)}, u32[]{:S(2)}, u32[]{:S(2)}) collective-permute-start(f32[64,128]{1,0:T(8,128)S(1)} %combine.1.refs_0_), channel_id=1, source_target_pairs={{0,8},{8,0},{16,24},{24,16},{1,9},{9,1},{17,25},{25,17},{2,10},{10... | collective-permute-start | bytes 98312 | tf_op jit(solution)/shard_map/ppermute | solution.py:26
  35.2 6.1 %collective-permute-start.7 = (f32[64,128]{1,0:T(8,128)S(1)}, f32[64,128]{1,0:T(8,128)S(1)}, u32[]{:S(2)}, u32[]{:S(2)}) collective-permute-start(f32[64,128]{1,0:T(8,128)S(1)} %combine.1.refs_0_), channel_id=1, source_target_pairs={{0,16},{8,24},{16,0},{24,8},{1,17},{9,25},{17,1},{25,9},{2,18},{10... | collective-permute-start | bytes 98312 | tf_op jit(solution)/shard_map/ppermute | solution.py:26
  38.6 5.7 %collective-permute-start.9 = (f32[64,128]{1,0:T(8,128)S(1)}, f32[64,128]{1,0:T(8,128)S(1)}, u32[]{:S(2)}, u32[]{:S(2)}) collective-permute-start(f32[64,128]{1,0:T(8,128)S(1)} %combine.1.refs_0_), channel_id=1, source_target_pairs={{0,24},{8,16},{16,8},{24,0},{1,25},{9,17},{17,9},{25,1},{2,26},{10... | collective-permute-start | bytes 98312 | tf_op jit(solution)/shard_map/ppermute | solution.py:26
  40.1 4.2 %copy-start.1 = (f32[64,128]{1,0:T(8,128)}, f32[64,128]{1,0:T(8,128)S(1)}, u32[]{:S(2)}) copy-start(f32[64,128]{1,0:T(8,128)S(1)} %collective-permute-done.8.refs_0_.refs_1_) | copy-start | bytes 98308
  41.3 3.0 %copy-start.2 = (f32[64,128]{1,0:T(8,128)}, f32[64,128]{1,0:T(8,128)S(1)}, u32[]{:S(2)}) copy-start(f32[64,128]{1,0:T(8,128)S(1)} %collective-permute-done.7.refs_0_.refs_2_) | copy-start | bytes 98308
  42.5 11.2 %copy-start.13 = (s32[8]{0:T(128)S(1)}, s32[8]{0:T(128)}, u32[]{:S(2)}) copy-start(s32[8]{0:T(128)} %param.14) | copy-start | bytes 100
  42.5 12.8 %copy-start.8 = (f32[1024]{0:T(1024)S(1)}, f32[1024]{0:T(1024)}, u32[]{:S(2)}) copy-start(f32[1024]{0:T(1024)} %param.11) | copy-start | bytes 12292
  42.5 12.8 %copy-start.11 = (f32[1024]{0:T(1024)S(1)}, f32[1024]{0:T(1024)}, u32[]{:S(2)}) copy-start(f32[1024]{0:T(1024)} %param.12) | copy-start | bytes 12292
  42.5 12.8 %copy-start.12 = (f32[1024]{0:T(1024)S(1)}, f32[1024]{0:T(1024)}, u32[]{:S(2)}) copy-start(f32[1024]{0:T(1024)} %param.13) | copy-start | bytes 12292
  44.4 1.2 %copy-start.3 = (f32[64,128]{1,0:T(8,128)}, f32[64,128]{1,0:T(8,128)S(1)}, u32[]{:S(2)}) copy-start(f32[64,128]{1,0:T(8,128)S(1)} %collective-permute-done.9.refs_3_) | copy-start | bytes 98308
  45.6 5.2 %collective-permute-start.11 = (f32[128,128]{1,0:T(8,128)S(1)}, f32[128,128]{1,0:T(8,128)S(1)}, u32[]{:S(2)}, u32[]{:S(2)}) collective-permute-start(f32[128,128]{1,0:T(8,128)S(1)} %get-tuple-element.33), channel_id=1, source_target_pairs={{0,1},{1,0},{2,3},{3,2},{4,5},{5,4},{6,7},{7,6},{8,9},{9,8},{10,11... | collective-permute-start | bytes 196616 | tf_op jit(solution)/shard_map/ppermute | solution.py:26
  47.2 3.6 %collective-permute-start.10 = (f32[8,128]{1,0:T(8,128)S(1)}, f32[8,128]{1,0:T(8,128)S(1)}, u32[]{:S(2)}, u32[]{:S(2)}) collective-permute-start(f32[8,128]{1,0:T(8,128)S(1)} %get-tuple-element.32), channel_id=1, source_target_pairs={{0,1},{1,0},{2,3},{3,2},{4,5},{5,4},{6,7},{7,6},{8,9},{9,8},{10,11... | collective-permute-start | bytes 12296 | tf_op jit(solution)/shard_map/ppermute | solution.py:26
  50.8 3.0 %copy-start.7 = (f32[128,128]{1,0:T(8,128)}, f32[128,128]{1,0:T(8,128)S(1)}, u32[]{:S(2)}) copy-start(f32[128,128]{1,0:T(8,128)S(1)} %collective-permute-done.11.theirs_ref) | copy-start | bytes 196612
  50.8 4.5 %collective-permute-start.12 = (f32[8,128]{1,0:T(8,128)S(1)}, f32[8,128]{1,0:T(8,128)S(1)}, u32[]{:S(2)}, u32[]{:S(2)}) collective-permute-start(f32[8,128]{1,0:T(8,128)S(1)} %add.18), channel_id=1, source_target_pairs={{0,2},{2,4},{4,6},{6,0},{1,3},{3,5},{5,7},{7,1},{8,10},{10,12},{12... | collective-permute-start | bytes 12296 | tf_op jit(solution)/shard_map/ppermute | solution.py:30
  50.9 4.5 %collective-permute-start.13 = (f32[8,128]{1,0:T(8,128)S(1)}, f32[8,128]{1,0:T(8,128)S(1)}, u32[]{:S(2)}, u32[]{:S(2)}) collective-permute-start(f32[8,128]{1,0:T(8,128)S(1)} %add.18), channel_id=1, source_target_pairs={{0,4},{2,6},{4,0},{6,2},{1,5},{3,7},{5,1},{7,3},{8,12},{10,14},{12... | collective-permute-start | bytes 12296 | tf_op jit(solution)/shard_map/ppermute | solution.py:30
  52.4 3.0 %collective-permute-start.14 = (f32[8,128]{1,0:T(8,128)S(1)}, f32[8,128]{1,0:T(8,128)S(1)}, u32[]{:S(2)}, u32[]{:S(2)}) collective-permute-start(f32[8,128]{1,0:T(8,128)S(1)} %add.18), channel_id=1, source_target_pairs={{0,6},{2,0},{4,2},{6,4},{1,7},{3,1},{5,3},{7,5},{8,14},{10,8},{12,... | collective-permute-start | bytes 12296 | tf_op jit(solution)/shard_map/ppermute | solution.py:30

commit v6 on v5

--- a/solution.py
+++ b/solution.py
@@ -476,14 +476,16 @@
 
 
 def back_last_kernel(n, js, kept_0_ref, kept_a_ref, kept_b_ref, before_ref, *refs):
-    parts, (own_ref, other_ref, theirs_ref) = refs[:n], refs[n:]
+    parts, (own_ref, theirs_ref) = refs[:n], refs[n:]
+    e_rows = own_ref.shape[0]
     rows = parts[0].shape[0] // 2
     for j in range(n):
-        theirs_ref[j * rows : (j + 1) * rows, :] = parts[j][rows : 2 * rows, :]
+        at = e_rows + j * rows
+        theirs_ref[at : at + rows, :] = parts[j][rows : 2 * rows, :]
     total = before_ref[...] + product(n, (kept_0_ref, kept_a_ref, kept_b_ref), js, [parts[j] for j in js])
     for i in range(own_ref.shape[0]):
         own_ref[i : i + 1, :] = total[0:1, i * LANES : (i + 1) * LANES]
-        other_ref[i : i + 1, :] = total[1:2, i * LANES : (i + 1) * LANES]
+        theirs_ref[i : i + 1, :] = total[1:2, i * LANES : (i + 1) * LANES]
 
 
 def back_last(kept, js, parts, n, before):
@@ -492,8 +494,11 @@
     return pl.pallas_call(
         functools.partial(back_last_kernel, n, js),
         in_specs=[VMEM] * (4 + n),
-        out_specs=[VMEM] * 3,
-        out_shape=[grad, grad, jax.ShapeDtypeStruct((n * quarter // LANES, LANES), F32)],
+        out_specs=[VMEM] * 2,
+        out_shape=[
+            grad,
+            jax.ShapeDtypeStruct((markers // LANES + n * quarter // LANES, LANES), F32),
+        ],
         compiler_params=pltpu.CompilerParams(vmem_limit_bytes=LIMIT),
         cost_estimate=pl.CostEstimate(
             flops=4 * quarter * markers * len(js),
@@ -507,11 +512,14 @@
 def assemble_kernel(n, theirs_ref, *refs):
     parts, out_ref = refs[:n], refs[n]
     rows = parts[0].shape[0] // 2
+    e_rows = theirs_ref.shape[0] - n * rows
     chain, rec = lax.axis_index("chain"), lax.axis_index("rec")
     for j in range(n):
         owner = rec ^ j
         out_ref[chain * n + owner] = parts[j][0:rows, :]
-        out_ref[(1 - chain) * n + owner] = theirs_ref[j * rows : (j + 1) * rows, :]
+        out_ref[(1 - chain) * n + owner] = theirs_ref[
+            e_rows + j * rows : e_rows + (j + 1) * rows, :
+        ]
 
 
 def assemble(theirs, parts, n):
@@ -570,9 +578,9 @@
     steps = [list(range(j, min(j + n // 4, n))) for j in range(1, n, n // 4)]
     for js in steps[:-1]:
         grads = back(kept, js, [parts[j] for j in js], n, grads)
-    own, other, halves = back_last(kept, steps[-1], parts, n, grads)
-    grad_part = own + swap(other, "chain", 2, 1)
-    grad_part, swapped = lax.optimization_barrier((grad_part, swap(halves, "chain", 2, 1)))
+    own, theirs = back_last(kept, steps[-1], parts, n, grads)
+    swapped = swap(theirs, "chain", 2, 1)
+    grad_part = own + swapped[: own.shape[0]]
     resid_sum = assemble(swapped, parts, n).reshape(-1)
     others = [shift(grad_part, "ani", n_ani, j) for j in range(1, n_ani)]
 

time: 56.2 us -> 55.4 us (0.986)
    ppermute x12 -> x11, starting transfers between devices: 16.4 us -> 15.9 us  [swap(): return lax.ppermute(x, axis, [(i, i ^ j) for i in range(size)])]
    ppermute x12 -> x11, waiting for transfers between devices: 9.3 us -> 8.91 us  [swap(): return lax.ppermute(x, axis, [(i, i ^ j) for i in range(size)])]
  transfers between devices with their start and end apart: 15 -> 14, of which waited for: 4 -> 4; matrix products, arithmetic and copies ran while one was open for 0% -> 0% of each run, Pallas kernels for 35% -> 35%
where the time goes in v6:
time: 55.4 us; the launch traced here: 55.2 us
  Pallas kernels  24.5 us (44%)
  starting transfers between devices  18.9 us (34%)
  waiting for transfers between devices  8.91 us (16%)
  between operations  1.49 us (3%)
  local copies, waits for them, and re-layouts  0.72 us (1%)
  other arithmetic  0.67 us (1%)
    ppermute x11, starting transfers between devices, swap(): return lax.ppermute(x, axis, [(i, i ^ j) for i in range(size)])  15.9 us
    ppermute x11, waiting for transfers between devices, swap(): return lax.ppermute(x, axis, [(i, i ^ j) for i in range(size)])  8.91 us
    pallas_call x1, Pallas kernels, front_a(): pl.pallas_call(functools.partial(front_a_kernel, n), in_specs=[VMEM] + [A...  6.37 us
    pallas_call x1, Pallas kernels, front_c(): pl.pallas_call(functools.partial(front_c_kernel, n), in_specs=[VMEM] * 4,...  4.44 us
    pallas_call x1, Pallas kernels, front_b(): pl.pallas_call(functools.partial(front_b_kernel, n, len(srcs)), in_specs=...  3.74 us
    pallas_call x3, Pallas kernels, back(): pl.pallas_call(functools.partial(back_kernel, n, js), in_specs=[VMEM] * (...  3.58 us
    pallas_call x1, Pallas kernels, prepare(): pl.pallas_call(functools.partial(prepare_kernel, bins, n), in_specs=[SMEM...  3.52 us
    ppermute x3, starting transfers between devices, shift(): return lax.ppermute(x, axis, [(i, (i + j) % size) for i in range(size)])  2.95 us
  transfers between devices with their start and end apart: 14, of which 4 were waited for; matrix products, arithmetic and copies ran while one was open for 0% of the time, Pallas kernels for 35%

profile of v6, /device:TPU:0, one launch (start us, length us, event | category | flops | bytes accessed | tf_op | source)
XLA Modules:
  0.0 55.2 jit_solution(13807066255236821062)
XLA Ops:
  0.6 3.0 %collective-permute-start.1 = (f32[16,128]{1,0:T(8,128)}, f32[16,128]{1,0:T(8,128)S(1)}, u32[]{:S(2)}, u32[]{:S(2)}) collective-permute-start(f32[16,128]{1,0:T(8,128)} %bitcast.24), channel_id=1, source_target_pairs={{0,1},{1,0},{2,3},{3,2},{4,5},{5,4},{6,7},{7,6},{8,9},{9,8},{10,11... | collective-permute-start | bytes 24584 | tf_op jit(solution)/shard_map/ppermute | solution.py:26
  3.7 0.1 collective-permute-start
  4.4 3.5 %prepare.1 = (bf16[4096,1024]{1,0:T(8,128)(2,1)S(1)}, f32[192,128]{1,0:T(8,128)}) custom-call(s32[1]{0:T(128)S(6)} %copy.12.live_ref, s32[64,128]{1,0:T(8,128)} %bitcast.19, f32[64,128]{1,0:T(8,128)} %bitcast.20, s32[64,128]{1,0:T(8,128)} %bitcast.21, bf16[32768,1024]{1,0:T(8,128)(2,1)} %refs_7_.1), custom_call_target="tpu_custom_call" | custom-call | flops 65536 | bytes 8388608 | tf_op jit(solution)/shard_map/prepare/pallas_call | solution.py:93
  7.9 0.0 copy-start.10
  8.0 0.1 collective-permute-start.2
  8.0 2.0 %collective-permute-start.3 = (f32[192,128]{1,0:T(8,128)}, f32[192,128]{1,0:T(8,128)S(1)}, u32[]{:S(2)}, u32[]{:S(2)}) collective-permute-start(f32[192,128]{1,0:T(8,128)} %get-tuple-element.20.refs_0_), channel_id=1, source_target_pairs={{0,4},{2,6},{4,0},{6,2},{1,5},{3,7},{5,1},{7,3},{8,12},{10,14},{12... | collective-permute-start | bytes 294920 | tf_op jit(solution)/shard_map/ppermute | solution.py:26
  10.0 0.1 collective-permute-start.4
  10.1 6.4 %front_a.1 = (bf16[8208,1024]{1,0:T(8,128)(2,1)S(1)}, f32[2,64,128]{2,1,0:T(8,128)}) custom-call(bf16[4096,1024]{1,0:T(8,128)(2,1)S(1)} %get-tuple-element.16.kept_0_ref, f32[8,128]{1,0:T(8,128)} %bitcast.23, f32[8,128]{1,0:T(8,128)} %copy-done.10, bf16[32768,1024]{1,0:T(8,128)(2,1)} %refs_7_.1), custom_call_target="tpu_custom_call" | custom-call | flops 33554432 | bytes 16777216 | tf_op jit(solution)/shard_map/front_a/pallas_call | solution.py:249
  16.6 0.6 %copy-done.4 = f32[192,128]{1,0:T(8,128)} copy-done((f32[192,128]{1,0:T(8,128)}, f32[192,128]{1,0:T(8,128)S(1)}, u32[]{:S(2)}) %copy-start.4) | copy-done | bytes 98328
  17.1 0.0 copy-done.5
  17.2 0.0 copy-done.6
  17.2 3.7 %front_b.1 = (bf16[4096,1024]{1,0:T(8,128)(2,1)S(1)}, f32[2,160,128]{2,1,0:T(8,128)S(1)}, f32[2,96,128]{2,1,0:T(8,128)S(1)}) custom-call(bf16[4096,1024]{1,0:T(8,128)(2,1)S(1)} %get-tuple-element.16.kept_0_ref, bf16[8208,1024]{1,0:T(8,128)(2,1)S(1)} %get-tuple-element.19.kept_a_ref, f32[192,128]{1,0:T(8,128)} %get-tuple-element.20.refs_0_, ...), custom_call_target="tpu_custom_call" | custom-call | flops 67108864 | bytes 16777216 | tf_op jit(solution)/shard_map/front_b/pallas_call | solution.py:325
  21.0 1.9 %collective-permute-start.5 = (f32[2,160,128]{2,1,0:T(8,128)S(1)}, f32[2,160,128]{2,1,0:T(8,128)S(1)}, u32[]{:S(2)}, u32[]{:S(2)}) collective-permute-start(f32[2,160,128]{2,1,0:T(8,128)S(1)} %get-tuple-element.24), channel_id=1, source_target_pairs={{0,8},{8,0},{16,24},{24,16},{1,9},{9,1},{17,25},{25,17},{2,10},{10... | collective-permute-start | bytes 491528 | tf_op jit(solution)/shard_map/ppermute | solution.py:26
  22.9 4.4 %front_c.1 = (f32[160,128]{1,0:T(8,128)S(1)}, f32[160,128]{1,0:T(8,128)S(1)}) custom-call(bf16[4096,1024]{1,0:T(8,128)(2,1)S(1)} %get-tuple-element.16.kept_0_ref, bf16[8208,1024]{1,0:T(8,128)(2,1)S(1)} %get-tuple-element.19.kept_a_ref, bf16[4096,1024]{1,0:T(8,128)(2,1)S(1)} %get-tuple-element.23.kept_b_ref, f32[2,96,128]{2,1,0:T(8,128)S(1)} %get-tuple-element.25.rest_ref), custom_call_target="tpu_custom_call" | custom-call | flops 33554432 | bytes 16777216 | tf_op jit(solution)/shard_map/front_c/pallas_call | solution.py:375
  27.3 0.3 collective-permute-done.5.came_ref
  27.6 2.8 %collective-permute-start.6 = (f32[160,128]{1,0:T(8,128)S(1)}, f32[160,128]{1,0:T(8,128)S(1)}, u32[]{:S(2)}, u32[]{:S(2)}) collective-permute-start(f32[160,128]{1,0:T(8,128)S(1)} %merge.1), channel_id=1, source_target_pairs={{0,16},{8,24},{16,0},{24,8},{1,17},{9,25},{17,1},{25,9},{2,18},{10... | collective-permute-start | bytes 245768 | tf_op jit(solution)/shard_map/ppermute | solution.py:26
  30.4 4.1 %collective-permute-done.6.refs_1_ = f32[160,128]{1,0:T(8,128)S(1)} collective-permute-done((f32[160,128]{1,0:T(8,128)S(1)}, f32[160,128]{1,0:T(8,128)S(1)}, u32[]{:S(2)}, u32[]{:S(2)}) %collective-permute-start.6) | collective-permute-done | bytes 81952 | tf_op jit(solution)/shard_map/ppermute | solution.py:26
  34.6 0.7 %collective-permute-start.8 = (f32[64,128]{1,0:T(8,128)S(1)}, f32[64,128]{1,0:T(8,128)S(1)}, u32[]{:S(2)}, u32[]{:S(2)}) collective-permute-start(f32[64,128]{1,0:T(8,128)S(1)} %combine.1.refs_0_), channel_id=1, source_target_pairs={{0,8},{8,0},{16,24},{24,16},{1,9},{9,1},{17,25},{25,17},{2,10},{10... | collective-permute-start | bytes 98312 | tf_op jit(solution)/shard_map/ppermute | solution.py:26
  35.2 3.4 %collective-permute-start.7 = (f32[64,128]{1,0:T(8,128)S(1)}, f32[64,128]{1,0:T(8,128)S(1)}, u32[]{:S(2)}, u32[]{:S(2)}) collective-permute-start(f32[64,128]{1,0:T(8,128)S(1)} %combine.1.refs_0_), channel_id=1, source_target_pairs={{0,16},{8,24},{16,0},{24,8},{1,17},{9,25},{17,1},{25,9},{2,18},{10... | collective-permute-start | bytes 98312 | tf_op jit(solution)/shard_map/ppermute | solution.py:26
  38.6 0.4 collective-permute-start.9
  39.0 1.2 %back.3.refs_1_ = f32[8,1024]{1,0:T(8,128)S(1)} custom-call(bf16[4096,1024]{1,0:T(8,128)(2,1)S(1)} %get-tuple-element.16.kept_0_ref, bf16[8208,1024]{1,0:T(8,128)(2,1)S(1)} %get-tuple-element.19.kept_a_ref, bf16[4096,1024]{1,0:T(8,128)(2,1)S(1)} %get-tuple-element.23.kept_b_ref, f32[64,128]{1,0:T(8,128)S(1)} %combine.1.refs_0_), custom_call_target="tpu_custom_call" | custom-call | flops 16777216 | bytes 8388608 | tf_op jit(solution)/shard_map/back/pallas_call | solution.py:463
  40.2 1.2 %back.4.refs_1_ = f32[8,1024]{1,0:T(8,128)S(1)} custom-call(bf16[4096,1024]{1,0:T(8,128)(2,1)S(1)} %get-tuple-element.16.kept_0_ref, bf16[8208,1024]{1,0:T(8,128)(2,1)S(1)} %get-tuple-element.19.kept_a_ref, bf16[4096,1024]{1,0:T(8,128)(2,1)S(1)} %get-tuple-element.23.kept_b_ref, f32[64,128]{1,0:T(8,128)S(1)} %collective-permute-done.8.refs_0_.refs_1_, ...), custom_call_target="tpu_custom_call" | custom-call | flops 16777216 | bytes 8388608 | tf_op jit(solution)/shard_map/back/pallas_call | solution.py:463
  41.4 1.2 %back.5.before_ref = f32[8,1024]{1,0:T(8,128)S(1)} custom-call(bf16[4096,1024]{1,0:T(8,128)(2,1)S(1)} %get-tuple-element.16.kept_0_ref, bf16[8208,1024]{1,0:T(8,128)(2,1)S(1)} %get-tuple-element.19.kept_a_ref, bf16[4096,1024]{1,0:T(8,128)(2,1)S(1)} %get-tuple-element.23.kept_b_ref, f32[64,128]{1,0:T(8,128)S(1)} %collective-permute-done.7.refs_0_.refs_2_, ...), custom_call_target="tpu_custom_call" | custom-call | flops 16777216 | bytes 8388608 | tf_op jit(solution)/shard_map/back/pallas_call | solution.py:463
  42.6 0.0 copy-start.12
  42.6 1.7 %collective-permute-done.9.refs_3_ = f32[64,128]{1,0:T(8,128)S(1)} collective-permute-done((f32[64,128]{1,0:T(8,128)S(1)}, f32[64,128]{1,0:T(8,128)S(1)}, u32[]{:S(2)}, u32[]{:S(2)}) %collective-permute-start.9) | collective-permute-done | bytes 32800 | tf_op jit(solution)/shard_map/ppermute | solution.py:26
  44.3 1.2 %back_last.1 = (f32[8,128]{1,0:T(8,128)S(1)}, f32[136,128]{1,0:T(8,128)S(1)}) custom-call(bf16[4096,1024]{1,0:T(8,128)(2,1)S(1)} %get-tuple-element.16.kept_0_ref, bf16[8208,1024]{1,0:T(8,128)(2,1)S(1)} %get-tuple-element.19.kept_a_ref, bf16[4096,1024]{1,0:T(8,128)(2,1)S(1)} %get-tuple-element.23.kept_b_ref, f32[8,1024]{1,0:T(8,128)S(1)} %back.5.before_ref, ...), custom_call_target="tpu_custom_call" | custom-call | flops 16777216 | bytes 8388608 | tf_op jit(solution)/shard_map/back_last/pallas_call | solution.py:494
  45.5 1.6 %collective-permute-start.10 = (f32[136,128]{1,0:T(8,128)S(1)}, f32[136,128]{1,0:T(8,128)S(1)}, u32[]{:S(2)}, u32[]{:S(2)}) collective-permute-start(f32[136,128]{1,0:T(8,128)S(1)} %get-tuple-element.29), channel_id=1, source_target_pairs={{0,1},{1,0},{2,3},{3,2},{4,5},{5,4},{6,7},{7,6},{8,9},{9,8},{10,11... | collective-permute-start | bytes 208904 | tf_op jit(solution)/shard_map/ppermute | solution.py:26
  47.1 2.8 %collective-permute-done.10.theirs_ref = f32[136,128]{1,0:T(8,128)S(1)} collective-permute-done((f32[136,128]{1,0:T(8,128)S(1)}, f32[136,128]{1,0:T(8,128)S(1)}, u32[]{:S(2)}, u32[]{:S(2)}) %collective-permute-start.10) | collective-permute-done | bytes 69664 | tf_op jit(solution)/shard_map/ppermute | solution.py:26
  49.9 1.6 %collective-permute-start.12 = (f32[8,128]{1,0:T(8,128)S(1)}, f32[8,128]{1,0:T(8,128)S(1)}, u32[]{:S(2)}, u32[]{:S(2)}) collective-permute-start(f32[8,128]{1,0:T(8,128)S(1)} %slice_add_fusion), channel_id=1, source_target_pairs={{0,4},{2,6},{4,0},{6,2},{1,5},{3,7},{5,1},{7,3},{8,12},{10,14},{12... | collective-permute-start | bytes 12296 | tf_op jit(solution)/shard_map/ppermute | solution.py:30
  51.5 1.4 %collective-permute-start.13 = (f32[8,128]{1,0:T(8,128)S(1)}, f32[8,128]{1,0:T(8,128)S(1)}, u32[]{:S(2)}, u32[]{:S(2)}) collective-permute-start(f32[8,128]{1,0:T(8,128)S(1)} %slice_add_fusion), channel_id=1, source_target_pairs={{0,6},{2,0},{4,2},{6,4},{1,7},{3,1},{5,3},{7,5},{8,14},{10,8},{12,... | collective-permute-start | bytes 12296 | tf_op jit(solution)/shard_map/ppermute | solution.py:30
  52.9 1.6 %assemble.1 = f32[8,32,128]{2,1,0:T(8,128)} custom-call(f32[136,128]{1,0:T(8,128)} %copy-done.7, f32[64,128]{1,0:T(8,128)} %copy-done, f32[64,128]{1,0:T(8,128)} %copy-done.1, f32[64,128]{1,0:T(8,128)} %copy-done.2, f32[64,128]{1,0:T(8,128)} %copy-done.3), custom_call_target="tpu_custom_call" | custom-call | flops 65536 | bytes 262144 | tf_op jit(solution)/shard_map/assemble/pallas_call | solution.py:527
  54.5 0.7 %fusion.3 = f32[1024]{0:T(1024)} fusion(f32[1024]{0:T(1024)S(1)} %copy-done.8, f32[1024]{0:T(1024)S(1)} %copy-done.11, f32[1024]{0:T(1024)S(1)} %copy-done.12, f32[8,128]{1,0:T(8,128)S(1)} %collective-permute-done.13, f32[8,128]{1,0:T(8,128)S(1)} %collective-permute-done.12, f32[8,128]{1,0:T(8,128)S(1)} %slice_add_fusion, ...), kind=kLoop, calls=%fused_computation.5 | loop fusion | flops 10240 | bytes 32776 | tf_op jit(solution)/shard_map/jit(_where)/select_n | solution.py:594
  (38 shorter events, 0.1 us)
Async XLA Ops:
  0.6 7.3 %collective-permute-start.1 = (f32[16,128]{1,0:T(8,128)}, f32[16,128]{1,0:T(8,128)S(1)}, u32[]{:S(2)}, u32[]{:S(2)}) collective-permute-start(f32[16,128]{1,0:T(8,128)} %bitcast.24), channel_id=1, source_target_pairs={{0,1},{1,0},{2,3},{3,2},{4,5},{5,4},{6,7},{7,6},{8,9},{9,8},{10,11... | collective-permute-start | bytes 24584 | tf_op jit(solution)/shard_map/ppermute | solution.py:26
  3.7 4.3 %collective-permute-start = (f32[8,128]{1,0:T(8,128)}, f32[8,128]{1,0:T(8,128)S(1)}, u32[]{:S(2)}, u32[]{:S(2)}) collective-permute-start(f32[8,128]{1,0:T(8,128)} %bitcast.22), channel_id=1, source_target_pairs={{0,1},{1,0},{2,3},{3,2},{4,5},{5,4},{6,7},{7,6},{8,9},{9,8},{10,11... | collective-permute-start | bytes 12296 | tf_op jit(solution)/shard_map/ppermute | solution.py:26
  7.9 2.2 %copy-start.10 = (f32[8,128]{1,0:T(8,128)}, f32[8,128]{1,0:T(8,128)S(1)}, u32[]{:S(2)}) copy-start(f32[8,128]{1,0:T(8,128)S(1)} %collective-permute-done.other_any) | copy-start | bytes 12292
  8.0 8.5 %copy-start.9 = (f32[16,128]{1,0:T(8,128)}, f32[16,128]{1,0:T(8,128)S(1)}, u32[]{:S(2)}) copy-start(f32[16,128]{1,0:T(8,128)S(1)} %collective-permute-done.1.refs_5_) | copy-start | bytes 24580
  8.0 8.5 %collective-permute-start.2 = (f32[192,128]{1,0:T(8,128)}, f32[192,128]{1,0:T(8,128)S(1)}, u32[]{:S(2)}, u32[]{:S(2)}) collective-permute-start(f32[192,128]{1,0:T(8,128)} %get-tuple-element.20.refs_0_), channel_id=1, source_target_pairs={{0,2},{2,0},{4,6},{6,4},{1,3},{3,1},{5,7},{7,5},{8,10},{10,8},{12,... | collective-permute-start | bytes 294920 | tf_op jit(solution)/shard_map/ppermute | solution.py:26
  8.0 8.5 %collective-permute-start.3 = (f32[192,128]{1,0:T(8,128)}, f32[192,128]{1,0:T(8,128)S(1)}, u32[]{:S(2)}, u32[]{:S(2)}) collective-permute-start(f32[192,128]{1,0:T(8,128)} %get-tuple-element.20.refs_0_), channel_id=1, source_target_pairs={{0,4},{2,6},{4,0},{6,2},{1,5},{3,7},{5,1},{7,3},{8,12},{10,14},{12... | collective-permute-start | bytes 294920 | tf_op jit(solution)/shard_map/ppermute | solution.py:26
  10.0 6.5 %collective-permute-start.4 = (f32[192,128]{1,0:T(8,128)}, f32[192,128]{1,0:T(8,128)S(1)}, u32[]{:S(2)}, u32[]{:S(2)}) collective-permute-start(f32[192,128]{1,0:T(8,128)} %get-tuple-element.20.refs_0_), channel_id=1, source_target_pairs={{0,6},{2,4},{4,2},{6,0},{1,7},{3,5},{5,3},{7,1},{8,14},{10,12},{12... | collective-permute-start | bytes 294920 | tf_op jit(solution)/shard_map/ppermute | solution.py:26
  16.5 0.6 %copy-start.4 = (f32[192,128]{1,0:T(8,128)}, f32[192,128]{1,0:T(8,128)S(1)}, u32[]{:S(2)}) copy-start(f32[192,128]{1,0:T(8,128)S(1)} %collective-permute-done.2.refs_1_) | copy-start | bytes 294916
  16.5 0.7 %copy-start.5 = (f32[192,128]{1,0:T(8,128)}, f32[192,128]{1,0:T(8,128)S(1)}, u32[]{:S(2)}) copy-start(f32[192,128]{1,0:T(8,128)S(1)} %collective-permute-done.3.refs_2_) | copy-start | bytes 294916
  16.5 0.7 %copy-start.6 = (f32[192,128]{1,0:T(8,128)}, f32[192,128]{1,0:T(8,128)S(1)}, u32[]{:S(2)}) copy-start(f32[192,128]{1,0:T(8,128)S(1)} %collective-permute-done.4.refs_3_) | copy-start | bytes 294916
  21.0 6.6 %collective-permute-start.5 = (f32[2,160,128]{2,1,0:T(8,128)S(1)}, f32[2,160,128]{2,1,0:T(8,128)S(1)}, u32[]{:S(2)}, u32[]{:S(2)}) collective-permute-start(f32[2,160,128]{2,1,0:T(8,128)S(1)} %get-tuple-element.24), channel_id=1, source_target_pairs={{0,8},{8,0},{16,24},{24,16},{1,9},{9,1},{17,25},{25,17},{2,10},{10... | collective-permute-start | bytes 491528 | tf_op jit(solution)/shard_map/ppermute | solution.py:26
  27.6 6.9 %collective-permute-start.6 = (f32[160,128]{1,0:T(8,128)S(1)}, f32[160,128]{1,0:T(8,128)S(1)}, u32[]{:S(2)}, u32[]{:S(2)}) collective-permute-start(f32[160,128]{1,0:T(8,128)S(1)} %merge.1), channel_id=1, source_target_pairs={{0,16},{8,24},{16,0},{24,8},{1,17},{9,25},{17,1},{25,9},{2,18},{10... | collective-permute-start | bytes 245768 | tf_op jit(solution)/shard_map/ppermute | solution.py:26
  34.5 9.8 %copy-start = (f32[64,128]{1,0:T(8,128)}, f32[64,128]{1,0:T(8,128)S(1)}, u32[]{:S(2)}) copy-start(f32[64,128]{1,0:T(8,128)S(1)} %combine.1.refs_0_) | copy-start | bytes 98308
  34.6 5.6 %collective-permute-start.8 = (f32[64,128]{1,0:T(8,128)S(1)}, f32[64,128]{1,0:T(8,128)S(1)}, u32[]{:S(2)}, u32[]{:S(2)}) collective-permute-start(f32[64,128]{1,0:T(8,128)S(1)} %combine.1.refs_0_), channel_id=1, source_target_pairs={{0,8},{8,0},{16,24},{24,16},{1,9},{9,1},{17,25},{25,17},{2,10},{10... | collective-permute-start | bytes 98312 | tf_op jit(solution)/shard_map/ppermute | solution.py:26
  35.2 6.2 %collective-permute-start.7 = (f32[64,128]{1,0:T(8,128)S(1)}, f32[64,128]{1,0:T(8,128)S(1)}, u32[]{:S(2)}, u32[]{:S(2)}) collective-permute-start(f32[64,128]{1,0:T(8,128)S(1)} %combine.1.refs_0_), channel_id=1, source_target_pairs={{0,16},{8,24},{16,0},{24,8},{1,17},{9,25},{17,1},{25,9},{2,18},{10... | collective-permute-start | bytes 98312 | tf_op jit(solution)/shard_map/ppermute | solution.py:26
  38.6 5.7 %collective-permute-start.9 = (f32[64,128]{1,0:T(8,128)S(1)}, f32[64,128]{1,0:T(8,128)S(1)}, u32[]{:S(2)}, u32[]{:S(2)}) collective-permute-start(f32[64,128]{1,0:T(8,128)S(1)} %combine.1.refs_0_), channel_id=1, source_target_pairs={{0,24},{8,16},{16,8},{24,0},{1,25},{9,17},{17,9},{25,1},{2,26},{10... | collective-permute-start | bytes 98312 | tf_op jit(solution)/shard_map/ppermute | solution.py:26
  40.2 4.1 %copy-start.1 = (f32[64,128]{1,0:T(8,128)}, f32[64,128]{1,0:T(8,128)S(1)}, u32[]{:S(2)}) copy-start(f32[64,128]{1,0:T(8,128)S(1)} %collective-permute-done.8.refs_0_.refs_1_) | copy-start | bytes 98308
  41.4 2.9 %copy-start.2 = (f32[64,128]{1,0:T(8,128)}, f32[64,128]{1,0:T(8,128)S(1)}, u32[]{:S(2)}) copy-start(f32[64,128]{1,0:T(8,128)S(1)} %collective-permute-done.7.refs_0_.refs_2_) | copy-start | bytes 98308
  42.6 10.3 %copy-start.13 = (s32[8]{0:T(128)S(1)}, s32[8]{0:T(128)}, u32[]{:S(2)}) copy-start(s32[8]{0:T(128)} %param.14) | copy-start | bytes 100
  42.6 11.9 %copy-start.8 = (f32[1024]{0:T(1024)S(1)}, f32[1024]{0:T(1024)}, u32[]{:S(2)}) copy-start(f32[1024]{0:T(1024)} %param.11) | copy-start | bytes 12292
  42.6 11.9 %copy-start.11 = (f32[1024]{0:T(1024)S(1)}, f32[1024]{0:T(1024)}, u32[]{:S(2)}) copy-start(f32[1024]{0:T(1024)} %param.12) | copy-start | bytes 12292
  42.6 11.9 %copy-start.12 = (f32[1024]{0:T(1024)S(1)}, f32[1024]{0:T(1024)}, u32[]{:S(2)}) copy-start(f32[1024]{0:T(1024)} %param.13) | copy-start | bytes 12292
  44.3 1.2 %copy-start.3 = (f32[64,128]{1,0:T(8,128)}, f32[64,128]{1,0:T(8,128)S(1)}, u32[]{:S(2)}) copy-start(f32[64,128]{1,0:T(8,128)S(1)} %collective-permute-done.9.refs_3_) | copy-start | bytes 98308
  45.5 4.3 %collective-permute-start.10 = (f32[136,128]{1,0:T(8,128)S(1)}, f32[136,128]{1,0:T(8,128)S(1)}, u32[]{:S(2)}, u32[]{:S(2)}) collective-permute-start(f32[136,128]{1,0:T(8,128)S(1)} %get-tuple-element.29), channel_id=1, source_target_pairs={{0,1},{1,0},{2,3},{3,2},{4,5},{5,4},{6,7},{7,6},{8,9},{9,8},{10,11... | collective-permute-start | bytes 208904 | tf_op jit(solution)/shard_map/ppermute | solution.py:26
  49.9 3.0 %copy-start.7 = (f32[136,128]{1,0:T(8,128)}, f32[136,128]{1,0:T(8,128)S(1)}, u32[]{:S(2)}) copy-start(f32[136,128]{1,0:T(8,128)S(1)} %collective-permute-done.10.theirs_ref) | copy-start | bytes 208900
  49.9 4.6 %collective-permute-start.11 = (f32[8,128]{1,0:T(8,128)S(1)}, f32[8,128]{1,0:T(8,128)S(1)}, u32[]{:S(2)}, u32[]{:S(2)}) collective-permute-start(f32[8,128]{1,0:T(8,128)S(1)} %slice_add_fusion), channel_id=1, source_target_pairs={{0,2},{2,4},{4,6},{6,0},{1,3},{3,5},{5,7},{7,1},{8,10},{10,12},{12... | collective-permute-start | bytes 12296 | tf_op jit(solution)/shard_map/ppermute | solution.py:30
  49.9 4.6 %collective-permute-start.12 = (f32[8,128]{1,0:T(8,128)S(1)}, f32[8,128]{1,0:T(8,128)S(1)}, u32[]{:S(2)}, u32[]{:S(2)}) collective-permute-start(f32[8,128]{1,0:T(8,128)S(1)} %slice_add_fusion), channel_id=1, source_target_pairs={{0,4},{2,6},{4,0},{6,2},{1,5},{3,7},{5,1},{7,3},{8,12},{10,14},{12... | collective-permute-start | bytes 12296 | tf_op jit(solution)/shard_map/ppermute | solution.py:30
  51.5 3.0 %collective-permute-start.13 = (f32[8,128]{1,0:T(8,128)S(1)}, f32[8,128]{1,0:T(8,128)S(1)}, u32[]{:S(2)}, u32[]{:S(2)}) collective-permute-start(f32[8,128]{1,0:T(8,128)S(1)} %slice_add_fusion), channel_id=1, source_target_pairs={{0,6},{2,0},{4,2},{6,4},{1,7},{3,1},{5,3},{7,5},{8,14},{10,8},{12,... | collective-permute-start | bytes 12296 | tf_op jit(solution)/shard_map/ppermute | solution.py:30
